TPU v7x, 32 devices: a whole 2x2x4 slice. The times are simulated.
32 devices in a mesh: atoms: 4 (over y, x), frames: 8 (over z, core).
Axes of the slice: x: 2, y: 2, z: 4, core: 2. Of those that a mesh axis runs over, the one named last changes fastest.
Arguments:
- frames: float32 [192, 3, 98304], P('frames', None, 'atoms'), may hold values from -48 to 48
- mean_structure: float32 [3, 98304], P(None, 'atoms'), may hold values from -16 to 16
- atom_weight: float32 [98304], P('atoms'), may hold values from 1 to 32
- subspace: bfloat16 [32, 3, 98304], P(None, None, 'atoms'), may hold values from -6 to 6
Outputs:
- new_mean: float32 [3, 98304], P(None, ('atoms', 'frames'))
- image: float32 [32, 3, 98304], P(None, None, ('atoms', 'frames'))
- basis: float32 [32, 3, 98304], P(None, None, ('atoms', 'frames'))
All inputs are finite; a program needn't handle non-finite values.
Results may differ from a plain program's by a relative error of at most 0.0076.
Values may be sent and summed in bfloat16 or wider, within the bound.
No kernel may reach another device: no remote copies, remote signals or barrier semaphores. Data moves between devices by JAX's collectives and lax.ppermute only.
A program may use at most 128 MiB of HBM per device.

v0:
```python
import jax
import jax.numpy as jnp
from jax import lax
from jax.sharding import PartitionSpec as P

A = 98304
NEWTON = 8


def newton_polar(moment):
    norm = jnp.sqrt(jnp.sum(moment * moment, axis=(1, 2)))
    x = moment / norm[:, None, None]
    for step in range(NEWTON):
        x00, x01, x02 = (x[:, 0, 0], x[:, 0, 1], x[:, 0, 2])
        x10, x11, x12 = (x[:, 1, 0], x[:, 1, 1], x[:, 1, 2])
        x20, x21, x22 = (x[:, 2, 0], x[:, 2, 1], x[:, 2, 2])
        c00 = x11 * x22 - x12 * x21
        c01 = x12 * x20 - x10 * x22
        c02 = x10 * x21 - x11 * x20
        c10 = x02 * x21 - x01 * x22
        c11 = x00 * x22 - x02 * x20
        c12 = x01 * x20 - x00 * x21
        c20 = x01 * x12 - x02 * x11
        c21 = x02 * x10 - x00 * x12
        c22 = x00 * x11 - x01 * x10
        determ = x00 * c00 + x01 * c01 + x02 * c02
        cofac = jnp.stack(
            [
                jnp.stack([c00, c01, c02], axis=1),
                jnp.stack([c10, c11, c12], axis=1),
                jnp.stack([c20, c21, c22], axis=1),
            ],
            axis=1,
        )
        x = 0.5 * (x + cofac / determ[:, None, None])
    return x


def per_device(frames, mean_structure, atom_weight, subspace):
    highest = lax.Precision.HIGHEST
    frame_count = frames.shape[0] * lax.axis_size("frames")
    weighted = atom_weight[None, :] * mean_structure
    local_first = jnp.einsum("a,fia->fi", atom_weight, frames, precision=highest)
    local_second = jnp.einsum("ia,fja->fij", weighted, frames, precision=highest)
    total, mean_sum, first, second = lax.psum(
        (jnp.sum(atom_weight), jnp.sum(weighted, axis=1), local_first, local_second), "atoms"
    )
    mean_center = mean_sum / total
    moment = second / total - mean_center[None, :, None] * (first / total)[:, None, :]
    frame_center = first / total
    rotation = newton_polar(moment)
    anchor = mean_center[:, None] - mean_structure
    moved = jnp.einsum("fij,fja->fia", rotation, frames, precision=highest)
    offset = jnp.einsum("fij,fj->fi", rotation, frame_center, precision=highest)
    displaced = (moved - offset[:, :, None] + anchor[None]).astype(jnp.bfloat16)
    frame_rows = displaced.shape[0]
    vectors = subspace.shape[0]
    local_proj = jnp.einsum(
        "fc,kc->fk",
        displaced.reshape(frame_rows, -1),
        subspace.reshape(vectors, -1),
        preferred_element_type=jnp.float32,
    )
    projection = lax.psum(local_proj, "atoms")
    proj_total = lax.psum(jnp.sum(local_proj, axis=0), ("atoms", "frames"))
    centered_projection = (projection - proj_total / frame_count).astype(jnp.bfloat16)
    term = jnp.einsum(
        "fk,fia->kia", centered_projection, displaced, preferred_element_type=jnp.float32
    )
    shift_sum = jnp.sum(displaced, axis=0, dtype=jnp.float32)
    stacked = jnp.concatenate([term, shift_sum[None]], axis=0)
    reduced = lax.psum_scatter(stacked, "frames", scatter_dimension=2, tiled=True)
    image_sum = reduced[:vectors]
    mean_shift = reduced[vectors]
    image = image_sum / frame_count
    width = image.shape[2]
    own_mean = lax.dynamic_slice_in_dim(mean_structure, lax.axis_index("frames") * width, width, 1)
    new_mean = own_mean + mean_shift / frame_count
    flat = image.reshape(vectors, -1)
    gram = lax.psum(jnp.dot(flat, flat.T, precision=highest), ("atoms", "frames")) / (3 * A)
    lower = jnp.linalg.cholesky(gram)
    basis = jax.scipy.linalg.solve_triangular(lower, flat, lower=True)
    return (new_mean, image, basis.reshape(image.shape))


def solution(mesh):
    return jax.shard_map(
        per_device,
        mesh=mesh,
        in_specs=(P("frames", None, "atoms"), P(None, "atoms"), P("atoms"), P(None, None, "atoms")),
        out_specs=(
            P(None, ("atoms", "frames")),
            P(None, None, ("atoms", "frames")),
            P(None, None, ("atoms", "frames")),
        ),
        check_vma=False,
    )
```

profile of v0, /device:TPU:0, one launch (start us, length us, event | category | flops | bytes accessed | tf_op | source)
XLA Modules:
  0.0 332.4 jit_solution(2896459653265227953)
XLA Ops:
  7.2 0.0 copy-start.5
  7.2 0.0 reduce-scatter.2.cloned.1.call-start
  7.2 0.0 copy-start
  7.2 1.5 multiply_reduce_fusion
  8.7 16.4 %convolution_bitcast_fusion.1 = f32[24,3,3]{0,1,2:T(4,128)S(1)} fusion(f32[24,3,24576]{2,0,1:T(8,128)} %param.4, f32[3,24576]{1,0:T(4,128)} %param.5, f32[24576]{0:T(1024)} %param.6), kind=kOutput, calls=%fused_computation.16 | convolution fusion | flops 63774720 | bytes 7471968 | tf_op jit(solution)/shard_map/ia,fja->fij/dot_general | solution.py:44
  25.1 0.0 copy-start.4
  25.1 0.0 copy-done.5
  25.1 0.0 copy-done
  25.2 5.6 %fusion.31 = f32[1,24,3]{0,1,2:T(8,128)S(1)} fusion(f32[24576,1,1]{0,1,2:T(1,128)S(1)} %bitcast.241, f32[24,3,24576]{2,0,1:T(8,128)S(1)} %copy-done), kind=kOutput, calls=%fused_computation.165 | convolution fusion | flops 21233664 | bytes 7176480 | tf_op jit(solution)/shard_map/a,fia->fi/dot_general | solution.py:43
  30.8 0.1 copy.71
  30.9 0.6 reduce_sum.45
  31.5 12.3 %all-reduce = (f32[24,3,3]{0,1,2:T(4,128)S(1)}, f32[24,3]{0,1:T(4,128)S(1)}, f32[]{:T(128)}, f32[3]{0:T(128)S(1)}) all-reduce(f32[24,3,3]{0,1,2:T(4,128)S(1)} %convolution_bitcast_fusion.1, f32[24,3]{0,1:T(4,128)S(1)} %bitcast.242, f32[]{:T(128)} %reduce_sum.45, ...), channel_id=1, replica_groups=mesh['atoms'=4,'frames'=8] {'atoms'}, use_global_device_ids=true, to_apply=%region_0.0 | all-reduce | flops 292 | bytes 2336 | tf_op jit(solution)/shard_map/psum | solution.py:45
  43.8 0.6 broadcast_divide_fusion.1
  44.4 0.7 broadcast_divide_fusion.2
  45.1 0.7 multiply_reduce_fusion.1
  46.6 0.1 fusion.26
  46.7 0.1 fusion.27
  46.9 0.1 fusion.28
  47.0 0.7 fusion.43
  47.7 0.0 copy-done.4
  47.7 0.0 slice-start
  47.7 0.1 broadcast_subtract_fusion
  47.9 0.1 fusion.29
  48.0 0.1 copy.62
  48.1 0.1 copy.72
  48.2 0.3 fusion.32
  48.5 0.0 slice-start.1
  48.5 29.3 %convert_reduce_fusion = (f32[3,24576]{1,0:T(4,128)S(1)}, bf16[24,3,24576]{2,1,0:T(4,128)(2,1)S(1)}) fusion(f32[3,24576]{1,0:T(4,128)S(1)} %broadcast_subtract_fusion, f32[24,3]{1,0:T(8,128)S(1)} %bitcast.267, f32[24,3,3]{2,1,0:T(4,128)S(1)} %copy.62, f32[24,3,24576]{2,0,1:T(8,128)} %param.4), kind=kOutput, calls=%fused_computation.5 | convolution fusion | flops 72474624 | bytes 11207808 | tf_op jit(solution)/shard_map/fij,fja->fia/dot_general | solution.py:53
  77.8 0.0 copy-start.2
  77.8 2.1 copy-done.2
  80.0 0.0 slice-done
  80.0 0.0 slice-done.1
  80.0 5.2 %fusion.30 = (f32[32]{0:T(128)S(1)}, f32[24,32]{1,0:T(8,128)S(1)}) fusion(bf16[32,3,24576]{2,0,1:T(8,128)(2,1)S(1)} %bitcast.240, bf16[24,3,24576]{2,1,0:T(4,128)(2,1)S(1)} %get-tuple-element.90), kind=kOutput, calls=%fused_computation.163 | convolution fusion | flops 113246944 | bytes 8260736 | tf_op jit(solution)/shard_map/fc,kc->fk/dot_general | solution.py:58
  85.2 14.0 %psum.53 = f32[24,32]{1,0:T(8,128)S(1)} all-reduce(f32[24,32]{1,0:T(8,128)S(1)} %get-tuple-element.92), channel_id=1, replica_groups=mesh['atoms'=4,'frames'=8] {'atoms'}, use_global_device_ids=true, to_apply=%region_7.0 | all-reduce | flops 768 | bytes 6144 | tf_op jit(solution)/shard_map/psum | solution.py:64
  99.2 39.4 %psum.54 = f32[32]{0:T(128)S(1)} all-reduce(f32[32]{0:T(128)S(1)} %get-tuple-element.91), channel_id=1, replica_groups=mesh['atoms'=4,'frames'=8] {'atoms','frames'}, use_global_device_ids=true, to_apply=%region_9.0 | all-reduce | flops 32 | bytes 256 | tf_op jit(solution)/shard_map/psum | solution.py:65
  138.7 0.2 broadcast_in_dim.3
  138.9 9.0 %fusion.3 = f32[32,3,24576]{2,0,1:T(8,128)S(1)} fusion(bf16[24,3,24576]{2,1,0:T(4,128)(2,1)} %copy-done.2, f32[24,32]{1,0:T(8,128)S(1)} %psum.53, f32[32]{0:T(128)S(1)} %broadcast_multiply_fusion.1), kind=kOutput, calls=%fused_computation.6 | convolution fusion | flops 113247744 | bytes 12979328 | tf_op jit(solution)/shard_map/fk,fia->kia/dot_general | solution.py:67
  147.9 5.7 %pad_maximum_fusion = f32[33,3,24576]{2,0,1:T(8,128)} fusion(f32[1,3,24576]{2,0,1:T(1,128)S(1)} %broadcast_in_dim.3, f32[32,3,24576]{2,0,1:T(8,128)S(1)} %fusion.3), kind=kLoop, calls=%fused_computation.3 | loop fusion | flops 2433024 | bytes 19464192 | tf_op jit(solution)/shard_map/concatenate | solution.py:71
  153.5 0.0 reduce-scatter.2.cloned.1.call-update
  153.6 121.9 %reduce-scatter.2.cloned.1.call-done = f32[33,3,3072]{2,0,1:T(8,128)} async-done(((f32[33,3,24576]{2,0,1:T(8,128)}), f32[33,3,3072]{2,0,1:T(8,128)}) %reduce-scatter.2.cloned.1.call-update) | async-done | bytes 1216528 | tf_op jit(solution)/shard_map/reduce_scatter | solution.py:72
  275.5 0.0 copy-start.3
  275.5 1.5 slice_multiply_fusion
  277.0 0.0 copy-start.1
  277.0 1.1 convolution_bitcast_fusion
  278.1 37.9 %psum.55 = f32[32,32]{0,1:T(8,128)S(1)} all-reduce(f32[32,32]{0,1:T(8,128)S(1)} %convolution_bitcast_fusion), channel_id=1, replica_groups=mesh['atoms'=4,'frames'=8] {'atoms','frames'}, use_global_device_ids=true, to_apply=%region_12.0 | all-reduce | flops 1024 | bytes 8192 | tf_op jit(solution)/shard_map/psum | solution.py:80
  315.9 0.1 copy.67
  316.0 2.9 cholesky.16
  319.0 0.6 compare_reduce_fusion
  319.6 0.7 fusion.16
  320.3 2.4 custom-call.7
  322.7 0.0 copy-done.3
  322.7 0.1 slice_multiply_fusion.1
  322.8 0.6 bitcast_add_fusion
  323.4 2.1 fusion.7
  325.6 0.0 copy-done.1
  (74 shorter events, 0.7 us)
Async XLA Ops:
  7.2 18.0 %copy-start.5 = (f32[24576]{0:T(1024)S(1)}, f32[24576]{0:T(1024)}, u32[]{:S(2)}) copy-start(f32[24576]{0:T(1024)} %param.6) | copy-start | bytes 294916
  7.2 268.3 %reduce-scatter.2.cloned.1.call-start = ((), (), s32[]{:S(2)}) async-start(), calls=%async_computation.1 | async-start | bytes 13271040 | tf_op jit(solution)/shard_map/reduce_scatter | solution.py:72
  7.2 17.9 %copy-start = (f32[24,3,24576]{2,0,1:T(8,128)S(1)}, f32[24,3,24576]{2,0,1:T(8,128)}, u32[]{:S(2)}) copy-start(f32[24,3,24576]{2,0,1:T(8,128)} %param.4) | copy-start | bytes 21233668
  25.1 22.6 %copy-start.4 = (f32[3,24576]{1,0:T(4,128)S(1)}, f32[3,24576]{1,0:T(4,128)}, u32[]{:S(2)}) copy-start(f32[3,24576]{1,0:T(4,128)} %param.5) | copy-start | bytes 884740
  47.7 32.3 %slice-start = ((s8[4718592]{0:T(1024)(128)(4,1)}), s8[524288]{0:T(1024)(128)(4,1)S(1)}, s32[]{:S(2)}) async-start(s8[4718592]{0:T(1024)(128)(4,1)} %bitcast.239), calls=%async_computation.2 | async-start | bytes 1048576
  48.5 31.4 %slice-start.1 = ((s8[4718592]{0:T(1024)(128)(4,1)}), s8[4194304]{0:T(1024)(128)(4,1)S(1)}, s32[]{:S(2)}) async-start(s8[4718592]{0:T(1024)(128)(4,1)} %bitcast.239), calls=%async_computation.3 | async-start | bytes 8388608
  77.8 2.1 copy-start.2
  275.5 47.2 %copy-start.3 = (f32[33,3,3072]{2,0,1:T(8,128)S(1)}, f32[33,3,3072]{2,0,1:T(8,128)}, u32[]{:S(2)}) copy-start(f32[33,3,3072]{2,0,1:T(8,128)} %reduce-scatter.2.cloned.1.call-done) | copy-start | bytes 3649540
  277.0 48.6 %copy-start.1 = (f32[32,3,3072]{2,0,1:T(8,128)}, f32[32,3,3072]{2,0,1:T(8,128)S(1)}, u32[]{:S(2)}) copy-start(f32[32,3,3072]{2,0,1:T(8,128)S(1)} %slice_multiply_fusion) | copy-start | bytes 3538948
Sparse Core Ops, SparseCore 0:
  153.7 121.7 reduce-scatter.1
where the time goes:
time: 334 us; the launch traced here: 332 us
  waiting for transfers between devices  122 us (37%)
  blocking collectives  104 us (31%)
  matrix products  69 us (21%)
  other arithmetic  20.3 us (6%)
  between operations  14.7 us (4%)
    reduce_scatter x1, waiting for transfers between devices, per_device(): lax.psum_scatter(stacked, 'frames', scatter_dimension=2, tiled=True)  122 us
    psum x1, blocking collectives, per_device(): proj_total = lax.psum(jnp.sum(local_proj, axis=0), ('atoms', 'frames'))  39.4 us
    psum x1, blocking collectives, per_device(): lax.psum(jnp.dot(flat, flat.T, precision=highest), ('atoms', 'frames'))  37.9 us
    dot_general x1, matrix products, per_device(): moved = jnp.einsum('fij,fja->fia', rotation, frames, precision=highest)  29.3 us
    dot_general x1, matrix products, per_device(): jnp.einsum('ia,fja->fij', weighted, frames, precision=highest)  16.4 us
    psum x1, blocking collectives, per_device(): projection = lax.psum(local_proj, 'atoms')  14 us
    psum x1, blocking collectives, per_device(): lax.psum((jnp.sum(atom_weight), jnp.sum(weighted, axis=1), local_first, l...  12.3 us
    dot_general x1, matrix products, per_device(): jnp.einsum('fk,fia->kia', centered_projection, displaced, preferred_eleme...  8.98 us
  transfers between devices with their start and end apart: 1, of which 1 were waited for; matrix products, arithmetic and copies ran while one was open for 0% of the time, Pallas kernels for 0%

commit v1 on v0

v1 whole, which is shorter than its diff:
```python
import functools

import jax
import jax.numpy as jnp
from jax import lax
from jax.experimental import pallas as pl
from jax.experimental.pallas import tpu as pltpu
from jax.sharding import PartitionSpec as P

NEWTON = 8
LANES = 128
F32 = jnp.float32
BF16 = jnp.bfloat16
TILE = 256
PANEL = 4
VMEM_LIMIT = 24 * 1024 * 1024


def params():
    return pltpu.CompilerParams(vmem_limit_bytes=VMEM_LIMIT)


def in_vmem(count):
    return [pl.BlockSpec(memory_space=pltpu.VMEM)] * count


def split3(value):
    high = value.astype(BF16)
    rest = value - high.astype(F32)
    middle = rest.astype(BF16)
    low = (rest - middle.astype(F32)).astype(BF16)
    return high, middle, low


def dot_nt(a, b):
    return lax.dot_general(a, b, (((1,), (1,)), ((), ())), preferred_element_type=F32)


def dot_nn(a, b, precision=None):
    return lax.dot_general(
        a, b, (((1,), (0,)), ((), ())), preferred_element_type=F32, precision=precision
    )


def moments_kernel(
    _, x_hbm, m_hbm, w_hbm, s_hbm, out_ref, x_ref, m_ref, w_ref, lhs_ref, rhs_ref, sems
):
    rows, atoms = x_ref.shape
    vectors = s_hbm.shape[0]
    chunks = sems.shape[1] - 1
    chunk = atoms // chunks
    n = rows + 8
    copies = [
        [
            pltpu.make_async_copy(m_hbm, m_ref, sems.at[0, chunks]),
            pltpu.make_async_copy(w_hbm, w_ref, sems.at[1, chunks]),
        ]
    ]
    for t in range(chunks):
        lanes = pl.ds(t * chunk, chunk)
        copies.append(
            [
                pltpu.make_async_copy(x_hbm.at[:, lanes], x_ref.at[:, lanes], sems.at[0, t]),
                pltpu.make_async_copy(
                    s_hbm.at[:, lanes], rhs_ref.at[0:vectors, lanes], sems.at[1, t]
                ),
            ]
        )
    for group in copies:
        for copy in group:
            copy.start()
    for copy in copies[0]:
        copy.wait()
    row = lax.broadcasted_iota(jnp.int32, (8, TILE), 0)
    ones = jnp.where(row == 3, 1.0, 0.0)
    total = jnp.zeros(out_ref.shape, F32)
    for t in range(chunks):
        for copy in copies[t + 1]:
            copy.wait()
        for start in range(0, chunk, TILE):
            lanes = slice(t * chunk + start, t * chunk + start + TILE)
            here = slice(start, start + TILE)
            left = ones
            for i in range(3):
                left = jnp.where(row == i, m_ref[i : i + 1, lanes], left)
            value = jnp.concatenate([x_ref[:, lanes], left], axis=0)
            high = value.astype(BF16)
            lhs_ref[t % 2, 0:n, here] = high
            lhs_ref[t % 2, n : 2 * n, here] = (value - high.astype(F32)).astype(BF16)
            pieces = [v.astype(F32) for v in split3(left * w_ref[:, lanes])]
            aux = jnp.concatenate(pieces + [jnp.zeros(left.shape, F32)], axis=0)
            rhs_ref[vectors:, lanes] = aux.astype(BF16)
        sums = dot_nt(lhs_ref[t % 2], rhs_ref[:, t * chunk : (t + 1) * chunk])
        total = total + (sums[0:n] + sums[n : 2 * n])
    out_ref[...] = total


def moments(where_, x, mean, weight, sub):
    rows, atoms = x.shape
    vectors = sub.shape[0]
    chunks = 16
    chunk = atoms // chunks
    n = rows + 8
    return pl.pallas_call(
        moments_kernel,
        in_specs=[pl.BlockSpec(memory_space=pltpu.SMEM)] + [pl.BlockSpec(memory_space=pl.ANY)] * 4,
        out_specs=in_vmem(2),
        out_shape=(jax.ShapeDtypeStruct((n, LANES), F32), jax.ShapeDtypeStruct(x.shape, F32)),
        scratch_shapes=[
            pltpu.VMEM(mean.shape, F32),
            pltpu.VMEM(weight.shape, F32),
            pltpu.VMEM((2, 2 * n, chunk), BF16),
            pltpu.VMEM((LANES, atoms), BF16),
            pltpu.SemaphoreType.DMA((2, chunks + 1)),
        ],
        compiler_params=params(),
        name="moments",
    )(where_, x, mean, weight, sub)


def rotate_kernel(frame_rows, vectors, *refs):
    parts, (coef_ref, proj_ref) = refs[:-2], refs[-2:]
    sums = parts[0][...]
    for ref in parts[1:]:
        sums = sums + ref[...]
    folded = sums + pltpu.roll(sums, LANES - 8, 1) + pltpu.roll(sums, LANES - 16, 1)
    base = 3 * vectors
    tail = 3 * frame_rows
    shape = (frame_rows, LANES)
    lane = lax.broadcasted_iota(jnp.int32, shape, 1)

    def scalar(r, c):
        return jnp.broadcast_to(folded[r : r + 1, c : c + 1], shape)

    def column(j, c):
        return jnp.broadcast_to(folded[j * frame_rows : (j + 1) * frame_rows, c : c + 1], shape)

    total = scalar(tail + 3, base + 3)
    center = [scalar(tail + 3, base + i) / total for i in range(3)]
    frame_center = [column(j, base + 3) / total for j in range(3)]
    x = [
        [column(j, base + i) / total - center[i] * frame_center[j] for j in range(3)]
        for i in range(3)
    ]
    square = sum(x[i][j] * x[i][j] for i in range(3) for j in range(3))
    norm = jnp.sqrt(square)
    x = [[x[i][j] / norm for j in range(3)] for i in range(3)]
    for _ in range(NEWTON):
        cof = [
            [
                x[(i + 1) % 3][(j + 1) % 3] * x[(i + 2) % 3][(j + 2) % 3]
                - x[(i + 1) % 3][(j + 2) % 3] * x[(i + 2) % 3][(j + 1) % 3]
                for j in range(3)
            ]
            for i in range(3)
        ]
        determ = x[0][0] * cof[0][0] + x[0][1] * cof[0][1] + x[0][2] * cof[0][2]
        inverse = 1.0 / determ
        x = [[0.5 * (x[i][j] + cof[i][j] * inverse) for j in range(3)] for i in range(3)]
    shift = [
        center[i] - (x[i][0] * frame_center[0] + x[i][1] * frame_center[1] + x[i][2] * frame_center[2])
        for i in range(3)
    ]
    for i in range(3):
        for j in range(3):
            at = (3 * i + j) * frame_rows
            coef_ref[at : at + frame_rows, :] = x[i][j]
        at = (9 + i) * frame_rows
        coef_ref[at : at + frame_rows, :] = shift[i]

    def by_group(values):
        return jnp.where(lane < vectors, values[0], jnp.where(lane < 2 * vectors, values[1], values[2]))

    y = by_group(shift) * sums[tail + 3 : tail + 4, :]
    y = y - by_group([sums[tail + i : tail + i + 1, :] for i in range(3)])
    for j in range(3):
        block = sums[j * frame_rows : (j + 1) * frame_rows, :]
        y = y + by_group([x[i][j] for i in range(3)]) * block
    y = y + pltpu.roll(y, LANES - vectors, 1) + pltpu.roll(y, LANES - 2 * vectors, 1)
    y = jnp.where(lane < vectors, y, 0.0)
    proj_ref[...] = y


def rotate(parts, frame_rows, vectors):
    return pl.pallas_call(
        functools.partial(rotate_kernel, frame_rows, vectors),
        out_shape=(
            jax.ShapeDtypeStruct((12 * frame_rows, LANES), F32),
            jax.ShapeDtypeStruct((frame_rows, LANES), F32),
        ),
        compiler_params=params(),
        name="rotate",
    )(*parts)


def first_block(chip, line):
    end = jnp.logical_or(chip == 0, chip == line - 1)
    return jnp.where(end, line - 1 - chip, chip)


def displace_kernel(keep, first, line, frame_rows, width, idx, x_ref, m_ref, coef_ref, out_ref):
    core = lax.rem(idx[0], 2)
    side = core if keep else 1 - core
    made_first = first_block(idx[0] // 2, line)

    def coef(i):
        return coef_ref[i * frame_rows : (i + 1) * frame_rows, :]

    def do_block(b, _):
        block = made_first if first else b + (b >= made_first).astype(jnp.int32)
        for start in range(0, width, LANES):
            lanes = pl.ds(pl.multiple_of((2 * block + side) * width + start, LANES), LANES)
            x = [x_ref[j * frame_rows : (j + 1) * frame_rows, lanes] for j in range(3)]
            result = []
            for i in range(3):
                value = coef(3 * i) * x[0] + coef(3 * i + 1) * x[1] + coef(3 * i + 2) * x[2]
                result.append(value + (coef(9 + i) - m_ref[i : i + 1, lanes]))
            to = pl.ds(pl.multiple_of(b * width + start, LANES), LANES)
            out_ref[:, to] = jnp.concatenate(result, axis=0).astype(BF16)
        return 0

    lax.fori_loop(0, 1 if first else line - 1, do_block, 0)


def displace(where_, x, mean, coef, line, keep, first):
    rows, atoms = x.shape
    width = atoms // (2 * line)
    out_width = width if first else (line - 1) * width
    return pl.pallas_call(
        functools.partial(displace_kernel, keep, first, line, rows // 3, width),
        in_specs=[pl.BlockSpec(memory_space=pltpu.SMEM)] + in_vmem(3),
        out_specs=pl.BlockSpec(memory_space=pltpu.VMEM),
        out_shape=jax.ShapeDtypeStruct((rows, out_width), BF16),
        compiler_params=params(),
        name="displace",
    )(where_, x, mean, coef)


def weights_kernel(frame_rows, vectors, own_ref, other_ref, c_ref, e_ref, mean_ref):
    total = jnp.sum(own_ref[...] + other_ref[...], axis=0, keepdims=True)
    mean = total / (2 * frame_rows)
    lane = lax.broadcasted_iota(jnp.int32, (frame_rows, LANES), 1)
    for source, out in ((own_ref, c_ref), (other_ref, e_ref)):
        value = jnp.where(lane < vectors, source[...] - mean, 0.0)
        blocks = [value, pltpu.roll(value, vectors, 1), pltpu.roll(value, 2 * vectors, 1)]
        blocks.append(jnp.zeros((LANES - 3 * frame_rows, LANES), F32))
        table = jnp.concatenate(blocks, axis=0).T
        out[...] = table[0 : 3 * vectors, 0 : 3 * frame_rows].astype(BF16)
    mean_ref[...] = jnp.broadcast_to(jnp.where(lane[0:1] < vectors, mean, 0.0), (8, LANES))


def weights(own, other, frame_rows, vectors):
    out = jax.ShapeDtypeStruct((3 * vectors, 3 * frame_rows), BF16)
    return pl.pallas_call(
        functools.partial(weights_kernel, frame_rows, vectors),
        in_specs=in_vmem(2),
        out_specs=in_vmem(3),
        out_shape=(out, out, jax.ShapeDtypeStruct((8, LANES), F32)),
        compiler_params=params(),
        name="weights",
    )(own, other)


def ones_rows(rows):
    row = lax.broadcasted_iota(jnp.int32, (8, rows), 0)
    column = lax.broadcasted_iota(jnp.int32, (8, rows), 1)
    inside = jnp.logical_and(column >= row * (rows // 3), column < (row + 1) * (rows // 3))
    return jnp.where(inside, 1.0, 0.0).astype(BF16)


def both(left, right, a, b):
    return dot_nn(left, a) + dot_nn(right, b)


def as_column(row, vectors):
    return jnp.broadcast_to(row, (LANES, LANES)).T[0:vectors, 0:1]


def read_slab(slab, width):
    at = 3 * width // LANES
    center = jnp.sum(slab[at : at + 3], axis=0, keepdims=True)
    total = jnp.sum(slab[at + 3 : at + 6], axis=0, keepdims=True)
    return center, total


def write_slab(slab_ref, received, sums, center, total, width):
    tiles = width // LANES
    slab_ref[...] = received
    for i in range(3):
        for tile in range(tiles):
            at = i * tiles + tile
            part = sums[i : i + 1, tile * LANES : (tile + 1) * LANES]
            slab_ref[at : at + 1, :] = received[at : at + 1, :] + part
    for i, piece in enumerate([*split3(center), *split3(total)]):
        at = 3 * tiles + i
        slab_ref[at : at + 1, :] = piece.astype(F32)


def term_kernel(block, starts, line, p, pieces, vectors, width, idx, *refs):
    (c_ref, e_ref, mean_ref, a_ref, b_ref), refs = refs[0:5], list(refs[5:])
    slab_ref = refs.pop() if p == 0 else None
    out_ref = refs.pop()
    chip = idx[0] // 2
    if block is None:
        at = 0
    else:
        at = block(chip)
        at = jnp.clip(at - (at > first_block(chip, line)).astype(jnp.int32), 0, line - 2)
    piece_width = width // pieces
    lanes = pl.ds(pl.multiple_of(at * width + p * piece_width, LANES), piece_width)
    value = both(c_ref[...], e_ref[...], a_ref[:, lanes], b_ref[:, lanes])
    mean = mean_ref[0:1, :]
    center, total = mean, mean
    slab = jnp.zeros((value.shape[0], LANES), F32)
    ones = ones_rows(a_ref.shape[0])
    if refs:
        slab = refs[0][:, piece_width:].astype(F32)
        before, summed_means = read_slab(slab, width)
        center = jnp.where(chip == starts, mean, before)
        total = mean + summed_means
        column = as_column(mean - center, vectors)
        sums = both(ones, ones, a_ref[:, lanes], b_ref[:, lanes])
        moved = [column * sums[i : i + 1, :] for i in range(3)]
        value = value + jnp.concatenate(moved, axis=0)
        value = value + refs[p][:, 0:piece_width].astype(F32)
    out_ref[:, 0:piece_width] = value.astype(BF16)
    if p == 0:
        lanes = pl.ds(pl.multiple_of(at * width, LANES), width)
        sums = both(ones, ones, a_ref[:, lanes], b_ref[:, lanes])
        write_slab(slab_ref, slab, sums, center, total, width)
        out_ref[:, piece_width:] = slab_ref[...].astype(BF16)


def term(where_, scales, displaced, received, block, starts, line, p, pieces, vectors, width):
    rows = scales[0].shape[0]
    args = (*scales, *displaced, *received)
    out_width = width // pieces + (LANES if p == 0 else 0)
    return pl.pallas_call(
        functools.partial(term_kernel, block, starts, line, p, pieces, vectors, width),
        in_specs=[pl.BlockSpec(memory_space=pltpu.SMEM)] + in_vmem(len(args)),
        out_specs=pl.BlockSpec(memory_space=pltpu.VMEM),
        out_shape=jax.ShapeDtypeStruct((rows, out_width), BF16),
        scratch_shapes=[pltpu.VMEM((rows, LANES), F32)] if p == 0 else [],
        compiler_params=params(),
        name="term",
    )(where_, *args)


def image_kernel(line, p, pieces, vectors, width, frame_count, idx, *refs):
    refs = list(refs)
    c_ref, e_ref, mean_ref = [refs.pop(0) for _ in range(3)]
    firsts, rests = [[refs.pop(0) for _ in range(2)] for _ in range(2)]
    carriers = [refs.pop(0) for _ in range(2)]
    other_ref = refs.pop(0)
    block_ref = refs.pop()
    new_mean_ref = refs.pop() if p == 0 else None
    gram_ref, image_ref = refs.pop(), refs.pop()
    received = carriers if p == 0 else refs
    chip = idx[0] // 2
    made_first = first_block(chip, line)
    at = pl.multiple_of(jnp.clip(chip - (chip > made_first).astype(jnp.int32), 0, line - 2) * width, LANES)
    for n in range(2):

        @pl.when(chip == made_first)
        def _(n=n):
            block_ref[n] = firsts[n][...]

        @pl.when(chip != made_first)
        def _(n=n):
            block_ref[n] = rests[n][:, pl.ds(at, width)]

    piece_width = width // pieces
    lanes = slice(p * piece_width, (p + 1) * piece_width)
    value = both(c_ref[...], e_ref[...], block_ref[0, :, lanes], block_ref[1, :, lanes])
    for ref in received:
        value = value + ref[:, 0:piece_width].astype(F32)

    ones = ones_rows(block_ref.shape[1])
    sums = both(ones, ones, block_ref[0], block_ref[1])
    mean = mean_ref[0:1, :]
    slabs = [ref[:, piece_width:].astype(F32) for ref in carriers]
    centers, totals = zip(*(read_slab(slab, width) for slab in slabs))
    center = (mean + totals[0] + totals[1]) / line
    columns = [as_column(v - center, vectors) for v in (mean, *centers)]
    tiles, piece_tiles = width // LANES, piece_width // LANES
    gram = jnp.zeros((2 * vectors, LANES), F32)
    for i in range(3):
        rows = slice(i * vectors, (i + 1) * vectors)
        moved = []
        for tile in range(p * piece_tiles, (p + 1) * piece_tiles):
            part = columns[0] * sums[i : i + 1, tile * LANES : (tile + 1) * LANES]
            row = i * tiles + tile
            for column, slab in zip(columns[1:], slabs):
                part = part + column * slab[row : row + 1, :]
            moved.append(part)
        part = (value[rows] + jnp.concatenate(moved, axis=1)) / frame_count
        image_ref[rows, :] = part
        high = part.astype(BF16)
        low = (part - high.astype(F32)).astype(BF16)
        lhs = jnp.concatenate([high, low], axis=0)
        rhs = jnp.concatenate([lhs, jnp.zeros((LANES - 2 * vectors, piece_width), BF16)], axis=0)
        gram = gram + dot_nt(lhs, rhs)
    gram = gram[0:vectors] + gram[vectors : 2 * vectors]
    gram = gram + pltpu.roll(gram, LANES - vectors, 1)
    lane = lax.broadcasted_iota(jnp.int32, gram.shape, 1)
    gram = jnp.where(lane < vectors, gram, 0.0)
    packed = gram[0:8]
    for g in range(1, vectors // 8):
        packed = packed + pltpu.roll(gram[8 * g : 8 * g + 8], vectors * g, 1)
    if p > 0:
        packed = packed + other_ref[...]
    gram_ref[...] = packed
    if p == 0:
        total = slabs[0] + slabs[1]
        for i in range(3):
            for tile in range(tiles):
                start = (idx[0] * tiles + tile) * LANES
                old = other_ref[i : i + 1, pl.ds(pl.multiple_of(start, LANES), LANES)]
                row = i * tiles + tile
                here = slice(tile * LANES, (tile + 1) * LANES)
                added = (total[row : row + 1, :] + sums[i : i + 1, here]) / frame_count
                new_mean_ref[i : i + 1, here] = old + added


def image_piece(
    where_, scales, firsts, rests, carriers, received, other, line, p, pieces, vectors, width,
    frame_count,
):
    rows = scales[0].shape[0]
    args = [*scales, *firsts, *rests, *carriers, other]
    out_shape = [
        jax.ShapeDtypeStruct((rows, width // pieces), F32),
        jax.ShapeDtypeStruct((8, LANES), F32),
    ]
    if p == 0:
        out_shape.append(jax.ShapeDtypeStruct((3, width), F32))
    else:
        args += received
    return pl.pallas_call(
        functools.partial(image_kernel, line, p, pieces, vectors, width, frame_count),
        in_specs=[pl.BlockSpec(memory_space=pltpu.SMEM)] + in_vmem(len(args)),
        out_specs=in_vmem(len(out_shape)),
        out_shape=out_shape,
        scratch_shapes=[pltpu.VMEM((2, firsts[0].shape[0], width), BF16)],
        compiler_params=params(),
        name="image_piece",
    )(where_, *args)


def fold_kernel(*refs):
    value = refs[0][...]
    for ref in refs[1:-1]:
        value = value + ref[...]
    refs[-1][...] = value


def fold(parts):
    return pl.pallas_call(
        fold_kernel,
        in_specs=in_vmem(len(parts)),
        out_specs=pl.BlockSpec(memory_space=pltpu.VMEM),
        out_shape=jax.ShapeDtypeStruct(parts[0].shape, F32),
        compiler_params=params(),
        name="fold",
    )(*parts)


def exchanged(value, axis, size, bits):
    masks = [0]
    for bit in bits:
        masks += [mask | (1 << bit) for mask in masks]
    return [value] + [
        lax.ppermute(value, axis, [(i, i ^ mask) for i in range(size)]) for mask in masks[:0:-1]
    ]


def summed(value, axis, size, bits):
    groups = [bits[start : start + 2] for start in range(0, len(bits), 2)]
    for group in groups[:-1]:
        value = fold(exchanged(value, axis, size, group))
    return exchanged(value, axis, size, groups[-1])


def basis_kernel(vectors, coordinates, gram_count, *refs):
    grams, pieces, (image_ref, basis_ref) = refs[:gram_count], refs[gram_count:-2], refs[-2:]
    packed = grams[0][...]
    for ref in grams[1:]:
        packed = packed + ref[...]
    packed = packed / coordinates
    groups = [packed]
    for g in range(1, vectors // 8):
        groups.append(pltpu.roll(packed, LANES - vectors * g, 1))
    gram = jnp.concatenate(groups, axis=0)
    row = lax.broadcasted_iota(jnp.int32, gram.shape, 0)
    lane = lax.broadcasted_iota(jnp.int32, gram.shape, 1)
    a = jnp.where(lane < vectors, gram, jnp.where(lane == row + vectors, 1.0, 0.0))
    for panel in range(0, vectors, PANEL):
        columns = [
            jnp.broadcast_to(a[:, j : j + 1], a.shape) for j in range(panel, panel + PANEL)
        ]
        for q in range(PANEL):
            j = panel + q
            factor = columns[q] * (1.0 / columns[q][j : j + 1, :])
            factor = jnp.where(row > j, factor, 0.0)
            for r in range(q + 1, PANEL):
                columns[r] = columns[r] - factor * columns[r][j : j + 1, :]
            a = a - factor * a[j : j + 1, :]
    diagonal = jnp.sum(jnp.where(lane == row, a, 0.0), axis=1, keepdims=True)
    a = a * (1.0 / jnp.sqrt(diagonal))
    a = jnp.where(lane < vectors, pltpu.roll(a, LANES - vectors, 1), 0.0)
    high = a.astype(BF16).astype(F32)
    left = high + pltpu.roll(high, vectors, 1) + pltpu.roll(a - high, 2 * vectors, 1)
    left = left.astype(BF16)[:, 0 : 3 * vectors]
    start = 0
    for ref in pieces:
        lanes = slice(start, start + ref.shape[1])
        start += ref.shape[1]
        for i in range(3):
            rows = slice(i * vectors, (i + 1) * vectors)
            part = ref[rows, :]
            high = part.astype(BF16)
            low = (part - high.astype(F32)).astype(BF16)
            basis_ref[rows, lanes] = dot_nn(left, jnp.concatenate([high, low, high], axis=0))
            image_ref[rows, lanes] = part


def basis_of(grams, images, vectors, coordinates):
    rows = images[0].shape[0]
    width = sum(v.shape[1] for v in images)
    return pl.pallas_call(
        functools.partial(basis_kernel, vectors, coordinates, len(grams)),
        in_specs=in_vmem(len(grams) + len(images)),
        out_specs=in_vmem(2),
        out_shape=[jax.ShapeDtypeStruct((rows, width), F32)] * 2,
        compiler_params=params(),
        name="basis",
    )(*grams, *images)


def along_line(line, pieces, make_first, make):
    def to_right(z):
        return [(2 * z + core, 2 * z + 2 + core) for core in range(2)]

    def to_left(z):
        return [(2 * z + core, 2 * z - 2 + core) for core in range(2)]

    ends = to_right(0) + to_left(line - 1)
    right = [lax.ppermute(make_first(p), "frames", ends) for p in range(pieces)]
    left = list(right)
    for step in range(2, line):

        def right_block(chip, step=step):
            return jnp.minimum(line - step + chip, line - 1)

        def left_block(chip, step=step):
            return jnp.maximum(step - line + chip, 0)

        right_pairs = [pair for z in range(step) for pair in to_right(z)]
        left_pairs = [pair for z in range(step) for pair in to_left(line - 1 - z)]
        next_right, next_left = [], []
        for p in range(pieces):
            out = make(right[: p + 1], right_block, 0, p)
            next_right.append(lax.ppermute(out, "frames", right_pairs))
            out = make(left[: p + 1], left_block, line - 1, p)
            next_left.append(lax.ppermute(out, "frames", left_pairs))
        right, left = next_right, next_left
    return right, left


def per_device(atom_devices, frame_devices, frames, mean_structure, atom_weight, subspace):
    frame_rows, _, atoms = frames.shape
    vectors = subspace.shape[0]
    frame_count = frame_rows * frame_devices
    width = atoms // frame_devices
    line = frame_devices // 2
    pieces = 2 if (width // LANES) % 2 == 0 else 1
    assert line > 2 and 3 * width // LANES + 6 <= 3 * vectors

    x = jnp.transpose(frames, (1, 0, 2)).reshape(3 * frame_rows, atoms)
    sub = jnp.transpose(subspace, (1, 0, 2)).reshape(3 * vectors, atoms)
    where_ = lax.axis_index("frames").astype(jnp.int32).reshape(1)

    inputs = (x, mean_structure, atom_weight.reshape(1, atoms), sub)
    local, x = moments(where_, *(pltpu.with_memory_space_constraint(v, pltpu.HBM) for v in inputs))
    atom_bits = range(atom_devices.bit_length() - 1)
    coef, proj = rotate(summed(local, "atoms", atom_devices, atom_bits), frame_rows, vectors)

    swap = [(i, i ^ 1) for i in range(frame_devices)]
    proj_other = lax.ppermute(proj, "frames", swap)

    def made(keep, first, after):
        late = lax.optimization_barrier((coef, after))[0]
        return displace(where_, x, mean_structure, late, line, keep, first)

    first_sent = made(False, True, proj)
    first_own = made(True, True, first_sent)
    firsts = (first_own, lax.ppermute(first_sent, "frames", swap))
    rest_sent = made(False, False, (proj_other, first_own))
    rest_sent = lax.optimization_barrier((rest_sent, firsts[1]))[0]
    rest_other = lax.ppermute(rest_sent, "frames", swap)
    scales = weights(proj, proj_other, frame_rows, vectors)

    def make_first(p):
        nonlocal last
        last = term(where_, scales, firsts, (), None, 0, line, p, pieces, vectors, width)
        return last

    def make(received, block, starts, p):
        return term(
            where_, scales, rests(), received, block, starts, line, p, pieces, vectors, width
        )

    last, kept = None, []

    def rests():
        if not kept:
            kept.append(made(True, False, last))
        return kept[0], rest_other

    right, left = along_line(line, pieces, make_first, make)
    carriers = (right[0], left[0])
    images, gram = [], None
    for p in range(pieces):
        image, gram, *more = image_piece(
            where_, scales, firsts, rests(), carriers, (right[p], left[p]),
            mean_structure if p == 0 else gram, line, p, pieces, vectors, width, frame_count,
        )
        images.append(image)
        if p == 0:
            (new_mean,) = more
    gram = fold(summed(gram, "atoms", atom_devices, atom_bits))
    gram = fold(exchanged(gram, "frames", frame_devices, [0]))
    grams = summed(gram, "frames", frame_devices, range(1, frame_devices.bit_length() - 1))
    image, basis = basis_of(grams, images, vectors, 3 * atoms * atom_devices)

    def placed(value):
        return jnp.transpose(value.reshape(3, vectors, width), (1, 0, 2))

    return new_mean, placed(image), placed(basis)


def solution(mesh):
    return jax.shard_map(
        functools.partial(per_device, mesh.shape["atoms"], mesh.shape["frames"]),
        mesh=mesh,
        in_specs=(P("frames", None, "atoms"), P(None, "atoms"), P("atoms"), P(None, None, "atoms")),
        out_specs=(
            P(None, ("atoms", "frames")),
            P(None, None, ("atoms", "frames")),
            P(None, None, ("atoms", "frames")),
        ),
        check_vma=False,
    )
```

time: 334 us -> 84.6 us (0.25)
  blocking collectives: 104 us -> 0 us
  waiting for transfers between devices: 122 us -> 23.2 us
  matrix products: 69 us -> 0 us
  starting transfers between devices: 0.04 us -> 40.1 us
  other arithmetic: 20.3 us -> 0 us
  Pallas kernels: 0 us -> 20 us
  between operations: 14.7 us -> 0.89 us
    reduce_scatter x1 -> x0, waiting for transfers between devices: 122 us -> none  [per_device(): lax.psum_scatter(stacked, 'frames', scatter_dimension=2, tiled=True)]
    psum x4 -> x0, blocking collectives: 104 us -> none  [the longest x1 39.4 us: per_device(): proj_total = lax.psum(jnp.sum(local_proj, axis=0), ('atoms', 'frames'))]
    dot_general x7 -> x0, matrix products: 66.8 us -> none  [the longest x1 29.3 us: per_device(): moved = jnp.einsum('fij,fja->fia', rotation, frames, precision=highest)]
    ppermute x0 -> x23, starting transfers between devices: none -> 40.1 us  [the longest x4 18.1 us: along_line(): next_right.append(lax.ppermute(out, 'frames', right_pairs))]
    ppermute x0 -> x23, waiting for transfers between devices: none -> 23.2 us  [the longest x10 9.39 us: exchanged(): lax.ppermute(value, axis, [(i, i ^ mask) for i in range(size)])]
    pallas_call x0 -> x22, Pallas kernels: none -> 20 us  [the longest x1 6.52 us: moments(): pl.pallas_call(moments_kernel, in_specs=[pl.BlockSpec(memory_space=pltpu....]
    another operation x28 -> x0, other arithmetic: 6.92 us -> none  [the longest x3 3.59 us: per_device(): lower = jnp.linalg.cholesky(gram)]
    concatenate x1 -> x0, other arithmetic: 5.66 us -> none  [per_device(): stacked = jnp.concatenate([term, shift_sum[None]], axis=0)]
  transfers between devices with their start and end apart: 1 -> 23, of which waited for: 1 -> 15; matrix products, arithmetic and copies ran while one was open for 0% -> 0% of each run, Pallas kernels for 0% -> 10%
where the time goes in v1:
time: 84.6 us; the launch traced here: 84.3 us
  starting transfers between devices  40.1 us (47%)
  waiting for transfers between devices  23.2 us (27%)
  Pallas kernels  20 us (24%)
  between operations  0.89 us (1%)
    ppermute x4, starting transfers between devices, along_line(): next_right.append(lax.ppermute(out, 'frames', right_pairs))  18.1 us
    ppermute x10, starting transfers between devices, exchanged(): lax.ppermute(value, axis, [(i, i ^ mask) for i in range(size)])  12.5 us
    ppermute x10, waiting for transfers between devices, exchanged(): lax.ppermute(value, axis, [(i, i ^ mask) for i in range(size)])  9.39 us
    pallas_call x1, Pallas kernels, moments(): pl.pallas_call(moments_kernel, in_specs=[pl.BlockSpec(memory_space=pltpu....  6.52 us
    ppermute x2, waiting for transfers between devices, along_line(): right = [lax.ppermute(make_first(p), 'frames', ends) for p in range(pieces)]  5.29 us
    ppermute x4, waiting for transfers between devices, along_line(): next_left.append(lax.ppermute(out, 'frames', left_pairs))  5.24 us
    pallas_call x10, Pallas kernels, term(): pl.pallas_call(functools.partial(term_kernel, block, starts, line, p, pie...  4.87 us
    ppermute x2, starting transfers between devices, along_line(): right = [lax.ppermute(make_first(p), 'frames', ends) for p in range(pieces)]  4.82 us
  transfers between devices with their start and end apart: 23, of which 15 were waited for; matrix products, arithmetic and copies ran while one was open for 0% of the time, Pallas kernels for 10%

profile of v1, /device:TPU:0, one launch (start us, length us, event | category | flops | bytes accessed | tf_op | source)
XLA Modules:
  0.0 84.3 jit_solution(17469081095311745154)
XLA Ops:
  0.6 6.5 %moments.1 = (f32[80,128]{1,0:T(8,128)S(1)}, f32[72,24576]{1,0:T(8,128)S(1)}) custom-call(s32[1]{0:T(128)} %bitcast._.idx, f32[72,24576]{1,0:T(8,128)} %bitcast.14, f32[3,24576]{1,0:T(4,128)} %refs_9_.1, f32[1,24576]{1,0:T(1,128)} %bitcast.16, bf16[96,24576]{1,0:T(8,128)(2,1)} %bitcast.15), custom_call_target="tpu_custom_call" | custom-call | tf_op jit(solution)/shard_map/moments/pallas_call | solution.py:104
  7.2 4.0 %collective-permute-start = (f32[80,128]{1,0:T(8,128)S(1)}, f32[80,128]{1,0:T(8,128)S(1)}, u32[]{:S(2)}, u32[]{:S(2)}) collective-permute-start(f32[80,128]{1,0:T(8,128)S(1)} %get-tuple-element.22.refs_0_), channel_id=1, source_target_pairs={{0,24},{8,16},{16,8},{24,0},{1,25},{9,17},{17,9},{25,1},{2,26},{10... | collective-permute-start | bytes 122888 | tf_op jit(solution)/shard_map/ppermute | solution.py:473
  11.1 0.5 collective-permute-start.1
  11.6 0.1 collective-permute-start.2
  11.8 1.3 %collective-permute-done.refs_1_ = f32[80,128]{1,0:T(8,128)S(1)} collective-permute-done((f32[80,128]{1,0:T(8,128)S(1)}, f32[80,128]{1,0:T(8,128)S(1)}, u32[]{:S(2)}, u32[]{:S(2)}) %collective-permute-start) | collective-permute-done | bytes 40992 | tf_op jit(solution)/shard_map/ppermute | solution.py:473
  13.1 2.0 %collective-permute-done.1.refs_2_ = f32[80,128]{1,0:T(8,128)S(1)} collective-permute-done((f32[80,128]{1,0:T(8,128)S(1)}, f32[80,128]{1,0:T(8,128)S(1)}, u32[]{:S(2)}, u32[]{:S(2)}) %collective-permute-start.1) | collective-permute-done | bytes 40992 | tf_op jit(solution)/shard_map/ppermute | solution.py:473
  15.1 0.5 collective-permute-done.2.refs_3_
  15.6 0.6 rotate.1
  16.2 0.3 displace.4
  16.5 0.1 collective-permute-start.4
  16.6 0.5 collective-permute-start.3
  17.1 0.3 displace.5.refs_3_
  17.3 1.0 %collective-permute-done.3.other_ref = f32[24,128]{1,0:T(8,128)S(1)} collective-permute-done((f32[24,128]{1,0:T(8,128)S(1)}, f32[24,128]{1,0:T(8,128)S(1)}, u32[]{:S(2)}, u32[]{:S(2)}) %collective-permute-start.3) | collective-permute-done | bytes 12320 | tf_op jit(solution)/shard_map/ppermute | solution.py:589
  18.4 0.9 %displace.7 = bf16[72,9216]{1,0:T(8,128)(2,1)S(1)} custom-call(s32[1]{0:T(128)} %bitcast._.idx, f32[72,24576]{1,0:T(8,128)S(1)} %get-tuple-element.27.x_ref, f32[3,24576]{1,0:T(4,128)S(1)} %copy-done, f32[288,128]{1,0:T(8,128)S(1)} %get-tuple-element.31.coef_ref), custom_call_target="tpu_custom_call" | custom-call | tf_op jit(solution)/shard_map/displace/pallas_call | solution.py:229
  19.3 0.0 collective-permute-done.4.refs_4_
  19.3 0.2 collective-permute-start.5
  19.5 0.2 weights.1
  19.7 0.4 term.11
  20.1 3.5 %collective-permute-start.6 = (bf16[96,1664]{1,0:T(8,128)(2,1)S(1)}, bf16[96,1664]{1,0:T(8,128)(2,1)S(1)}, u32[]{:S(2)}, u32[]{:S(2)}) collective-permute-start(bf16[96,1664]{1,0:T(8,128)(2,1)S(1)} %term.11), channel_id=1, source_target_pairs={{0,2},{1,3},{6,4},{7,5},{8,10},{9,11},{14,12},{15,13},{16,18},{17,... | collective-permute-start | bytes 958472 | tf_op jit(solution)/shard_map/ppermute | solution.py:548
  23.6 0.3 term.10
  23.9 1.3 %collective-permute-start.11 = (bf16[96,1536]{1,0:T(8,128)(2,1)S(1)}, bf16[96,1536]{1,0:T(8,128)(2,1)S(1)}, u32[]{:S(2)}, u32[]{:S(2)}) collective-permute-start(bf16[96,1536]{1,0:T(8,128)(2,1)S(1)} %term.10), channel_id=1, source_target_pairs={{0,2},{1,3},{6,4},{7,5},{8,10},{9,11},{14,12},{15,13},{16,18},{17,... | collective-permute-start | bytes 884744 | tf_op jit(solution)/shard_map/ppermute | solution.py:548
  25.2 0.9 %displace.6.refs_3_.refs_5_ = bf16[72,9216]{1,0:T(8,128)(2,1)S(1)} custom-call(s32[1]{0:T(128)} %bitcast._.idx, f32[72,24576]{1,0:T(8,128)S(1)} %get-tuple-element.27.x_ref, f32[3,24576]{1,0:T(4,128)S(1)} %copy-done, f32[288,128]{1,0:T(8,128)S(1)} %get-tuple-element.31.coef_ref), custom_call_target="tpu_custom_call" | custom-call | tf_op jit(solution)/shard_map/displace/pallas_call | solution.py:229
  26.2 5.3 %collective-permute-done.6.refs_5_ = bf16[96,1664]{1,0:T(8,128)(2,1)S(1)} collective-permute-done((bf16[96,1664]{1,0:T(8,128)(2,1)S(1)}, bf16[96,1664]{1,0:T(8,128)(2,1)S(1)}, u32[]{:S(2)}, u32[]{:S(2)}) %collective-permute-start.6) | collective-permute-done | bytes 319520 | tf_op jit(solution)/shard_map/ppermute | solution.py:548
  31.5 0.0 collective-permute-done.5.refs_4_.refs_6_
  31.5 0.6 term.12
  32.1 4.4 %collective-permute-start.7 = (bf16[96,1664]{1,0:T(8,128)(2,1)S(1)}, bf16[96,1664]{1,0:T(8,128)(2,1)S(1)}, u32[]{:S(2)}, u32[]{:S(2)}) collective-permute-start(bf16[96,1664]{1,0:T(8,128)(2,1)S(1)} %term.12), channel_id=1, source_target_pairs={{0,2},{1,3},{2,4},{3,5},{8,10},{9,11},{10,12},{11,13},{16,18},{17,... | collective-permute-start | bytes 958472 | tf_op jit(solution)/shard_map/ppermute | solution.py:563
  36.5 0.6 term.14
  37.1 0.7 collective-permute-start.9
  37.8 0.0 collective-permute-done.11.refs_6_
  37.8 0.5 term.16
  38.2 4.4 %collective-permute-start.12 = (bf16[96,1536]{1,0:T(8,128)(2,1)S(1)}, bf16[96,1536]{1,0:T(8,128)(2,1)S(1)}, u32[]{:S(2)}, u32[]{:S(2)}) collective-permute-start(bf16[96,1536]{1,0:T(8,128)(2,1)S(1)} %term.16), channel_id=1, source_target_pairs={{0,2},{1,3},{2,4},{3,5},{8,10},{9,11},{10,12},{11,13},{16,18},{17,... | collective-permute-start | bytes 884744 | tf_op jit(solution)/shard_map/ppermute | solution.py:563
  42.6 0.5 term.18
  43.1 0.7 collective-permute-start.14
  43.8 0.8 collective-permute-done.7.refs_5_
  44.6 0.6 term.13
  45.2 4.4 %collective-permute-start.8 = (bf16[96,1664]{1,0:T(8,128)(2,1)S(1)}, bf16[96,1664]{1,0:T(8,128)(2,1)S(1)}, u32[]{:S(2)}, u32[]{:S(2)}) collective-permute-start(bf16[96,1664]{1,0:T(8,128)(2,1)S(1)} %term.13), channel_id=1, source_target_pairs={{0,2},{1,3},{2,4},{3,5},{4,6},{5,7},{8,10},{9,11},{10,12},{11,13},... | collective-permute-start | bytes 958472 | tf_op jit(solution)/shard_map/ppermute | solution.py:563
  49.6 0.0 collective-permute-done.9.refs_5_
  49.6 0.6 term.15
  50.3 1.3 %collective-permute-start.10 = (bf16[96,1664]{1,0:T(8,128)(2,1)S(1)}, bf16[96,1664]{1,0:T(8,128)(2,1)S(1)}, u32[]{:S(2)}, u32[]{:S(2)}) collective-permute-start(bf16[96,1664]{1,0:T(8,128)(2,1)S(1)} %term.15), channel_id=1, source_target_pairs={{6,4},{7,5},{4,2},{5,3},{2,0},{3,1},{14,12},{15,13},{12,10},{13,11... | collective-permute-start | bytes 958472 | tf_op jit(solution)/shard_map/ppermute | solution.py:565
  51.6 0.4 term.17
  52.0 4.9 %collective-permute-start.13 = (bf16[96,1536]{1,0:T(8,128)(2,1)S(1)}, bf16[96,1536]{1,0:T(8,128)(2,1)S(1)}, u32[]{:S(2)}, u32[]{:S(2)}) collective-permute-start(bf16[96,1536]{1,0:T(8,128)(2,1)S(1)} %term.17), channel_id=1, source_target_pairs={{0,2},{1,3},{2,4},{3,5},{4,6},{5,7},{8,10},{9,11},{10,12},{11,13},... | collective-permute-start | bytes 884744 | tf_op jit(solution)/shard_map/ppermute | solution.py:563
  56.9 0.0 collective-permute-done.14.refs_6_
  56.9 0.4 term.19
  57.3 1.3 %collective-permute-start.15 = (bf16[96,1536]{1,0:T(8,128)(2,1)S(1)}, bf16[96,1536]{1,0:T(8,128)(2,1)S(1)}, u32[]{:S(2)}, u32[]{:S(2)}) collective-permute-start(bf16[96,1536]{1,0:T(8,128)(2,1)S(1)} %term.19), channel_id=1, source_target_pairs={{6,4},{7,5},{4,2},{5,3},{2,0},{3,1},{14,12},{15,13},{12,10},{13,11... | collective-permute-start | bytes 884744 | tf_op jit(solution)/shard_map/ppermute | solution.py:565
  58.6 0.0 collective-permute-done.8.refs_7_
  58.7 2.2 %collective-permute-done.10.refs_8_ = bf16[96,1664]{1,0:T(8,128)(2,1)S(1)} collective-permute-done((bf16[96,1664]{1,0:T(8,128)(2,1)S(1)}, bf16[96,1664]{1,0:T(8,128)(2,1)S(1)}, u32[]{:S(2)}, u32[]{:S(2)}) %collective-permute-start.10) | collective-permute-done | bytes 319520 | tf_op jit(solution)/shard_map/ppermute | solution.py:565
  60.8 1.3 %image_piece.2 = (f32[96,1536]{1,0:T(8,128)S(1)}, f32[8,128]{1,0:T(8,128)S(1)}, f32[3,3072]{1,0:T(4,128)}) custom-call(s32[1]{0:T(128)} %bitcast._.idx, bf16[96,72]{1,0:T(8,128)(2,1)S(1)} %get-tuple-element.24.refs_0_, bf16[96,72]{1,0:T(8,128)(2,1)S(1)} %get-tuple-element.25.refs_1_, f32[8,128]{1,0:T(8,128)S(1)} %get-tuple-element.26.refs_2_, ...), custom_call_target="tpu_custom_call" | custom-call | tf_op jit(solution)/shard_map/image_piece/pallas_call | solution.py:439
  62.1 1.4 %collective-permute-done.13.refs_10_ = bf16[96,1536]{1,0:T(8,128)(2,1)S(1)} collective-permute-done((bf16[96,1536]{1,0:T(8,128)(2,1)S(1)}, bf16[96,1536]{1,0:T(8,128)(2,1)S(1)}, u32[]{:S(2)}, u32[]{:S(2)}) %collective-permute-start.13) | collective-permute-done | bytes 294944 | tf_op jit(solution)/shard_map/ppermute | solution.py:563
  63.6 3.1 %collective-permute-done.15.refs_11_ = bf16[96,1536]{1,0:T(8,128)(2,1)S(1)} collective-permute-done((bf16[96,1536]{1,0:T(8,128)(2,1)S(1)}, bf16[96,1536]{1,0:T(8,128)(2,1)S(1)}, u32[]{:S(2)}, u32[]{:S(2)}) %collective-permute-start.15) | collective-permute-done | bytes 294944 | tf_op jit(solution)/shard_map/ppermute | solution.py:565
  66.6 1.2 %image_piece.3 = (f32[96,1536]{1,0:T(8,128)S(1)}, f32[8,128]{1,0:T(8,128)S(1)}) custom-call(s32[1]{0:T(128)} %bitcast._.idx, bf16[96,72]{1,0:T(8,128)(2,1)S(1)} %get-tuple-element.24.refs_0_, bf16[96,72]{1,0:T(8,128)(2,1)S(1)} %get-tuple-element.25.refs_1_, f32[8,128]{1,0:T(8,128)S(1)} %get-tuple-element.26.refs_2_, bf16[72,3072]{1,0:T(8,128)(2,1)S(1)} %displace.5.refs_3_, ...), custom_call_target="tpu_custom_call" | custom-call | tf_op jit(solution)/shard_map/image_piece/pallas_call | solution.py:439
  67.8 1.5 %collective-permute-start.16 = (f32[8,128]{1,0:T(8,128)S(1)}, f32[8,128]{1,0:T(8,128)S(1)}, u32[]{:S(2)}, u32[]{:S(2)}) collective-permute-start(f32[8,128]{1,0:T(8,128)S(1)} %get-tuple-element.35.refs_0_), channel_id=1, source_target_pairs={{0,24},{8,16},{16,8},{24,0},{1,25},{9,17},{17,9},{25,1},{2,26},{10... | collective-permute-start | bytes 12296 | tf_op jit(solution)/shard_map/ppermute | solution.py:473
  69.3 0.5 collective-permute-start.17
  69.8 1.5 %collective-permute-start.18 = (f32[8,128]{1,0:T(8,128)S(1)}, f32[8,128]{1,0:T(8,128)S(1)}, u32[]{:S(2)}, u32[]{:S(2)}) collective-permute-start(f32[8,128]{1,0:T(8,128)S(1)} %get-tuple-element.35.refs_0_), channel_id=1, source_target_pairs={{0,8},{8,0},{16,24},{24,16},{1,9},{9,1},{17,25},{25,17},{2,10},{10... | collective-permute-start | bytes 12296 | tf_op jit(solution)/shard_map/ppermute | solution.py:473
  71.3 1.0 %collective-permute-done.16.refs_1_ = f32[8,128]{1,0:T(8,128)S(1)} collective-permute-done((f32[8,128]{1,0:T(8,128)S(1)}, f32[8,128]{1,0:T(8,128)S(1)}, u32[]{:S(2)}, u32[]{:S(2)}) %collective-permute-start.16) | collective-permute-done | bytes 4128 | tf_op jit(solution)/shard_map/ppermute | solution.py:473
  72.3 0.6 collective-permute-done.17.refs_2_
  72.9 0.5 collective-permute-done.18.refs_3_
  73.4 0.0 collective-permute-start.19
  73.5 1.2 %collective-permute-done.19.refs_1_ = f32[8,128]{1,0:T(8,128)S(1)} collective-permute-done((f32[8,128]{1,0:T(8,128)S(1)}, f32[8,128]{1,0:T(8,128)S(1)}, u32[]{:S(2)}, u32[]{:S(2)}) %collective-permute-start.19) | collective-permute-done | bytes 4128 | tf_op jit(solution)/shard_map/ppermute | solution.py:473
  74.6 3.0 %collective-permute-start.21 = (f32[8,128]{1,0:T(8,128)S(1)}, f32[8,128]{1,0:T(8,128)S(1)}, u32[]{:S(2)}, u32[]{:S(2)}) collective-permute-start(f32[8,128]{1,0:T(8,128)S(1)} %fold.3.refs_0_), channel_id=1, source_target_pairs={{0,4},{1,5},{2,6},{3,7},{4,0},{5,1},{6,2},{7,3},{8,12},{9,13},{10,... | collective-permute-start | bytes 12296 | tf_op jit(solution)/shard_map/ppermute | solution.py:473
  77.6 1.4 %collective-permute-start.22 = (f32[8,128]{1,0:T(8,128)S(1)}, f32[8,128]{1,0:T(8,128)S(1)}, u32[]{:S(2)}, u32[]{:S(2)}) collective-permute-start(f32[8,128]{1,0:T(8,128)S(1)} %fold.3.refs_0_), channel_id=1, source_target_pairs={{0,2},{1,3},{2,0},{3,1},{4,6},{5,7},{6,4},{7,5},{8,10},{9,11},{10,... | collective-permute-start | bytes 12296 | tf_op jit(solution)/shard_map/ppermute | solution.py:473
  79.0 1.0 %collective-permute-done.20.refs_1_ = f32[8,128]{1,0:T(8,128)S(1)} collective-permute-done((f32[8,128]{1,0:T(8,128)S(1)}, f32[8,128]{1,0:T(8,128)S(1)}, u32[]{:S(2)}, u32[]{:S(2)}) %collective-permute-start.20) | collective-permute-done | bytes 4128 | tf_op jit(solution)/shard_map/ppermute | solution.py:473
  80.0 0.0 collective-permute-done.21.refs_2_
  80.0 1.2 %collective-permute-done.22.refs_3_ = f32[8,128]{1,0:T(8,128)S(1)} collective-permute-done((f32[8,128]{1,0:T(8,128)S(1)}, f32[8,128]{1,0:T(8,128)S(1)}, u32[]{:S(2)}, u32[]{:S(2)}) %collective-permute-start.22) | collective-permute-done | bytes 4128 | tf_op jit(solution)/shard_map/ppermute | solution.py:473
  81.3 3.0 %basis.1 = (f32[96,3072]{1,0:T(8,128)}, f32[96,3072]{1,0:T(8,128)}) custom-call(f32[8,128]{1,0:T(8,128)S(1)} %fold.3.refs_0_, f32[8,128]{1,0:T(8,128)S(1)} %collective-permute-done.20.refs_1_, f32[8,128]{1,0:T(8,128)S(1)} %collective-permute-done.21.refs_2_, f32[8,128]{1,0:T(8,128)S(1)} %collective-permute-done.22.refs_3_, ...), custom_call_target="tpu_custom_call" | custom-call | tf_op jit(solution)/shard_map/basis/pallas_call | solution.py:530
  (6 shorter events, 0.0 us)
Async XLA Ops:
  0.6 15.6 %copy-start = (f32[3,24576]{1,0:T(4,128)S(1)}, f32[3,24576]{1,0:T(4,128)}, u32[]{:S(2)}) copy-start(f32[3,24576]{1,0:T(4,128)} %refs_9_.1) | copy-start | bytes 884740
  7.2 5.9 %collective-permute-start = (f32[80,128]{1,0:T(8,128)S(1)}, f32[80,128]{1,0:T(8,128)S(1)}, u32[]{:S(2)}, u32[]{:S(2)}) collective-permute-start(f32[80,128]{1,0:T(8,128)S(1)} %get-tuple-element.22.refs_0_), channel_id=1, source_target_pairs={{0,24},{8,16},{16,8},{24,0},{1,25},{9,17},{17,9},{25,1},{2,26},{10... | collective-permute-start | bytes 122888 | tf_op jit(solution)/shard_map/ppermute | solution.py:473
  11.1 4.0 %collective-permute-start.1 = (f32[80,128]{1,0:T(8,128)S(1)}, f32[80,128]{1,0:T(8,128)S(1)}, u32[]{:S(2)}, u32[]{:S(2)}) collective-permute-start(f32[80,128]{1,0:T(8,128)S(1)} %get-tuple-element.22.refs_0_), channel_id=1, source_target_pairs={{0,16},{8,24},{16,0},{24,8},{1,17},{9,25},{17,1},{25,9},{2,18},{10... | collective-permute-start | bytes 122888 | tf_op jit(solution)/shard_map/ppermute | solution.py:473
  11.6 4.0 %collective-permute-start.2 = (f32[80,128]{1,0:T(8,128)S(1)}, f32[80,128]{1,0:T(8,128)S(1)}, u32[]{:S(2)}, u32[]{:S(2)}) collective-permute-start(f32[80,128]{1,0:T(8,128)S(1)} %get-tuple-element.22.refs_0_), channel_id=1, source_target_pairs={{0,8},{8,0},{16,24},{24,16},{1,9},{9,1},{17,25},{25,17},{2,10},{10... | collective-permute-start | bytes 122888 | tf_op jit(solution)/shard_map/ppermute | solution.py:473
  16.5 2.8 %collective-permute-start.4 = (bf16[72,3072]{1,0:T(8,128)(2,1)S(1)}, bf16[72,3072]{1,0:T(8,128)(2,1)S(1)}, u32[]{:S(2)}, u32[]{:S(2)}) collective-permute-start(bf16[72,3072]{1,0:T(8,128)(2,1)S(1)} %displace.4), channel_id=1, source_target_pairs={{0,1},{1,0},{2,3},{3,2},{4,5},{5,4},{6,7},{7,6},{8,9},{9,8},{10,11... | collective-permute-start | bytes 1327112 | tf_op jit(solution)/shard_map/ppermute | solution.py:597
  16.6 1.8 %collective-permute-start.3 = (f32[24,128]{1,0:T(8,128)S(1)}, f32[24,128]{1,0:T(8,128)S(1)}, u32[]{:S(2)}, u32[]{:S(2)}) collective-permute-start(f32[24,128]{1,0:T(8,128)S(1)} %get-tuple-element.23.own_ref), channel_id=1, source_target_pairs={{0,1},{1,0},{2,3},{3,2},{4,5},{5,4},{6,7},{7,6},{8,9},{9,8},{10,11... | collective-permute-start | bytes 36872 | tf_op jit(solution)/shard_map/ppermute | solution.py:589
  19.3 12.1 %collective-permute-start.5 = (bf16[72,9216]{1,0:T(8,128)(2,1)S(1)}, bf16[72,9216]{1,0:T(8,128)(2,1)S(1)}, u32[]{:S(2)}, u32[]{:S(2)}) collective-permute-start(bf16[72,9216]{1,0:T(8,128)(2,1)S(1)} %displace.7), channel_id=1, source_target_pairs={{0,1},{1,0},{2,3},{3,2},{4,5},{5,4},{6,7},{7,6},{8,9},{9,8},{10,11... | collective-permute-start | bytes 3981320 | tf_op jit(solution)/shard_map/ppermute | solution.py:600
  20.1 11.4 %collective-permute-start.6 = (bf16[96,1664]{1,0:T(8,128)(2,1)S(1)}, bf16[96,1664]{1,0:T(8,128)(2,1)S(1)}, u32[]{:S(2)}, u32[]{:S(2)}) collective-permute-start(bf16[96,1664]{1,0:T(8,128)(2,1)S(1)} %term.11), channel_id=1, source_target_pairs={{0,2},{1,3},{6,4},{7,5},{8,10},{9,11},{14,12},{15,13},{16,18},{17,... | collective-permute-start | bytes 958472 | tf_op jit(solution)/shard_map/ppermute | solution.py:548
  23.9 13.9 %collective-permute-start.11 = (bf16[96,1536]{1,0:T(8,128)(2,1)S(1)}, bf16[96,1536]{1,0:T(8,128)(2,1)S(1)}, u32[]{:S(2)}, u32[]{:S(2)}) collective-permute-start(bf16[96,1536]{1,0:T(8,128)(2,1)S(1)} %term.10), channel_id=1, source_target_pairs={{0,2},{1,3},{6,4},{7,5},{8,10},{9,11},{14,12},{15,13},{16,18},{17,... | collective-permute-start | bytes 884744 | tf_op jit(solution)/shard_map/ppermute | solution.py:548
  32.1 12.6 %collective-permute-start.7 = (bf16[96,1664]{1,0:T(8,128)(2,1)S(1)}, bf16[96,1664]{1,0:T(8,128)(2,1)S(1)}, u32[]{:S(2)}, u32[]{:S(2)}) collective-permute-start(bf16[96,1664]{1,0:T(8,128)(2,1)S(1)} %term.12), channel_id=1, source_target_pairs={{0,2},{1,3},{2,4},{3,5},{8,10},{9,11},{10,12},{11,13},{16,18},{17,... | collective-permute-start | bytes 958472 | tf_op jit(solution)/shard_map/ppermute | solution.py:563
  37.1 12.6 %collective-permute-start.9 = (bf16[96,1664]{1,0:T(8,128)(2,1)S(1)}, bf16[96,1664]{1,0:T(8,128)(2,1)S(1)}, u32[]{:S(2)}, u32[]{:S(2)}) collective-permute-start(bf16[96,1664]{1,0:T(8,128)(2,1)S(1)} %term.14), channel_id=1, source_target_pairs={{6,4},{7,5},{4,2},{5,3},{14,12},{15,13},{12,10},{13,11},{22,20},{2... | collective-permute-start | bytes 958472 | tf_op jit(solution)/shard_map/ppermute | solution.py:565
  38.2 13.3 %collective-permute-start.12 = (bf16[96,1536]{1,0:T(8,128)(2,1)S(1)}, bf16[96,1536]{1,0:T(8,128)(2,1)S(1)}, u32[]{:S(2)}, u32[]{:S(2)}) collective-permute-start(bf16[96,1536]{1,0:T(8,128)(2,1)S(1)} %term.16), channel_id=1, source_target_pairs={{0,2},{1,3},{2,4},{3,5},{8,10},{9,11},{10,12},{11,13},{16,18},{17,... | collective-permute-start | bytes 884744 | tf_op jit(solution)/shard_map/ppermute | solution.py:563
  43.1 13.8 %collective-permute-start.14 = (bf16[96,1536]{1,0:T(8,128)(2,1)S(1)}, bf16[96,1536]{1,0:T(8,128)(2,1)S(1)}, u32[]{:S(2)}, u32[]{:S(2)}) collective-permute-start(bf16[96,1536]{1,0:T(8,128)(2,1)S(1)} %term.18), channel_id=1, source_target_pairs={{6,4},{7,5},{4,2},{5,3},{14,12},{15,13},{12,10},{13,11},{22,20},{2... | collective-permute-start | bytes 884744 | tf_op jit(solution)/shard_map/ppermute | solution.py:565
  45.2 13.4 %collective-permute-start.8 = (bf16[96,1664]{1,0:T(8,128)(2,1)S(1)}, bf16[96,1664]{1,0:T(8,128)(2,1)S(1)}, u32[]{:S(2)}, u32[]{:S(2)}) collective-permute-start(bf16[96,1664]{1,0:T(8,128)(2,1)S(1)} %term.13), channel_id=1, source_target_pairs={{0,2},{1,3},{2,4},{3,5},{4,6},{5,7},{8,10},{9,11},{10,12},{11,13},... | collective-permute-start | bytes 958472 | tf_op jit(solution)/shard_map/ppermute | solution.py:563
  50.3 10.6 %collective-permute-start.10 = (bf16[96,1664]{1,0:T(8,128)(2,1)S(1)}, bf16[96,1664]{1,0:T(8,128)(2,1)S(1)}, u32[]{:S(2)}, u32[]{:S(2)}) collective-permute-start(bf16[96,1664]{1,0:T(8,128)(2,1)S(1)} %term.15), channel_id=1, source_target_pairs={{6,4},{7,5},{4,2},{5,3},{2,0},{3,1},{14,12},{15,13},{12,10},{13,11... | collective-permute-start | bytes 958472 | tf_op jit(solution)/shard_map/ppermute | solution.py:565
  52.0 11.5 %collective-permute-start.13 = (bf16[96,1536]{1,0:T(8,128)(2,1)S(1)}, bf16[96,1536]{1,0:T(8,128)(2,1)S(1)}, u32[]{:S(2)}, u32[]{:S(2)}) collective-permute-start(bf16[96,1536]{1,0:T(8,128)(2,1)S(1)} %term.17), channel_id=1, source_target_pairs={{0,2},{1,3},{2,4},{3,5},{4,6},{5,7},{8,10},{9,11},{10,12},{11,13},... | collective-permute-start | bytes 884744 | tf_op jit(solution)/shard_map/ppermute | solution.py:563
  57.3 9.3 %collective-permute-start.15 = (bf16[96,1536]{1,0:T(8,128)(2,1)S(1)}, bf16[96,1536]{1,0:T(8,128)(2,1)S(1)}, u32[]{:S(2)}, u32[]{:S(2)}) collective-permute-start(bf16[96,1536]{1,0:T(8,128)(2,1)S(1)} %term.19), channel_id=1, source_target_pairs={{6,4},{7,5},{4,2},{5,3},{2,0},{3,1},{14,12},{15,13},{12,10},{13,11... | collective-permute-start | bytes 884744 | tf_op jit(solution)/shard_map/ppermute | solution.py:565
  67.8 4.6 %collective-permute-start.16 = (f32[8,128]{1,0:T(8,128)S(1)}, f32[8,128]{1,0:T(8,128)S(1)}, u32[]{:S(2)}, u32[]{:S(2)}) collective-permute-start(f32[8,128]{1,0:T(8,128)S(1)} %get-tuple-element.35.refs_0_), channel_id=1, source_target_pairs={{0,24},{8,16},{16,8},{24,0},{1,25},{9,17},{17,9},{25,1},{2,26},{10... | collective-permute-start | bytes 12296 | tf_op jit(solution)/shard_map/ppermute | solution.py:473
  69.3 3.6 %collective-permute-start.17 = (f32[8,128]{1,0:T(8,128)S(1)}, f32[8,128]{1,0:T(8,128)S(1)}, u32[]{:S(2)}, u32[]{:S(2)}) collective-permute-start(f32[8,128]{1,0:T(8,128)S(1)} %get-tuple-element.35.refs_0_), channel_id=1, source_target_pairs={{0,16},{8,24},{16,0},{24,8},{1,17},{9,25},{17,1},{25,9},{2,18},{10... | collective-permute-start | bytes 12296 | tf_op jit(solution)/shard_map/ppermute | solution.py:473
  69.8 3.6 %collective-permute-start.18 = (f32[8,128]{1,0:T(8,128)S(1)}, f32[8,128]{1,0:T(8,128)S(1)}, u32[]{:S(2)}, u32[]{:S(2)}) collective-permute-start(f32[8,128]{1,0:T(8,128)S(1)} %get-tuple-element.35.refs_0_), channel_id=1, source_target_pairs={{0,8},{8,0},{16,24},{24,16},{1,9},{9,1},{17,25},{25,17},{2,10},{10... | collective-permute-start | bytes 12296 | tf_op jit(solution)/shard_map/ppermute | solution.py:473
  73.4 1.2 %collective-permute-start.19 = (f32[8,128]{1,0:T(8,128)S(1)}, f32[8,128]{1,0:T(8,128)S(1)}, u32[]{:S(2)}, u32[]{:S(2)}) collective-permute-start(f32[8,128]{1,0:T(8,128)S(1)} %fold.2.refs_0_), channel_id=1, source_target_pairs={{0,1},{1,0},{2,3},{3,2},{4,5},{5,4},{6,7},{7,6},{8,9},{9,8},{10,11... | collective-permute-start | bytes 12296 | tf_op jit(solution)/shard_map/ppermute | solution.py:473
  74.6 5.4 %collective-permute-start.20 = (f32[8,128]{1,0:T(8,128)S(1)}, f32[8,128]{1,0:T(8,128)S(1)}, u32[]{:S(2)}, u32[]{:S(2)}) collective-permute-start(f32[8,128]{1,0:T(8,128)S(1)} %fold.3.refs_0_), channel_id=1, source_target_pairs={{0,6},{1,7},{2,4},{3,5},{4,2},{5,3},{6,0},{7,1},{8,14},{9,15},{10,... | collective-permute-start | bytes 12296 | tf_op jit(solution)/shard_map/ppermute | solution.py:473
  74.6 5.4 %collective-permute-start.21 = (f32[8,128]{1,0:T(8,128)S(1)}, f32[8,128]{1,0:T(8,128)S(1)}, u32[]{:S(2)}, u32[]{:S(2)}) collective-permute-start(f32[8,128]{1,0:T(8,128)S(1)} %fold.3.refs_0_), channel_id=1, source_target_pairs={{0,4},{1,5},{2,6},{3,7},{4,0},{5,1},{6,2},{7,3},{8,12},{9,13},{10,... | collective-permute-start | bytes 12296 | tf_op jit(solution)/shard_map/ppermute | solution.py:473
  77.6 3.6 %collective-permute-start.22 = (f32[8,128]{1,0:T(8,128)S(1)}, f32[8,128]{1,0:T(8,128)S(1)}, u32[]{:S(2)}, u32[]{:S(2)}) collective-permute-start(f32[8,128]{1,0:T(8,128)S(1)} %fold.3.refs_0_), channel_id=1, source_target_pairs={{0,2},{1,3},{2,0},{3,1},{4,6},{5,7},{6,4},{7,5},{8,10},{9,11},{10,... | collective-permute-start | bytes 12296 | tf_op jit(solution)/shard_map/ppermute | solution.py:473

commit v2 on v1

--- a/solution.py
+++ b/solution.py
@@ -18,6 +18,10 @@
 
 def params():
     return pltpu.CompilerParams(vmem_limit_bytes=VMEM_LIMIT)
+
+
+def cost(weight):
+    return pl.CostEstimate(flops=weight * 10**9, bytes_accessed=1, transcendentals=0)
 
 
 def in_vmem(count):
@@ -296,7 +300,7 @@
         slab_ref[at : at + 1, :] = piece.astype(F32)
 
 
-def term_kernel(block, starts, line, p, pieces, vectors, width, idx, *refs):
+def term_kernel(block, starts, line, p, spans, vectors, width, idx, *refs):
     (c_ref, e_ref, mean_ref, a_ref, b_ref), refs = refs[0:5], list(refs[5:])
     slab_ref = refs.pop() if p == 0 else None
     out_ref = refs.pop()
@@ -306,17 +310,17 @@
     else:
         at = block(chip)
         at = jnp.clip(at - (at > first_block(chip, line)).astype(jnp.int32), 0, line - 2)
-    piece_width = width // pieces
-    lanes = pl.ds(pl.multiple_of(at * width + p * piece_width, LANES), piece_width)
+    offset, piece_width = spans[p]
+    lanes = pl.ds(pl.multiple_of(at * width + offset, LANES), piece_width)
     value = both(c_ref[...], e_ref[...], a_ref[:, lanes], b_ref[:, lanes])
     mean = mean_ref[0:1, :]
     center, total = mean, mean
     slab = jnp.zeros((value.shape[0], LANES), F32)
     ones = ones_rows(a_ref.shape[0])
     if refs:
-        slab = refs[0][:, piece_width:].astype(F32)
-        before, summed_means = read_slab(slab, width)
-        center = jnp.where(chip == starts, mean, before)
+        slab = refs[0][:, spans[0][1] :].astype(F32)
+        center, summed_means = read_slab(slab, width)
+        center = jnp.where(starts(chip), mean, center)
         total = mean + summed_means
         column = as_column(mean - center, vectors)
         sums = both(ones, ones, a_ref[:, lanes], b_ref[:, lanes])
@@ -331,26 +335,27 @@
         out_ref[:, piece_width:] = slab_ref[...].astype(BF16)
 
 
-def term(where_, scales, displaced, received, block, starts, line, p, pieces, vectors, width):
+def term(where_, scales, displaced, received, block, starts, line, p, spans, vectors, width):
     rows = scales[0].shape[0]
     args = (*scales, *displaced, *received)
-    out_width = width // pieces + (LANES if p == 0 else 0)
+    out_width = spans[p][1] + (LANES if p == 0 else 0)
     return pl.pallas_call(
-        functools.partial(term_kernel, block, starts, line, p, pieces, vectors, width),
+        functools.partial(term_kernel, block, starts, line, p, spans, vectors, width),
         in_specs=[pl.BlockSpec(memory_space=pltpu.SMEM)] + in_vmem(len(args)),
         out_specs=pl.BlockSpec(memory_space=pltpu.VMEM),
         out_shape=jax.ShapeDtypeStruct((rows, out_width), BF16),
         scratch_shapes=[pltpu.VMEM((rows, LANES), F32)] if p == 0 else [],
         compiler_params=params(),
+        cost_estimate=cost(1),
         name="term",
     )(where_, *args)
 
 
-def image_kernel(line, p, pieces, vectors, width, frame_count, idx, *refs):
+def image_kernel(carrier_count, line, p, spans, vectors, width, frame_count, idx, *refs):
     refs = list(refs)
     c_ref, e_ref, mean_ref = [refs.pop(0) for _ in range(3)]
     firsts, rests = [[refs.pop(0) for _ in range(2)] for _ in range(2)]
-    carriers = [refs.pop(0) for _ in range(2)]
+    carriers = [refs.pop(0) for _ in range(carrier_count)]
     other_ref = refs.pop(0)
     block_ref = refs.pop()
     new_mean_ref = refs.pop() if p == 0 else None
@@ -369,8 +374,8 @@
         def _(n=n):
             block_ref[n] = rests[n][:, pl.ds(at, width)]
 
-    piece_width = width // pieces
-    lanes = slice(p * piece_width, (p + 1) * piece_width)
+    offset, piece_width = spans[p]
+    lanes = slice(offset, offset + piece_width)
     value = both(c_ref[...], e_ref[...], block_ref[0, :, lanes], block_ref[1, :, lanes])
     for ref in received:
         value = value + ref[:, 0:piece_width].astype(F32)
@@ -378,16 +383,16 @@
     ones = ones_rows(block_ref.shape[1])
     sums = both(ones, ones, block_ref[0], block_ref[1])
     mean = mean_ref[0:1, :]
-    slabs = [ref[:, piece_width:].astype(F32) for ref in carriers]
+    slabs = [ref[:, spans[0][1] :].astype(F32) for ref in carriers]
     centers, totals = zip(*(read_slab(slab, width) for slab in slabs))
-    center = (mean + totals[0] + totals[1]) / line
+    center = functools.reduce(jnp.add, totals, mean) / line
     columns = [as_column(v - center, vectors) for v in (mean, *centers)]
-    tiles, piece_tiles = width // LANES, piece_width // LANES
+    tiles = width // LANES
     gram = jnp.zeros((2 * vectors, LANES), F32)
     for i in range(3):
         rows = slice(i * vectors, (i + 1) * vectors)
         moved = []
-        for tile in range(p * piece_tiles, (p + 1) * piece_tiles):
+        for tile in range(offset // LANES, (offset + piece_width) // LANES):
             part = columns[0] * sums[i : i + 1, tile * LANES : (tile + 1) * LANES]
             row = i * tiles + tile
             for column, slab in zip(columns[1:], slabs):
@@ -411,7 +416,7 @@
         packed = packed + other_ref[...]
     gram_ref[...] = packed
     if p == 0:
-        total = slabs[0] + slabs[1]
+        total = functools.reduce(jnp.add, slabs)
         for i in range(3):
             for tile in range(tiles):
                 start = (idx[0] * tiles + tile) * LANES
@@ -423,13 +428,13 @@
 
 
 def image_piece(
-    where_, scales, firsts, rests, carriers, received, other, line, p, pieces, vectors, width,
+    where_, scales, firsts, rests, carriers, received, other, line, p, spans, vectors, width,
     frame_count,
 ):
     rows = scales[0].shape[0]
     args = [*scales, *firsts, *rests, *carriers, other]
     out_shape = [
-        jax.ShapeDtypeStruct((rows, width // pieces), F32),
+        jax.ShapeDtypeStruct((rows, spans[p][1]), F32),
         jax.ShapeDtypeStruct((8, LANES), F32),
     ]
     if p == 0:
@@ -437,12 +442,15 @@
     else:
         args += received
     return pl.pallas_call(
-        functools.partial(image_kernel, line, p, pieces, vectors, width, frame_count),
+        functools.partial(
+            image_kernel, len(carriers), line, p, spans, vectors, width, frame_count
+        ),
         in_specs=[pl.BlockSpec(memory_space=pltpu.SMEM)] + in_vmem(len(args)),
         out_specs=in_vmem(len(out_shape)),
         out_shape=out_shape,
         scratch_shapes=[pltpu.VMEM((2, firsts[0].shape[0], width), BF16)],
         compiler_params=params(),
+        cost_estimate=cost(2),
         name="image_piece",
     )(where_, *args)
 
@@ -482,7 +490,14 @@
 
 
 def basis_kernel(vectors, coordinates, gram_count, *refs):
-    grams, pieces, (image_ref, basis_ref) = refs[:gram_count], refs[gram_count:-2], refs[-2:]
+    grams, pieces = refs[:gram_count], refs[gram_count:-4]
+    image_hbm, basis_hbm, basis_ref, sems = refs[-4:]
+    copies, starts = [], [0]
+    for n, ref in enumerate(pieces):
+        starts.append(starts[n] + ref.shape[1])
+        lanes = pl.ds(starts[n], ref.shape[1])
+        copies.append(pltpu.make_async_copy(ref, image_hbm.at[:, lanes], sems.at[n, 3]))
+        copies[-1].start()
     packed = grams[0][...]
     for ref in grams[1:]:
         packed = packed + ref[...]
@@ -511,17 +526,21 @@
     high = a.astype(BF16).astype(F32)
     left = high + pltpu.roll(high, vectors, 1) + pltpu.roll(a - high, 2 * vectors, 1)
     left = left.astype(BF16)[:, 0 : 3 * vectors]
-    start = 0
-    for ref in pieces:
-        lanes = slice(start, start + ref.shape[1])
-        start += ref.shape[1]
+    for n, ref in enumerate(pieces):
         for i in range(3):
-            rows = slice(i * vectors, (i + 1) * vectors)
+            rows, lanes = pl.ds(i * vectors, vectors), pl.ds(starts[n], ref.shape[1])
             part = ref[rows, :]
             high = part.astype(BF16)
             low = (part - high.astype(F32)).astype(BF16)
             basis_ref[rows, lanes] = dot_nn(left, jnp.concatenate([high, low, high], axis=0))
-            image_ref[rows, lanes] = part
+            copies.append(
+                pltpu.make_async_copy(
+                    basis_ref.at[rows, lanes], basis_hbm.at[rows, lanes], sems.at[n, i]
+                )
+            )
+            copies[-1].start()
+    for copy in copies:
+        copy.wait()
 
 
 def basis_of(grams, images, vectors, coordinates):
@@ -530,20 +549,58 @@
     return pl.pallas_call(
         functools.partial(basis_kernel, vectors, coordinates, len(grams)),
         in_specs=in_vmem(len(grams) + len(images)),
-        out_specs=in_vmem(2),
+        out_specs=[pl.BlockSpec(memory_space=pl.ANY)] * 2,
         out_shape=[jax.ShapeDtypeStruct((rows, width), F32)] * 2,
+        scratch_shapes=[
+            pltpu.VMEM((rows, width), F32),
+            pltpu.SemaphoreType.DMA((len(images), 4)),
+        ],
         compiler_params=params(),
         name="basis",
     )(*grams, *images)
 
 
+def to_right(z):
+    return [(2 * z + core, 2 * z + 2 + core) for core in range(2)]
+
+
+def to_left(z):
+    return [(2 * z + core, 2 * z - 2 + core) for core in range(2)]
+
+
+def along_four(pieces, make_first, make):
+    inward, middle, outward = (to_right(z) + to_left(3 - z) for z in range(3))
+
+    def at_end(chip):
+        return jnp.logical_or(chip == 0, chip == 3)
+
+    def never(chip):
+        return chip < 0
+
+    def choose(*blocks):
+        def block(chip):
+            return sum(jnp.where(chip == z, d, 0) for z, d in enumerate(blocks))
+
+        return block
+
+    each = range(pieces)
+    first = [lax.ppermute(make_first(p), "frames", inward) for p in each]
+    ends, middles = [], []
+    for p in each:
+        out = make((), choose(2, 0, 0, 1), None, p, first[p])
+        ends.append(lax.ppermute(out, "frames", inward))
+        out = make(first[: p + 1], choose(0, 3, 0, 0), never, p)
+        middles.append(lax.ppermute(out, "frames", middle))
+    arrived = []
+    for p in each:
+        out = make(middles[: p + 1], choose(1, 0, 3, 2), at_end, p, ends[p])
+        end = lax.ppermute(out, "frames", inward + outward)
+        out = make(ends[: p + 1], choose(0, 2, 1, 0), never, p, out)
+        arrived.append([end, lax.ppermute(out, "frames", middle)])
+    return arrived
+
+
 def along_line(line, pieces, make_first, make):
-    def to_right(z):
-        return [(2 * z + core, 2 * z + 2 + core) for core in range(2)]
-
-    def to_left(z):
-        return [(2 * z + core, 2 * z - 2 + core) for core in range(2)]
-
     ends = to_right(0) + to_left(line - 1)
     right = [lax.ppermute(make_first(p), "frames", ends) for p in range(pieces)]
     left = list(right)
@@ -559,12 +616,12 @@
         left_pairs = [pair for z in range(step) for pair in to_left(line - 1 - z)]
         next_right, next_left = [], []
         for p in range(pieces):
-            out = make(right[: p + 1], right_block, 0, p)
+            out = make(right[: p + 1], right_block, lambda chip: chip == 0, p)
             next_right.append(lax.ppermute(out, "frames", right_pairs))
-            out = make(left[: p + 1], left_block, line - 1, p)
+            out = make(left[: p + 1], left_block, lambda chip: chip == line - 1, p)
             next_left.append(lax.ppermute(out, "frames", left_pairs))
         right, left = next_right, next_left
-    return right, left
+    return [[right[p], left[p]] for p in range(pieces)]
 
 
 def per_device(atom_devices, frame_devices, frames, mean_structure, atom_weight, subspace):
@@ -573,8 +630,10 @@
     frame_count = frame_rows * frame_devices
     width = atoms // frame_devices
     line = frame_devices // 2
-    pieces = 2 if (width // LANES) % 2 == 0 else 1
-    assert line > 2 and 3 * width // LANES + 6 <= 3 * vectors
+    tiles = width // LANES
+    assert line > 2 and tiles > 1 and 3 * tiles + 6 <= 3 * vectors
+    cut = tiles // 2 * LANES
+    spans = ((0, cut), (cut, width - cut))
 
     x = jnp.transpose(frames, (1, 0, 2)).reshape(3 * frame_rows, atoms)
     sub = jnp.transpose(subspace, (1, 0, 2)).reshape(3 * vectors, atoms)
@@ -595,35 +654,38 @@
     first_sent = made(False, True, proj)
     first_own = made(True, True, first_sent)
     firsts = (first_own, lax.ppermute(first_sent, "frames", swap))
-    rest_sent = made(False, False, (proj_other, first_own))
-    rest_sent = lax.optimization_barrier((rest_sent, firsts[1]))[0]
+    rest_sent = made(False, False, first_own)
+    rest_sent = lax.optimization_barrier((rest_sent, firsts[1], proj_other))[0]
     rest_other = lax.ppermute(rest_sent, "frames", swap)
     scales = weights(proj, proj_other, frame_rows, vectors)
 
+    last, kept = None, []
+
     def make_first(p):
         nonlocal last
-        last = term(where_, scales, firsts, (), None, 0, line, p, pieces, vectors, width)
+        last = term(where_, scales, firsts, (), None, None, line, p, spans, vectors, width)
         return last
-
-    def make(received, block, starts, p):
-        return term(
-            where_, scales, rests(), received, block, starts, line, p, pieces, vectors, width
-        )
-
-    last, kept = None, []
 
     def rests():
         if not kept:
             kept.append(made(True, False, last))
         return kept[0], rest_other
 
-    right, left = along_line(line, pieces, make_first, make)
-    carriers = (right[0], left[0])
+    def make(received, block, starts, p, after=None):
+        late = scales
+        if after is not None:
+            late = lax.optimization_barrier((scales, after))[0]
+        return term(where_, late, rests(), received, block, starts, line, p, spans, vectors, width)
+
+    if line == 4:
+        arrived = along_four(len(spans), make_first, make)
+    else:
+        arrived = along_line(line, len(spans), make_first, make)
     images, gram = [], None
-    for p in range(pieces):
+    for p in range(len(spans)):
         image, gram, *more = image_piece(
-            where_, scales, firsts, rests(), carriers, (right[p], left[p]),
-            mean_structure if p == 0 else gram, line, p, pieces, vectors, width, frame_count,
+            where_, scales, firsts, rests(), arrived[0], arrived[p],
+            mean_structure if p == 0 else gram, line, p, spans, vectors, width, frame_count,
         )
         images.append(image)
         if p == 0:

time: 84.6 us -> 81.1 us (0.959)
  starting transfers between devices: 40.1 us -> 35.4 us
  waiting for transfers between devices: 23.2 us -> 25.3 us
    ppermute x10, starting transfers between devices: 26.8 us -> 22.2 us  [the longest x2 8.83 us: along_four(): ends.append(lax.ppermute(out, 'frames', inward))]
    ppermute x10, waiting for transfers between devices: 12.8 us -> 14.8 us  [the longest x2 6.67 us: along_four(): end = lax.ppermute(out, 'frames', inward + outward)]
    ppermute x10, waiting for transfers between devices: 9.39 us -> 10.3 us  [exchanged(): lax.ppermute(value, axis, [(i, i ^ mask) for i in range(size)])]
    ppermute x1, waiting for transfers between devices: 1.04 us -> 0.11 us  [per_device(): proj_other = lax.ppermute(proj, 'frames', swap)]
  transfers between devices with their start and end apart: 23 -> 23, of which waited for: 15 -> 17; matrix products, arithmetic and copies ran while one was open for 0% -> 0% of each run, Pallas kernels for 10% -> 10%
where the time goes in v2:
time: 81.1 us; the launch traced here: 80.9 us
  starting transfers between devices  35.4 us (44%)
  waiting for transfers between devices  25.3 us (31%)
  Pallas kernels  19.3 us (24%)
  between operations  0.84 us (1%)
    ppermute x10, starting transfers between devices, exchanged(): lax.ppermute(value, axis, [(i, i ^ mask) for i in range(size)])  12.5 us
    ppermute x10, waiting for transfers between devices, exchanged(): lax.ppermute(value, axis, [(i, i ^ mask) for i in range(size)])  10.3 us
    ppermute x2, starting transfers between devices, along_four(): ends.append(lax.ppermute(out, 'frames', inward))  8.83 us
    ppermute x2, waiting for transfers between devices, along_four(): end = lax.ppermute(out, 'frames', inward + outward)  6.67 us
    pallas_call x1, Pallas kernels, moments(): pl.pallas_call(moments_kernel, in_specs=[pl.BlockSpec(memory_space=pltpu....  6.52 us
    ppermute x2, starting transfers between devices, along_four(): end = lax.ppermute(out, 'frames', inward + outward)  5.8 us
    ppermute x2, waiting for transfers between devices, along_four(): first = [lax.ppermute(make_first(p), 'frames', inward) for p in each]  5.46 us
    ppermute x2, starting transfers between devices, along_four(): first = [lax.ppermute(make_first(p), 'frames', inward) for p in each]  4.82 us
  transfers between devices with their start and end apart: 23, of which 17 were waited for; matrix products, arithmetic and copies ran while one was open for 0% of the time, Pallas kernels for 10%

profile of v2, /device:TPU:0, one launch (start us, length us, event | category | flops | bytes accessed | tf_op | source)
XLA Modules:
  0.0 80.9 jit_solution(9660136981748645242)
XLA Ops:
  0.6 6.5 %moments.1 = (f32[80,128]{1,0:T(8,128)S(1)}, f32[72,24576]{1,0:T(8,128)S(1)}) custom-call(s32[1]{0:T(128)} %bitcast._.idx, f32[72,24576]{1,0:T(8,128)} %bitcast.14, f32[3,24576]{1,0:T(4,128)} %refs_9_.1, f32[1,24576]{1,0:T(1,128)} %bitcast.16, bf16[96,24576]{1,0:T(8,128)(2,1)} %bitcast.15), custom_call_target="tpu_custom_call" | custom-call | tf_op jit(solution)/shard_map/moments/pallas_call | solution.py:108
  7.2 4.0 %collective-permute-start = (f32[80,128]{1,0:T(8,128)S(1)}, f32[80,128]{1,0:T(8,128)S(1)}, u32[]{:S(2)}, u32[]{:S(2)}) collective-permute-start(f32[80,128]{1,0:T(8,128)S(1)} %get-tuple-element.40.refs_0_), channel_id=1, source_target_pairs={{0,24},{8,16},{16,8},{24,0},{1,25},{9,17},{17,9},{25,1},{2,26},{10... | collective-permute-start | bytes 122888 | tf_op jit(solution)/shard_map/ppermute | solution.py:481
  11.1 0.5 collective-permute-start.1
  11.6 0.1 collective-permute-start.2
  11.8 1.3 %collective-permute-done.refs_1_ = f32[80,128]{1,0:T(8,128)S(1)} collective-permute-done((f32[80,128]{1,0:T(8,128)S(1)}, f32[80,128]{1,0:T(8,128)S(1)}, u32[]{:S(2)}, u32[]{:S(2)}) %collective-permute-start) | collective-permute-done | bytes 40992 | tf_op jit(solution)/shard_map/ppermute | solution.py:481
  13.1 2.0 %collective-permute-done.1.refs_2_ = f32[80,128]{1,0:T(8,128)S(1)} collective-permute-done((f32[80,128]{1,0:T(8,128)S(1)}, f32[80,128]{1,0:T(8,128)S(1)}, u32[]{:S(2)}, u32[]{:S(2)}) %collective-permute-start.1) | collective-permute-done | bytes 40992 | tf_op jit(solution)/shard_map/ppermute | solution.py:481
  15.1 0.5 collective-permute-done.2.refs_3_
  15.6 0.6 rotate.1
  16.2 0.3 displace.4
  16.5 0.1 collective-permute-start.4
  16.6 0.5 collective-permute-start.3
  17.1 0.3 displace.5.refs_3_
  17.3 0.9 %displace.7 = bf16[72,9216]{1,0:T(8,128)(2,1)S(1)} custom-call(s32[1]{0:T(128)} %bitcast._.idx, f32[72,24576]{1,0:T(8,128)S(1)} %get-tuple-element.45.x_ref, f32[3,24576]{1,0:T(4,128)S(1)} %copy-done, f32[288,128]{1,0:T(8,128)S(1)} %get-tuple-element.49.coef_ref), custom_call_target="tpu_custom_call" | custom-call | tf_op jit(solution)/shard_map/displace/pallas_call | solution.py:233
  18.3 0.1 collective-permute-done.3.other_ref
  18.4 0.0 collective-permute-done.4.refs_4_
  18.4 0.1 collective-permute-start.5
  18.5 0.2 weights.1
  18.7 0.4 term.11
  19.1 3.5 %collective-permute-start.6 = (bf16[96,1664]{1,0:T(8,128)(2,1)S(1)}, bf16[96,1664]{1,0:T(8,128)(2,1)S(1)}, u32[]{:S(2)}, u32[]{:S(2)}) collective-permute-start(bf16[96,1664]{1,0:T(8,128)(2,1)S(1)} %term.11), channel_id=1, source_target_pairs={{0,2},{1,3},{6,4},{7,5},{8,10},{9,11},{14,12},{15,13},{16,18},{17,... | collective-permute-start | bytes 958472 | tf_op jit(solution)/shard_map/ppermute | solution.py:587
  22.6 0.3 term.10
  22.9 1.3 %collective-permute-start.11 = (bf16[96,1536]{1,0:T(8,128)(2,1)S(1)}, bf16[96,1536]{1,0:T(8,128)(2,1)S(1)}, u32[]{:S(2)}, u32[]{:S(2)}) collective-permute-start(bf16[96,1536]{1,0:T(8,128)(2,1)S(1)} %term.10), channel_id=1, source_target_pairs={{0,2},{1,3},{6,4},{7,5},{8,10},{9,11},{14,12},{15,13},{16,18},{17,... | collective-permute-start | bytes 884744 | tf_op jit(solution)/shard_map/ppermute | solution.py:587
  24.2 0.9 %displace.6.refs_3_.refs_5_ = bf16[72,9216]{1,0:T(8,128)(2,1)S(1)} custom-call(s32[1]{0:T(128)} %bitcast._.idx, f32[72,24576]{1,0:T(8,128)S(1)} %get-tuple-element.45.x_ref, f32[3,24576]{1,0:T(4,128)S(1)} %copy-done, f32[288,128]{1,0:T(8,128)S(1)} %get-tuple-element.49.coef_ref), custom_call_target="tpu_custom_call" | custom-call | tf_op jit(solution)/shard_map/displace/pallas_call | solution.py:233
  25.2 5.3 %collective-permute-done.6.refs_5_ = bf16[96,1664]{1,0:T(8,128)(2,1)S(1)} collective-permute-done((bf16[96,1664]{1,0:T(8,128)(2,1)S(1)}, bf16[96,1664]{1,0:T(8,128)(2,1)S(1)}, u32[]{:S(2)}, u32[]{:S(2)}) %collective-permute-start.6) | collective-permute-done | bytes 319520 | tf_op jit(solution)/shard_map/ppermute | solution.py:587
  30.5 0.0 collective-permute-done.5.refs_4_.refs_6_
  30.5 0.4 term.12
  30.9 4.4 %collective-permute-start.7 = (bf16[96,1664]{1,0:T(8,128)(2,1)S(1)}, bf16[96,1664]{1,0:T(8,128)(2,1)S(1)}, u32[]{:S(2)}, u32[]{:S(2)}) collective-permute-start(bf16[96,1664]{1,0:T(8,128)(2,1)S(1)} %term.12), channel_id=1, source_target_pairs={{0,2},{1,3},{6,4},{7,5},{8,10},{9,11},{14,12},{15,13},{16,18},{17,... | collective-permute-start | bytes 958472 | tf_op jit(solution)/shard_map/ppermute | solution.py:591
  35.3 0.6 term.13
  35.9 0.7 collective-permute-start.8
  36.6 0.2 collective-permute-done.11.refs_6_
  36.8 0.3 term.16
  37.1 4.4 %collective-permute-start.12 = (bf16[96,1536]{1,0:T(8,128)(2,1)S(1)}, bf16[96,1536]{1,0:T(8,128)(2,1)S(1)}, u32[]{:S(2)}, u32[]{:S(2)}) collective-permute-start(bf16[96,1536]{1,0:T(8,128)(2,1)S(1)} %term.16), channel_id=1, source_target_pairs={{0,2},{1,3},{6,4},{7,5},{8,10},{9,11},{14,12},{15,13},{16,18},{17,... | collective-permute-start | bytes 884744 | tf_op jit(solution)/shard_map/ppermute | solution.py:591
  41.5 0.4 term.17
  41.9 0.7 collective-permute-start.13
  42.6 1.0 %collective-permute-done.7.refs_5_ = bf16[96,1664]{1,0:T(8,128)(2,1)S(1)} collective-permute-done((bf16[96,1664]{1,0:T(8,128)(2,1)S(1)}, bf16[96,1664]{1,0:T(8,128)(2,1)S(1)}, u32[]{:S(2)}, u32[]{:S(2)}) %collective-permute-start.7) | collective-permute-done | bytes 319520 | tf_op jit(solution)/shard_map/ppermute | solution.py:591
  43.6 0.0 collective-permute-done.8.refs_5_
  43.6 0.6 term.14
  44.2 2.8 %collective-permute-start.9 = (bf16[96,1664]{1,0:T(8,128)(2,1)S(1)}, bf16[96,1664]{1,0:T(8,128)(2,1)S(1)}, u32[]{:S(2)}, u32[]{:S(2)}) collective-permute-start(bf16[96,1664]{1,0:T(8,128)(2,1)S(1)} %term.14), channel_id=1, source_target_pairs={{0,2},{1,3},{6,4},{7,5},{4,6},{5,7},{2,0},{3,1},{8,10},{9,11},{14,... | collective-permute-start | bytes 958472 | tf_op jit(solution)/shard_map/ppermute | solution.py:597
  47.0 0.6 term.15
  47.6 0.7 collective-permute-start.10
  48.3 1.7 %collective-permute-done.12.refs_6_ = bf16[96,1536]{1,0:T(8,128)(2,1)S(1)} collective-permute-done((bf16[96,1536]{1,0:T(8,128)(2,1)S(1)}, bf16[96,1536]{1,0:T(8,128)(2,1)S(1)}, u32[]{:S(2)}, u32[]{:S(2)}) %collective-permute-start.12) | collective-permute-done | bytes 294944 | tf_op jit(solution)/shard_map/ppermute | solution.py:591
  49.9 0.0 collective-permute-done.13.refs_6_
  49.9 0.4 term.18
  50.4 3.0 %collective-permute-start.14 = (bf16[96,1536]{1,0:T(8,128)(2,1)S(1)}, bf16[96,1536]{1,0:T(8,128)(2,1)S(1)}, u32[]{:S(2)}, u32[]{:S(2)}) collective-permute-start(bf16[96,1536]{1,0:T(8,128)(2,1)S(1)} %term.18), channel_id=1, source_target_pairs={{0,2},{1,3},{6,4},{7,5},{4,6},{5,7},{2,0},{3,1},{8,10},{9,11},{14,... | collective-permute-start | bytes 884744 | tf_op jit(solution)/shard_map/ppermute | solution.py:597
  53.4 0.4 term.19
  53.9 0.7 collective-permute-start.15
  54.6 2.2 %collective-permute-done.9.refs_7_ = bf16[96,1664]{1,0:T(8,128)(2,1)S(1)} collective-permute-done((bf16[96,1664]{1,0:T(8,128)(2,1)S(1)}, bf16[96,1664]{1,0:T(8,128)(2,1)S(1)}, u32[]{:S(2)}, u32[]{:S(2)}) %collective-permute-start.9) | collective-permute-done | bytes 319520 | tf_op jit(solution)/shard_map/ppermute | solution.py:597
  56.8 0.0 collective-permute-done.10.refs_8_
  56.8 1.3 %image_piece.2 = (f32[96,1536]{1,0:T(8,128)S(1)}, f32[8,128]{1,0:T(8,128)S(1)}, f32[3,3072]{1,0:T(4,128)}) custom-call(s32[1]{0:T(128)} %bitcast._.idx, bf16[96,72]{1,0:T(8,128)(2,1)S(1)} %get-tuple-element.68.refs_0_, bf16[96,72]{1,0:T(8,128)(2,1)S(1)} %get-tuple-element.69.refs_1_, f32[8,128]{1,0:T(8,128)S(1)} %get-tuple-element.70.refs_2_, ...), custom_call_target="tpu_custom_call" | custom-call | flops 2000000000 | bytes 1 | tf_op jit(solution)/shard_map/image_piece/pallas_call | solution.py:444
  58.1 4.5 %collective-permute-done.14.refs_10_ = bf16[96,1536]{1,0:T(8,128)(2,1)S(1)} collective-permute-done((bf16[96,1536]{1,0:T(8,128)(2,1)S(1)}, bf16[96,1536]{1,0:T(8,128)(2,1)S(1)}, u32[]{:S(2)}, u32[]{:S(2)}) %collective-permute-start.14) | collective-permute-done | bytes 294944 | tf_op jit(solution)/shard_map/ppermute | solution.py:597
  62.6 1.2 %image_piece.3 = (f32[96,1536]{1,0:T(8,128)S(1)}, f32[8,128]{1,0:T(8,128)S(1)}) custom-call(s32[1]{0:T(128)} %bitcast._.idx, bf16[96,72]{1,0:T(8,128)(2,1)S(1)} %get-tuple-element.68.refs_0_, bf16[96,72]{1,0:T(8,128)(2,1)S(1)} %get-tuple-element.69.refs_1_, f32[8,128]{1,0:T(8,128)S(1)} %get-tuple-element.70.refs_2_, bf16[72,3072]{1,0:T(8,128)(2,1)S(1)} %displace.5.refs_3_, ...), custom_call_target="tpu_custom_call" | custom-call | flops 2000000000 | bytes 1 | tf_op jit(solution)/shard_map/image_piece/pallas_call | solution.py:444
  63.7 1.5 %collective-permute-start.16 = (f32[8,128]{1,0:T(8,128)S(1)}, f32[8,128]{1,0:T(8,128)S(1)}, u32[]{:S(2)}, u32[]{:S(2)}) collective-permute-start(f32[8,128]{1,0:T(8,128)S(1)} %get-tuple-element.71.refs_0_), channel_id=1, source_target_pairs={{0,24},{8,16},{16,8},{24,0},{1,25},{9,17},{17,9},{25,1},{2,26},{10... | collective-permute-start | bytes 12296 | tf_op jit(solution)/shard_map/ppermute | solution.py:481
  65.3 0.5 collective-permute-start.17
  65.8 1.5 %collective-permute-start.18 = (f32[8,128]{1,0:T(8,128)S(1)}, f32[8,128]{1,0:T(8,128)S(1)}, u32[]{:S(2)}, u32[]{:S(2)}) collective-permute-start(f32[8,128]{1,0:T(8,128)S(1)} %get-tuple-element.71.refs_0_), channel_id=1, source_target_pairs={{0,8},{8,0},{16,24},{24,16},{1,9},{9,1},{17,25},{25,17},{2,10},{10... | collective-permute-start | bytes 12296 | tf_op jit(solution)/shard_map/ppermute | solution.py:481
  67.3 1.0 %collective-permute-done.16.refs_1_ = f32[8,128]{1,0:T(8,128)S(1)} collective-permute-done((f32[8,128]{1,0:T(8,128)S(1)}, f32[8,128]{1,0:T(8,128)S(1)}, u32[]{:S(2)}, u32[]{:S(2)}) %collective-permute-start.16) | collective-permute-done | bytes 4128 | tf_op jit(solution)/shard_map/ppermute | solution.py:481
  68.3 0.6 collective-permute-done.17.refs_2_
  68.9 0.5 collective-permute-done.18.refs_3_
  69.4 1.2 %collective-permute-done.19.refs_1_ = f32[8,128]{1,0:T(8,128)S(1)} collective-permute-done((f32[8,128]{1,0:T(8,128)S(1)}, f32[8,128]{1,0:T(8,128)S(1)}, u32[]{:S(2)}, u32[]{:S(2)}) %collective-permute-start.19) | collective-permute-done | bytes 4128 | tf_op jit(solution)/shard_map/ppermute | solution.py:481
  70.6 2.5 %collective-permute-start.20 = (f32[8,128]{1,0:T(8,128)S(1)}, f32[8,128]{1,0:T(8,128)S(1)}, u32[]{:S(2)}, u32[]{:S(2)}) collective-permute-start(f32[8,128]{1,0:T(8,128)S(1)} %fold.3.refs_0_), channel_id=1, source_target_pairs={{0,6},{1,7},{2,4},{3,5},{4,2},{5,3},{6,0},{7,1},{8,14},{9,15},{10,... | collective-permute-start | bytes 12296 | tf_op jit(solution)/shard_map/ppermute | solution.py:481
  73.0 1.5 %collective-permute-start.21 = (f32[8,128]{1,0:T(8,128)S(1)}, f32[8,128]{1,0:T(8,128)S(1)}, u32[]{:S(2)}, u32[]{:S(2)}) collective-permute-start(f32[8,128]{1,0:T(8,128)S(1)} %fold.3.refs_0_), channel_id=1, source_target_pairs={{0,4},{1,5},{2,6},{3,7},{4,0},{5,1},{6,2},{7,3},{8,12},{9,13},{10,... | collective-permute-start | bytes 12296 | tf_op jit(solution)/shard_map/ppermute | solution.py:481
  74.5 0.4 collective-permute-start.22
  74.9 1.0 %collective-permute-done.20.refs_1_ = f32[8,128]{1,0:T(8,128)S(1)} collective-permute-done((f32[8,128]{1,0:T(8,128)S(1)}, f32[8,128]{1,0:T(8,128)S(1)}, u32[]{:S(2)}, u32[]{:S(2)}) %collective-permute-start.20) | collective-permute-done | bytes 4128 | tf_op jit(solution)/shard_map/ppermute | solution.py:481
  76.0 1.6 %collective-permute-done.21.refs_2_ = f32[8,128]{1,0:T(8,128)S(1)} collective-permute-done((f32[8,128]{1,0:T(8,128)S(1)}, f32[8,128]{1,0:T(8,128)S(1)}, u32[]{:S(2)}, u32[]{:S(2)}) %collective-permute-start.21) | collective-permute-done | bytes 4128 | tf_op jit(solution)/shard_map/ppermute | solution.py:481
  77.6 0.6 collective-permute-done.22.refs_3_
  78.1 2.7 %basis.1 = (f32[96,3072]{1,0:T(8,128)}, f32[96,3072]{1,0:T(8,128)}) custom-call(f32[8,128]{1,0:T(8,128)S(1)} %fold.3.refs_0_, f32[8,128]{1,0:T(8,128)S(1)} %collective-permute-done.20.refs_1_, f32[8,128]{1,0:T(8,128)S(1)} %collective-permute-done.21.refs_2_, f32[8,128]{1,0:T(8,128)S(1)} %collective-permute-done.22.refs_3_, ...), custom_call_target="tpu_custom_call" | custom-call | tf_op jit(solution)/shard_map/basis/pallas_call | solution.py:549
  (6 shorter events, 0.0 us)
Async XLA Ops:
  0.6 15.6 %copy-start = (f32[3,24576]{1,0:T(4,128)S(1)}, f32[3,24576]{1,0:T(4,128)}, u32[]{:S(2)}) copy-start(f32[3,24576]{1,0:T(4,128)} %refs_9_.1) | copy-start | bytes 884740
  7.2 5.9 %collective-permute-start = (f32[80,128]{1,0:T(8,128)S(1)}, f32[80,128]{1,0:T(8,128)S(1)}, u32[]{:S(2)}, u32[]{:S(2)}) collective-permute-start(f32[80,128]{1,0:T(8,128)S(1)} %get-tuple-element.40.refs_0_), channel_id=1, source_target_pairs={{0,24},{8,16},{16,8},{24,0},{1,25},{9,17},{17,9},{25,1},{2,26},{10... | collective-permute-start | bytes 122888 | tf_op jit(solution)/shard_map/ppermute | solution.py:481
  11.1 4.0 %collective-permute-start.1 = (f32[80,128]{1,0:T(8,128)S(1)}, f32[80,128]{1,0:T(8,128)S(1)}, u32[]{:S(2)}, u32[]{:S(2)}) collective-permute-start(f32[80,128]{1,0:T(8,128)S(1)} %get-tuple-element.40.refs_0_), channel_id=1, source_target_pairs={{0,16},{8,24},{16,0},{24,8},{1,17},{9,25},{17,1},{25,9},{2,18},{10... | collective-permute-start | bytes 122888 | tf_op jit(solution)/shard_map/ppermute | solution.py:481
  11.6 4.0 %collective-permute-start.2 = (f32[80,128]{1,0:T(8,128)S(1)}, f32[80,128]{1,0:T(8,128)S(1)}, u32[]{:S(2)}, u32[]{:S(2)}) collective-permute-start(f32[80,128]{1,0:T(8,128)S(1)} %get-tuple-element.40.refs_0_), channel_id=1, source_target_pairs={{0,8},{8,0},{16,24},{24,16},{1,9},{9,1},{17,25},{25,17},{2,10},{10... | collective-permute-start | bytes 122888 | tf_op jit(solution)/shard_map/ppermute | solution.py:481
  16.5 1.9 %collective-permute-start.4 = (bf16[72,3072]{1,0:T(8,128)(2,1)S(1)}, bf16[72,3072]{1,0:T(8,128)(2,1)S(1)}, u32[]{:S(2)}, u32[]{:S(2)}) collective-permute-start(bf16[72,3072]{1,0:T(8,128)(2,1)S(1)} %displace.4), channel_id=1, source_target_pairs={{0,1},{1,0},{2,3},{3,2},{4,5},{5,4},{6,7},{7,6},{8,9},{9,8},{10,11... | collective-permute-start | bytes 1327112 | tf_op jit(solution)/shard_map/ppermute | solution.py:656
  16.6 1.8 %collective-permute-start.3 = (f32[24,128]{1,0:T(8,128)S(1)}, f32[24,128]{1,0:T(8,128)S(1)}, u32[]{:S(2)}, u32[]{:S(2)}) collective-permute-start(f32[24,128]{1,0:T(8,128)S(1)} %get-tuple-element.41.own_ref), channel_id=1, source_target_pairs={{0,1},{1,0},{2,3},{3,2},{4,5},{5,4},{6,7},{7,6},{8,9},{9,8},{10,11... | collective-permute-start | bytes 36872 | tf_op jit(solution)/shard_map/ppermute | solution.py:648
  18.4 12.1 %collective-permute-start.5 = (bf16[72,9216]{1,0:T(8,128)(2,1)S(1)}, bf16[72,9216]{1,0:T(8,128)(2,1)S(1)}, u32[]{:S(2)}, u32[]{:S(2)}) collective-permute-start(bf16[72,9216]{1,0:T(8,128)(2,1)S(1)} %displace.7), channel_id=1, source_target_pairs={{0,1},{1,0},{2,3},{3,2},{4,5},{5,4},{6,7},{7,6},{8,9},{9,8},{10,11... | collective-permute-start | bytes 3981320 | tf_op jit(solution)/shard_map/ppermute | solution.py:659
  19.1 11.4 %collective-permute-start.6 = (bf16[96,1664]{1,0:T(8,128)(2,1)S(1)}, bf16[96,1664]{1,0:T(8,128)(2,1)S(1)}, u32[]{:S(2)}, u32[]{:S(2)}) collective-permute-start(bf16[96,1664]{1,0:T(8,128)(2,1)S(1)} %term.11), channel_id=1, source_target_pairs={{0,2},{1,3},{6,4},{7,5},{8,10},{9,11},{14,12},{15,13},{16,18},{17,... | collective-permute-start | bytes 958472 | tf_op jit(solution)/shard_map/ppermute | solution.py:587
  22.9 13.9 %collective-permute-start.11 = (bf16[96,1536]{1,0:T(8,128)(2,1)S(1)}, bf16[96,1536]{1,0:T(8,128)(2,1)S(1)}, u32[]{:S(2)}, u32[]{:S(2)}) collective-permute-start(bf16[96,1536]{1,0:T(8,128)(2,1)S(1)} %term.10), channel_id=1, source_target_pairs={{0,2},{1,3},{6,4},{7,5},{8,10},{9,11},{14,12},{15,13},{16,18},{17,... | collective-permute-start | bytes 884744 | tf_op jit(solution)/shard_map/ppermute | solution.py:587
  30.9 12.8 %collective-permute-start.7 = (bf16[96,1664]{1,0:T(8,128)(2,1)S(1)}, bf16[96,1664]{1,0:T(8,128)(2,1)S(1)}, u32[]{:S(2)}, u32[]{:S(2)}) collective-permute-start(bf16[96,1664]{1,0:T(8,128)(2,1)S(1)} %term.12), channel_id=1, source_target_pairs={{0,2},{1,3},{6,4},{7,5},{8,10},{9,11},{14,12},{15,13},{16,18},{17,... | collective-permute-start | bytes 958472 | tf_op jit(solution)/shard_map/ppermute | solution.py:591
  35.9 7.7 %collective-permute-start.8 = (bf16[96,1664]{1,0:T(8,128)(2,1)S(1)}, bf16[96,1664]{1,0:T(8,128)(2,1)S(1)}, u32[]{:S(2)}, u32[]{:S(2)}) collective-permute-start(bf16[96,1664]{1,0:T(8,128)(2,1)S(1)} %term.13), channel_id=1, source_target_pairs={{2,4},{3,5},{4,2},{5,3},{10,12},{11,13},{12,10},{13,11},{18,20},{1... | collective-permute-start | bytes 958472 | tf_op jit(solution)/shard_map/ppermute | solution.py:593
  37.1 12.9 %collective-permute-start.12 = (bf16[96,1536]{1,0:T(8,128)(2,1)S(1)}, bf16[96,1536]{1,0:T(8,128)(2,1)S(1)}, u32[]{:S(2)}, u32[]{:S(2)}) collective-permute-start(bf16[96,1536]{1,0:T(8,128)(2,1)S(1)} %term.16), channel_id=1, source_target_pairs={{0,2},{1,3},{6,4},{7,5},{8,10},{9,11},{14,12},{15,13},{16,18},{17,... | collective-permute-start | bytes 884744 | tf_op jit(solution)/shard_map/ppermute | solution.py:591
  41.9 8.0 %collective-permute-start.13 = (bf16[96,1536]{1,0:T(8,128)(2,1)S(1)}, bf16[96,1536]{1,0:T(8,128)(2,1)S(1)}, u32[]{:S(2)}, u32[]{:S(2)}) collective-permute-start(bf16[96,1536]{1,0:T(8,128)(2,1)S(1)} %term.17), channel_id=1, source_target_pairs={{2,4},{3,5},{4,2},{5,3},{10,12},{11,13},{12,10},{13,11},{18,20},{1... | collective-permute-start | bytes 884744 | tf_op jit(solution)/shard_map/ppermute | solution.py:593
  44.2 12.6 %collective-permute-start.9 = (bf16[96,1664]{1,0:T(8,128)(2,1)S(1)}, bf16[96,1664]{1,0:T(8,128)(2,1)S(1)}, u32[]{:S(2)}, u32[]{:S(2)}) collective-permute-start(bf16[96,1664]{1,0:T(8,128)(2,1)S(1)} %term.14), channel_id=1, source_target_pairs={{0,2},{1,3},{6,4},{7,5},{4,6},{5,7},{2,0},{3,1},{8,10},{9,11},{14,... | collective-permute-start | bytes 958472 | tf_op jit(solution)/shard_map/ppermute | solution.py:597
  47.6 9.2 %collective-permute-start.10 = (bf16[96,1664]{1,0:T(8,128)(2,1)S(1)}, bf16[96,1664]{1,0:T(8,128)(2,1)S(1)}, u32[]{:S(2)}, u32[]{:S(2)}) collective-permute-start(bf16[96,1664]{1,0:T(8,128)(2,1)S(1)} %term.15), channel_id=1, source_target_pairs={{2,4},{3,5},{4,2},{5,3},{10,12},{11,13},{12,10},{13,11},{18,20},{1... | collective-permute-start | bytes 958472 | tf_op jit(solution)/shard_map/ppermute | solution.py:599
  50.4 12.2 %collective-permute-start.14 = (bf16[96,1536]{1,0:T(8,128)(2,1)S(1)}, bf16[96,1536]{1,0:T(8,128)(2,1)S(1)}, u32[]{:S(2)}, u32[]{:S(2)}) collective-permute-start(bf16[96,1536]{1,0:T(8,128)(2,1)S(1)} %term.18), channel_id=1, source_target_pairs={{0,2},{1,3},{6,4},{7,5},{4,6},{5,7},{2,0},{3,1},{8,10},{9,11},{14,... | collective-permute-start | bytes 884744 | tf_op jit(solution)/shard_map/ppermute | solution.py:597
  53.9 8.7 %collective-permute-start.15 = (bf16[96,1536]{1,0:T(8,128)(2,1)S(1)}, bf16[96,1536]{1,0:T(8,128)(2,1)S(1)}, u32[]{:S(2)}, u32[]{:S(2)}) collective-permute-start(bf16[96,1536]{1,0:T(8,128)(2,1)S(1)} %term.19), channel_id=1, source_target_pairs={{2,4},{3,5},{4,2},{5,3},{10,12},{11,13},{12,10},{13,11},{18,20},{1... | collective-permute-start | bytes 884744 | tf_op jit(solution)/shard_map/ppermute | solution.py:599
  63.7 4.6 %collective-permute-start.16 = (f32[8,128]{1,0:T(8,128)S(1)}, f32[8,128]{1,0:T(8,128)S(1)}, u32[]{:S(2)}, u32[]{:S(2)}) collective-permute-start(f32[8,128]{1,0:T(8,128)S(1)} %get-tuple-element.71.refs_0_), channel_id=1, source_target_pairs={{0,24},{8,16},{16,8},{24,0},{1,25},{9,17},{17,9},{25,1},{2,26},{10... | collective-permute-start | bytes 12296 | tf_op jit(solution)/shard_map/ppermute | solution.py:481
  65.3 3.6 %collective-permute-start.17 = (f32[8,128]{1,0:T(8,128)S(1)}, f32[8,128]{1,0:T(8,128)S(1)}, u32[]{:S(2)}, u32[]{:S(2)}) collective-permute-start(f32[8,128]{1,0:T(8,128)S(1)} %get-tuple-element.71.refs_0_), channel_id=1, source_target_pairs={{0,16},{8,24},{16,0},{24,8},{1,17},{9,25},{17,1},{25,9},{2,18},{10... | collective-permute-start | bytes 12296 | tf_op jit(solution)/shard_map/ppermute | solution.py:481
  65.8 3.6 %collective-permute-start.18 = (f32[8,128]{1,0:T(8,128)S(1)}, f32[8,128]{1,0:T(8,128)S(1)}, u32[]{:S(2)}, u32[]{:S(2)}) collective-permute-start(f32[8,128]{1,0:T(8,128)S(1)} %get-tuple-element.71.refs_0_), channel_id=1, source_target_pairs={{0,8},{8,0},{16,24},{24,16},{1,9},{9,1},{17,25},{25,17},{2,10},{10... | collective-permute-start | bytes 12296 | tf_op jit(solution)/shard_map/ppermute | solution.py:481
  69.4 1.2 %collective-permute-start.19 = (f32[8,128]{1,0:T(8,128)S(1)}, f32[8,128]{1,0:T(8,128)S(1)}, u32[]{:S(2)}, u32[]{:S(2)}) collective-permute-start(f32[8,128]{1,0:T(8,128)S(1)} %fold.2.refs_0_), channel_id=1, source_target_pairs={{0,1},{1,0},{2,3},{3,2},{4,5},{5,4},{6,7},{7,6},{8,9},{9,8},{10,11... | collective-permute-start | bytes 12296 | tf_op jit(solution)/shard_map/ppermute | solution.py:481
  70.6 5.4 %collective-permute-start.20 = (f32[8,128]{1,0:T(8,128)S(1)}, f32[8,128]{1,0:T(8,128)S(1)}, u32[]{:S(2)}, u32[]{:S(2)}) collective-permute-start(f32[8,128]{1,0:T(8,128)S(1)} %fold.3.refs_0_), channel_id=1, source_target_pairs={{0,6},{1,7},{2,4},{3,5},{4,2},{5,3},{6,0},{7,1},{8,14},{9,15},{10,... | collective-permute-start | bytes 12296 | tf_op jit(solution)/shard_map/ppermute | solution.py:481
  73.0 4.5 %collective-permute-start.21 = (f32[8,128]{1,0:T(8,128)S(1)}, f32[8,128]{1,0:T(8,128)S(1)}, u32[]{:S(2)}, u32[]{:S(2)}) collective-permute-start(f32[8,128]{1,0:T(8,128)S(1)} %fold.3.refs_0_), channel_id=1, source_target_pairs={{0,4},{1,5},{2,6},{3,7},{4,0},{5,1},{6,2},{7,3},{8,12},{9,13},{10,... | collective-permute-start | bytes 12296 | tf_op jit(solution)/shard_map/ppermute | solution.py:481
  74.5 3.6 %collective-permute-start.22 = (f32[8,128]{1,0:T(8,128)S(1)}, f32[8,128]{1,0:T(8,128)S(1)}, u32[]{:S(2)}, u32[]{:S(2)}) collective-permute-start(f32[8,128]{1,0:T(8,128)S(1)} %fold.3.refs_0_), channel_id=1, source_target_pairs={{0,2},{1,3},{2,0},{3,1},{4,6},{5,7},{6,4},{7,5},{8,10},{9,11},{10,... | collective-permute-start | bytes 12296 | tf_op jit(solution)/shard_map/ppermute | solution.py:481

commit v3 on v2

--- a/solution.py
+++ b/solution.py
@@ -78,6 +78,11 @@
     row = lax.broadcasted_iota(jnp.int32, (8, TILE), 0)
     ones = jnp.where(row == 3, 1.0, 0.0)
     total = jnp.zeros(out_ref.shape, F32)
+
+    def product(t):
+        sums = dot_nt(lhs_ref[t % 2], rhs_ref[:, t * chunk : (t + 1) * chunk])
+        return sums[0:n] + sums[n : 2 * n]
+
     for t in range(chunks):
         for copy in copies[t + 1]:
             copy.wait()
@@ -94,8 +99,9 @@
             pieces = [v.astype(F32) for v in split3(left * w_ref[:, lanes])]
             aux = jnp.concatenate(pieces + [jnp.zeros(left.shape, F32)], axis=0)
             rhs_ref[vectors:, lanes] = aux.astype(BF16)
-        sums = dot_nt(lhs_ref[t % 2], rhs_ref[:, t * chunk : (t + 1) * chunk])
-        total = total + (sums[0:n] + sums[n : 2 * n])
+        if t > 0:
+            total = total + product(t - 1)
+    total = total + product(chunks - 1)
     out_ref[...] = total
 
 
@@ -351,59 +357,13 @@
     )(where_, *args)
 
 
-def image_kernel(carrier_count, line, p, spans, vectors, width, frame_count, idx, *refs):
-    refs = list(refs)
-    c_ref, e_ref, mean_ref = [refs.pop(0) for _ in range(3)]
-    firsts, rests = [[refs.pop(0) for _ in range(2)] for _ in range(2)]
-    carriers = [refs.pop(0) for _ in range(carrier_count)]
-    other_ref = refs.pop(0)
-    block_ref = refs.pop()
-    new_mean_ref = refs.pop() if p == 0 else None
-    gram_ref, image_ref = refs.pop(), refs.pop()
-    received = carriers if p == 0 else refs
-    chip = idx[0] // 2
-    made_first = first_block(chip, line)
-    at = pl.multiple_of(jnp.clip(chip - (chip > made_first).astype(jnp.int32), 0, line - 2) * width, LANES)
-    for n in range(2):
-
-        @pl.when(chip == made_first)
-        def _(n=n):
-            block_ref[n] = firsts[n][...]
-
-        @pl.when(chip != made_first)
-        def _(n=n):
-            block_ref[n] = rests[n][:, pl.ds(at, width)]
-
-    offset, piece_width = spans[p]
-    lanes = slice(offset, offset + piece_width)
-    value = both(c_ref[...], e_ref[...], block_ref[0, :, lanes], block_ref[1, :, lanes])
-    for ref in received:
-        value = value + ref[:, 0:piece_width].astype(F32)
-
-    ones = ones_rows(block_ref.shape[1])
-    sums = both(ones, ones, block_ref[0], block_ref[1])
-    mean = mean_ref[0:1, :]
-    slabs = [ref[:, spans[0][1] :].astype(F32) for ref in carriers]
-    centers, totals = zip(*(read_slab(slab, width) for slab in slabs))
-    center = functools.reduce(jnp.add, totals, mean) / line
-    columns = [as_column(v - center, vectors) for v in (mean, *centers)]
-    tiles = width // LANES
+def inner_products(parts, vectors):
     gram = jnp.zeros((2 * vectors, LANES), F32)
-    for i in range(3):
-        rows = slice(i * vectors, (i + 1) * vectors)
-        moved = []
-        for tile in range(offset // LANES, (offset + piece_width) // LANES):
-            part = columns[0] * sums[i : i + 1, tile * LANES : (tile + 1) * LANES]
-            row = i * tiles + tile
-            for column, slab in zip(columns[1:], slabs):
-                part = part + column * slab[row : row + 1, :]
-            moved.append(part)
-        part = (value[rows] + jnp.concatenate(moved, axis=1)) / frame_count
-        image_ref[rows, :] = part
+    for part in parts:
         high = part.astype(BF16)
         low = (part - high.astype(F32)).astype(BF16)
         lhs = jnp.concatenate([high, low], axis=0)
-        rhs = jnp.concatenate([lhs, jnp.zeros((LANES - 2 * vectors, piece_width), BF16)], axis=0)
+        rhs = jnp.concatenate([lhs, jnp.zeros((LANES - 2 * vectors, part.shape[1]), BF16)], axis=0)
         gram = gram + dot_nt(lhs, rhs)
     gram = gram[0:vectors] + gram[vectors : 2 * vectors]
     gram = gram + pltpu.roll(gram, LANES - vectors, 1)
@@ -412,47 +372,115 @@
     packed = gram[0:8]
     for g in range(1, vectors // 8):
         packed = packed + pltpu.roll(gram[8 * g : 8 * g + 8], vectors * g, 1)
-    if p > 0:
-        packed = packed + other_ref[...]
-    gram_ref[...] = packed
-    if p == 0:
-        total = functools.reduce(jnp.add, slabs)
+    return packed
+
+
+def image_kernel(line, spans, vectors, width, frame_count, idx, *refs):
+    refs = list(refs)
+    c_ref, e_ref, mean_ref = [refs.pop(0) for _ in range(3)]
+    firsts, rests = [[refs.pop(0) for _ in range(2)] for _ in range(2)]
+    old_ref = refs.pop(0)
+    image_ref, gram_ref, new_mean_ref, next_ref, block_ref = refs[-5:]
+    received = refs[:-5]
+    chip = idx[0] // 2
+    made_first = first_block(chip, line)
+    at = jnp.clip(chip - (chip > made_first).astype(jnp.int32), 0, line - 2) * width
+    for n in range(2):
+
+        @pl.when(chip == made_first)
+        def _(n=n):
+            block_ref[n] = firsts[n][...]
+
+        @pl.when(chip != made_first)
+        def _(n=n):
+            block_ref[n] = rests[n][:, pl.ds(pl.multiple_of(at, LANES), width)]
+
+    ones = ones_rows(block_ref.shape[1])
+    sums = both(ones, ones, block_ref[0], block_ref[1])
+    mean = mean_ref[0:1, :]
+    slabs = [ref[:, spans[0][1] :].astype(F32) for ref in received]
+    centers, totals = zip(*(read_slab(slab, width) for slab in slabs))
+    center = functools.reduce(jnp.add, totals, mean) / line
+    columns = [as_column(v - center, vectors) for v in (mean, *centers)]
+    tiles = width // LANES
+
+    def own_part(offset, piece_width):
+        lanes = slice(offset, offset + piece_width)
+        value = both(c_ref[...], e_ref[...], block_ref[0, :, lanes], block_ref[1, :, lanes])
+        parts = []
         for i in range(3):
-            for tile in range(tiles):
-                start = (idx[0] * tiles + tile) * LANES
-                old = other_ref[i : i + 1, pl.ds(pl.multiple_of(start, LANES), LANES)]
+            moved = []
+            for tile in range(offset // LANES, (offset + piece_width) // LANES):
+                part = columns[0] * sums[i : i + 1, tile * LANES : (tile + 1) * LANES]
                 row = i * tiles + tile
-                here = slice(tile * LANES, (tile + 1) * LANES)
-                added = (total[row : row + 1, :] + sums[i : i + 1, here]) / frame_count
-                new_mean_ref[i : i + 1, here] = old + added
-
-
-def image_piece(
-    where_, scales, firsts, rests, carriers, received, other, line, p, spans, vectors, width,
-    frame_count,
-):
+                for column, slab in zip(columns[1:], slabs):
+                    part = part + column * slab[row : row + 1, :]
+                moved.append(part)
+            rows = slice(i * vectors, (i + 1) * vectors)
+            parts.append(value[rows] + jnp.concatenate(moved, axis=1))
+        return parts
+
+    piece_width = spans[0][1]
+    parts = own_part(*spans[0])
+    for i in range(3):
+        rows = slice(i * vectors, (i + 1) * vectors)
+        for ref in received:
+            parts[i] = parts[i] + ref[rows, 0:piece_width].astype(F32)
+        parts[i] = parts[i] / frame_count
+        image_ref[rows, :] = parts[i]
+    gram_ref[...] = inner_products(parts, vectors)
+    for i, part in enumerate(own_part(*spans[1])):
+        next_ref[i * vectors : (i + 1) * vectors, :] = part
+    total = functools.reduce(jnp.add, slabs)
+    for i in range(3):
+        for tile in range(tiles):
+            start = (idx[0] * tiles + tile) * LANES
+            old = old_ref[i : i + 1, pl.ds(pl.multiple_of(start, LANES), LANES)]
+            row = i * tiles + tile
+            here = slice(tile * LANES, (tile + 1) * LANES)
+            added = (total[row : row + 1, :] + sums[i : i + 1, here]) / frame_count
+            new_mean_ref[i : i + 1, here] = old + added
+
+
+def first_piece(where_, scales, firsts, rests, mean, received, line, spans, vectors, width, frame_count):
     rows = scales[0].shape[0]
-    args = [*scales, *firsts, *rests, *carriers, other]
-    out_shape = [
-        jax.ShapeDtypeStruct((rows, spans[p][1]), F32),
-        jax.ShapeDtypeStruct((8, LANES), F32),
-    ]
-    if p == 0:
-        out_shape.append(jax.ShapeDtypeStruct((3, width), F32))
-    else:
-        args += received
-    return pl.pallas_call(
-        functools.partial(
-            image_kernel, len(carriers), line, p, spans, vectors, width, frame_count
-        ),
+    args = (*scales, *firsts, *rests, mean, *received)
+    shapes = ((rows, spans[0][1]), (8, LANES), (3, width), (rows, spans[1][1]))
+    return pl.pallas_call(
+        functools.partial(image_kernel, line, spans, vectors, width, frame_count),
         in_specs=[pl.BlockSpec(memory_space=pltpu.SMEM)] + in_vmem(len(args)),
-        out_specs=in_vmem(len(out_shape)),
-        out_shape=out_shape,
+        out_specs=in_vmem(len(shapes)),
+        out_shape=[jax.ShapeDtypeStruct(shape, F32) for shape in shapes],
         scratch_shapes=[pltpu.VMEM((2, firsts[0].shape[0], width), BF16)],
         compiler_params=params(),
         cost_estimate=cost(2),
-        name="image_piece",
+        name="first_piece",
     )(where_, *args)
+
+
+def finish_kernel(vectors, frame_count, own_ref, before_ref, *refs):
+    received, (image_ref, gram_ref) = refs[:-2], refs[-2:]
+    parts = []
+    for i in range(3):
+        rows = slice(i * vectors, (i + 1) * vectors)
+        part = own_ref[rows, :]
+        for ref in received:
+            part = part + ref[rows, :].astype(F32)
+        parts.append(part / frame_count)
+        image_ref[rows, :] = parts[i]
+    gram_ref[...] = before_ref[...] + inner_products(parts, vectors)
+
+
+def second_piece(own, gram, received, vectors, frame_count):
+    args = (own, gram, *received)
+    return pl.pallas_call(
+        functools.partial(finish_kernel, vectors, frame_count),
+        in_specs=in_vmem(len(args)),
+        out_specs=in_vmem(2),
+        out_shape=[jax.ShapeDtypeStruct(v.shape, F32) for v in (own, gram)],
+        compiler_params=params(),
+        name="second_piece",
+    )(*args)
 
 
 def fold_kernel(*refs):
@@ -681,15 +709,13 @@
         arrived = along_four(len(spans), make_first, make)
     else:
         arrived = along_line(line, len(spans), make_first, make)
-    images, gram = [], None
-    for p in range(len(spans)):
-        image, gram, *more = image_piece(
-            where_, scales, firsts, rests(), arrived[0], arrived[p],
-            mean_structure if p == 0 else gram, line, p, spans, vectors, width, frame_count,
-        )
-        images.append(image)
-        if p == 0:
-            (new_mean,) = more
+    image, gram, new_mean, second = first_piece(
+        where_, scales, firsts, rests(), mean_structure, arrived[0], line, spans, vectors, width,
+        frame_count,
+    )
+    images = [image]
+    image, gram = second_piece(second, gram, arrived[1], vectors, frame_count)
+    images.append(image)
     gram = fold(summed(gram, "atoms", atom_devices, atom_bits))
     gram = fold(exchanged(gram, "frames", frame_devices, [0]))
     grams = summed(gram, "frames", frame_devices, range(1, frame_devices.bit_length() - 1))

time: 81.1 us -> 81.4 us (level)
    pallas_call x1, Pallas kernels: 6.52 us -> 7.56 us  [moments(): pl.pallas_call(moments_kernel, in_specs=[pl.BlockSpec(memory_space=pltpu....]
    pallas_call x2, Pallas kernels: 2.47 us -> 1.59 us  [the longest x1 1.14 us: first_piece(): pl.pallas_call(functools.partial(image_kernel, line, spans, vectors, widt...]
where the time goes in v3:
time: 81.4 us; the launch traced here: 81.2 us
  starting transfers between devices  35.4 us (43%)
  waiting for transfers between devices  25.5 us (31%)
  Pallas kernels  19.5 us (24%)
  between operations  0.84 us (1%)
    ppermute x10, starting transfers between devices, exchanged(): lax.ppermute(value, axis, [(i, i ^ mask) for i in range(size)])  12.5 us
    ppermute x10, waiting for transfers between devices, exchanged(): lax.ppermute(value, axis, [(i, i ^ mask) for i in range(size)])  10.4 us
    ppermute x2, starting transfers between devices, along_four(): ends.append(lax.ppermute(out, 'frames', inward))  8.81 us
    pallas_call x1, Pallas kernels, moments(): pl.pallas_call(moments_kernel, in_specs=[pl.BlockSpec(memory_space=pltpu....  7.56 us
    ppermute x2, waiting for transfers between devices, along_four(): end = lax.ppermute(out, 'frames', inward + outward)  6.87 us
    ppermute x2, starting transfers between devices, along_four(): end = lax.ppermute(out, 'frames', inward + outward)  5.8 us
    ppermute x2, waiting for transfers between devices, along_four(): first = [lax.ppermute(make_first(p), 'frames', inward) for p in each]  5.47 us
    ppermute x2, starting transfers between devices, along_four(): first = [lax.ppermute(make_first(p), 'frames', inward) for p in each]  4.83 us
  transfers between devices with their start and end apart: 23, of which 17 were waited for; matrix products, arithmetic and copies ran while one was open for 0% of the time, Pallas kernels for 10%

profile of v3, /device:TPU:0, one launch (start us, length us, event | category | flops | bytes accessed | tf_op | source)
XLA Modules:
  0.0 81.2 jit_solution(5775027713450165893)
XLA Ops:
  0.6 7.6 %moments.1 = (f32[80,128]{1,0:T(8,128)S(1)}, f32[72,24576]{1,0:T(8,128)S(1)}) custom-call(s32[1]{0:T(128)} %bitcast._.idx, f32[72,24576]{1,0:T(8,128)} %bitcast.14, f32[3,24576]{1,0:T(4,128)} %refs_7_.1, f32[1,24576]{1,0:T(1,128)} %bitcast.16, bf16[96,24576]{1,0:T(8,128)(2,1)} %bitcast.15), custom_call_target="tpu_custom_call" | custom-call | tf_op jit(solution)/shard_map/moments/pallas_call | solution.py:114
  8.2 4.0 %collective-permute-start = (f32[80,128]{1,0:T(8,128)S(1)}, f32[80,128]{1,0:T(8,128)S(1)}, u32[]{:S(2)}, u32[]{:S(2)}) collective-permute-start(f32[80,128]{1,0:T(8,128)S(1)} %get-tuple-element.41.refs_0_), channel_id=1, source_target_pairs={{0,24},{8,16},{16,8},{24,0},{1,25},{9,17},{17,9},{25,1},{2,26},{10... | collective-permute-start | bytes 122888 | tf_op jit(solution)/shard_map/ppermute | solution.py:509
  12.2 0.5 collective-permute-start.1
  12.7 0.1 collective-permute-start.2
  12.8 1.3 %collective-permute-done.refs_1_ = f32[80,128]{1,0:T(8,128)S(1)} collective-permute-done((f32[80,128]{1,0:T(8,128)S(1)}, f32[80,128]{1,0:T(8,128)S(1)}, u32[]{:S(2)}, u32[]{:S(2)}) %collective-permute-start) | collective-permute-done | bytes 40992 | tf_op jit(solution)/shard_map/ppermute | solution.py:509
  14.2 2.0 %collective-permute-done.1.refs_2_ = f32[80,128]{1,0:T(8,128)S(1)} collective-permute-done((f32[80,128]{1,0:T(8,128)S(1)}, f32[80,128]{1,0:T(8,128)S(1)}, u32[]{:S(2)}, u32[]{:S(2)}) %collective-permute-start.1) | collective-permute-done | bytes 40992 | tf_op jit(solution)/shard_map/ppermute | solution.py:509
  16.2 0.5 collective-permute-done.2.refs_3_
  16.7 0.6 rotate.1
  17.3 0.3 displace.4
  17.5 0.1 collective-permute-start.4
  17.6 0.5 collective-permute-start.3
  18.1 0.3 displace.5.refs_3_
  18.4 0.9 %displace.7 = bf16[72,9216]{1,0:T(8,128)(2,1)S(1)} custom-call(s32[1]{0:T(128)} %bitcast._.idx, f32[72,24576]{1,0:T(8,128)S(1)} %get-tuple-element.46.x_ref, f32[3,24576]{1,0:T(4,128)S(1)} %copy-done, f32[288,128]{1,0:T(8,128)S(1)} %get-tuple-element.50.coef_ref), custom_call_target="tpu_custom_call" | custom-call | tf_op jit(solution)/shard_map/displace/pallas_call | solution.py:239
  19.3 0.1 collective-permute-done.3.other_ref
  19.4 0.0 collective-permute-done.4.refs_4_
  19.4 0.1 collective-permute-start.5
  19.6 0.2 weights.1
  19.7 0.4 term.11
  20.1 3.5 %collective-permute-start.6 = (bf16[96,1664]{1,0:T(8,128)(2,1)S(1)}, bf16[96,1664]{1,0:T(8,128)(2,1)S(1)}, u32[]{:S(2)}, u32[]{:S(2)}) collective-permute-start(bf16[96,1664]{1,0:T(8,128)(2,1)S(1)} %term.11), channel_id=1, source_target_pairs={{0,2},{1,3},{6,4},{7,5},{8,10},{9,11},{14,12},{15,13},{16,18},{17,... | collective-permute-start | bytes 958472 | tf_op jit(solution)/shard_map/ppermute | solution.py:615
  23.7 0.3 term.10
  24.0 1.3 %collective-permute-start.11 = (bf16[96,1536]{1,0:T(8,128)(2,1)S(1)}, bf16[96,1536]{1,0:T(8,128)(2,1)S(1)}, u32[]{:S(2)}, u32[]{:S(2)}) collective-permute-start(bf16[96,1536]{1,0:T(8,128)(2,1)S(1)} %term.10), channel_id=1, source_target_pairs={{0,2},{1,3},{6,4},{7,5},{8,10},{9,11},{14,12},{15,13},{16,18},{17,... | collective-permute-start | bytes 884744 | tf_op jit(solution)/shard_map/ppermute | solution.py:615
  25.3 0.9 %displace.6.refs_3_.refs_5_ = bf16[72,9216]{1,0:T(8,128)(2,1)S(1)} custom-call(s32[1]{0:T(128)} %bitcast._.idx, f32[72,24576]{1,0:T(8,128)S(1)} %get-tuple-element.46.x_ref, f32[3,24576]{1,0:T(4,128)S(1)} %copy-done, f32[288,128]{1,0:T(8,128)S(1)} %get-tuple-element.50.coef_ref), custom_call_target="tpu_custom_call" | custom-call | tf_op jit(solution)/shard_map/displace/pallas_call | solution.py:239
  26.2 5.3 %collective-permute-done.6.refs_5_ = bf16[96,1664]{1,0:T(8,128)(2,1)S(1)} collective-permute-done((bf16[96,1664]{1,0:T(8,128)(2,1)S(1)}, bf16[96,1664]{1,0:T(8,128)(2,1)S(1)}, u32[]{:S(2)}, u32[]{:S(2)}) %collective-permute-start.6) | collective-permute-done | bytes 319520 | tf_op jit(solution)/shard_map/ppermute | solution.py:615
  31.5 0.0 collective-permute-done.5.refs_4_.refs_6_
  31.5 0.4 term.12
  31.9 4.4 %collective-permute-start.7 = (bf16[96,1664]{1,0:T(8,128)(2,1)S(1)}, bf16[96,1664]{1,0:T(8,128)(2,1)S(1)}, u32[]{:S(2)}, u32[]{:S(2)}) collective-permute-start(bf16[96,1664]{1,0:T(8,128)(2,1)S(1)} %term.12), channel_id=1, source_target_pairs={{0,2},{1,3},{6,4},{7,5},{8,10},{9,11},{14,12},{15,13},{16,18},{17,... | collective-permute-start | bytes 958472 | tf_op jit(solution)/shard_map/ppermute | solution.py:619
  36.3 0.6 term.13
  36.9 0.7 collective-permute-start.8
  37.6 0.2 collective-permute-done.11.refs_6_
  37.8 0.3 term.16
  38.1 4.4 %collective-permute-start.12 = (bf16[96,1536]{1,0:T(8,128)(2,1)S(1)}, bf16[96,1536]{1,0:T(8,128)(2,1)S(1)}, u32[]{:S(2)}, u32[]{:S(2)}) collective-permute-start(bf16[96,1536]{1,0:T(8,128)(2,1)S(1)} %term.16), channel_id=1, source_target_pairs={{0,2},{1,3},{6,4},{7,5},{8,10},{9,11},{14,12},{15,13},{16,18},{17,... | collective-permute-start | bytes 884744 | tf_op jit(solution)/shard_map/ppermute | solution.py:619
  42.5 0.4 term.17
  43.0 0.7 collective-permute-start.13
  43.7 1.0 %collective-permute-done.7.refs_5_ = bf16[96,1664]{1,0:T(8,128)(2,1)S(1)} collective-permute-done((bf16[96,1664]{1,0:T(8,128)(2,1)S(1)}, bf16[96,1664]{1,0:T(8,128)(2,1)S(1)}, u32[]{:S(2)}, u32[]{:S(2)}) %collective-permute-start.7) | collective-permute-done | bytes 319520 | tf_op jit(solution)/shard_map/ppermute | solution.py:619
  44.7 0.0 collective-permute-done.8.refs_5_
  44.7 0.6 term.14
  45.3 2.8 %collective-permute-start.9 = (bf16[96,1664]{1,0:T(8,128)(2,1)S(1)}, bf16[96,1664]{1,0:T(8,128)(2,1)S(1)}, u32[]{:S(2)}, u32[]{:S(2)}) collective-permute-start(bf16[96,1664]{1,0:T(8,128)(2,1)S(1)} %term.14), channel_id=1, source_target_pairs={{0,2},{1,3},{6,4},{7,5},{4,6},{5,7},{2,0},{3,1},{8,10},{9,11},{14,... | collective-permute-start | bytes 958472 | tf_op jit(solution)/shard_map/ppermute | solution.py:625
  48.0 0.6 term.15
  48.6 0.7 collective-permute-start.10
  49.3 1.7 %collective-permute-done.12.refs_6_ = bf16[96,1536]{1,0:T(8,128)(2,1)S(1)} collective-permute-done((bf16[96,1536]{1,0:T(8,128)(2,1)S(1)}, bf16[96,1536]{1,0:T(8,128)(2,1)S(1)}, u32[]{:S(2)}, u32[]{:S(2)}) %collective-permute-start.12) | collective-permute-done | bytes 294944 | tf_op jit(solution)/shard_map/ppermute | solution.py:619
  51.0 0.0 collective-permute-done.13.refs_6_
  51.0 0.4 term.18
  51.4 3.0 %collective-permute-start.14 = (bf16[96,1536]{1,0:T(8,128)(2,1)S(1)}, bf16[96,1536]{1,0:T(8,128)(2,1)S(1)}, u32[]{:S(2)}, u32[]{:S(2)}) collective-permute-start(bf16[96,1536]{1,0:T(8,128)(2,1)S(1)} %term.18), channel_id=1, source_target_pairs={{0,2},{1,3},{6,4},{7,5},{4,6},{5,7},{2,0},{3,1},{8,10},{9,11},{14,... | collective-permute-start | bytes 884744 | tf_op jit(solution)/shard_map/ppermute | solution.py:625
  54.5 0.4 term.19
  54.9 0.7 collective-permute-start.15
  55.6 2.2 %collective-permute-done.9.refs_8_ = bf16[96,1664]{1,0:T(8,128)(2,1)S(1)} collective-permute-done((bf16[96,1664]{1,0:T(8,128)(2,1)S(1)}, bf16[96,1664]{1,0:T(8,128)(2,1)S(1)}, u32[]{:S(2)}, u32[]{:S(2)}) %collective-permute-start.9) | collective-permute-done | bytes 319520 | tf_op jit(solution)/shard_map/ppermute | solution.py:625
  57.8 1.1 %first_piece.1 = (f32[96,1536]{1,0:T(8,128)S(1)}, f32[8,128]{1,0:T(8,128)S(1)}, f32[3,3072]{1,0:T(4,128)}, f32[96,1536]{1,0:T(8,128)S(1)}) custom-call(s32[1]{0:T(128)} %bitcast._.idx, bf16[96,72]{1,0:T(8,128)(2,1)S(1)} %get-tuple-element.70.refs_0_, bf16[96,72]{1,0:T(8,128)(2,1)S(1)} %get-tuple-element.71.refs_1_, f32[8,128]{1,0:T(8,128)S(1)} %get-tuple-element.72.refs_2_, ...), custom_call_target="tpu_custom_call" | custom-call | flops 2000000000 | bytes 1 | tf_op jit(solution)/shard_map/first_piece/pallas_call | solution.py:449
  59.0 4.6 %collective-permute-done.14.refs_0_ = bf16[96,1536]{1,0:T(8,128)(2,1)S(1)} collective-permute-done((bf16[96,1536]{1,0:T(8,128)(2,1)S(1)}, bf16[96,1536]{1,0:T(8,128)(2,1)S(1)}, u32[]{:S(2)}, u32[]{:S(2)}) %collective-permute-start.14) | collective-permute-done | bytes 294944 | tf_op jit(solution)/shard_map/ppermute | solution.py:625
  63.6 0.0 collective-permute-done.15.refs_1_
  63.6 0.4 second_piece.1
  64.1 1.5 %collective-permute-start.16 = (f32[8,128]{1,0:T(8,128)S(1)}, f32[8,128]{1,0:T(8,128)S(1)}, u32[]{:S(2)}, u32[]{:S(2)}) collective-permute-start(f32[8,128]{1,0:T(8,128)S(1)} %get-tuple-element.73.refs_0_), channel_id=1, source_target_pairs={{0,24},{8,16},{16,8},{24,0},{1,25},{9,17},{17,9},{25,1},{2,26},{10... | collective-permute-start | bytes 12296 | tf_op jit(solution)/shard_map/ppermute | solution.py:509
  65.6 0.5 collective-permute-start.17
  66.1 1.5 %collective-permute-start.18 = (f32[8,128]{1,0:T(8,128)S(1)}, f32[8,128]{1,0:T(8,128)S(1)}, u32[]{:S(2)}, u32[]{:S(2)}) collective-permute-start(f32[8,128]{1,0:T(8,128)S(1)} %get-tuple-element.73.refs_0_), channel_id=1, source_target_pairs={{0,8},{8,0},{16,24},{24,16},{1,9},{9,1},{17,25},{25,17},{2,10},{10... | collective-permute-start | bytes 12296 | tf_op jit(solution)/shard_map/ppermute | solution.py:509
  67.6 1.0 %collective-permute-done.16.refs_1_ = f32[8,128]{1,0:T(8,128)S(1)} collective-permute-done((f32[8,128]{1,0:T(8,128)S(1)}, f32[8,128]{1,0:T(8,128)S(1)}, u32[]{:S(2)}, u32[]{:S(2)}) %collective-permute-start.16) | collective-permute-done | bytes 4128 | tf_op jit(solution)/shard_map/ppermute | solution.py:509
  68.6 0.6 collective-permute-done.17.refs_2_
  69.2 0.5 collective-permute-done.18.refs_3_
  69.7 1.2 %collective-permute-done.19.refs_1_ = f32[8,128]{1,0:T(8,128)S(1)} collective-permute-done((f32[8,128]{1,0:T(8,128)S(1)}, f32[8,128]{1,0:T(8,128)S(1)}, u32[]{:S(2)}, u32[]{:S(2)}) %collective-permute-start.19) | collective-permute-done | bytes 4128 | tf_op jit(solution)/shard_map/ppermute | solution.py:509
  70.9 2.5 %collective-permute-start.20 = (f32[8,128]{1,0:T(8,128)S(1)}, f32[8,128]{1,0:T(8,128)S(1)}, u32[]{:S(2)}, u32[]{:S(2)}) collective-permute-start(f32[8,128]{1,0:T(8,128)S(1)} %fold.3.refs_0_), channel_id=1, source_target_pairs={{0,6},{1,7},{2,4},{3,5},{4,2},{5,3},{6,0},{7,1},{8,14},{9,15},{10,... | collective-permute-start | bytes 12296 | tf_op jit(solution)/shard_map/ppermute | solution.py:509
  73.3 1.5 %collective-permute-start.21 = (f32[8,128]{1,0:T(8,128)S(1)}, f32[8,128]{1,0:T(8,128)S(1)}, u32[]{:S(2)}, u32[]{:S(2)}) collective-permute-start(f32[8,128]{1,0:T(8,128)S(1)} %fold.3.refs_0_), channel_id=1, source_target_pairs={{0,4},{1,5},{2,6},{3,7},{4,0},{5,1},{6,2},{7,3},{8,12},{9,13},{10,... | collective-permute-start | bytes 12296 | tf_op jit(solution)/shard_map/ppermute | solution.py:509
  74.9 0.4 collective-permute-start.22
  75.3 1.0 %collective-permute-done.20.refs_1_ = f32[8,128]{1,0:T(8,128)S(1)} collective-permute-done((f32[8,128]{1,0:T(8,128)S(1)}, f32[8,128]{1,0:T(8,128)S(1)}, u32[]{:S(2)}, u32[]{:S(2)}) %collective-permute-start.20) | collective-permute-done | bytes 4128 | tf_op jit(solution)/shard_map/ppermute | solution.py:509
  76.3 1.6 %collective-permute-done.21.refs_2_ = f32[8,128]{1,0:T(8,128)S(1)} collective-permute-done((f32[8,128]{1,0:T(8,128)S(1)}, f32[8,128]{1,0:T(8,128)S(1)}, u32[]{:S(2)}, u32[]{:S(2)}) %collective-permute-start.21) | collective-permute-done | bytes 4128 | tf_op jit(solution)/shard_map/ppermute | solution.py:509
  77.9 0.6 collective-permute-done.22.refs_3_
  78.5 2.7 %basis.1 = (f32[96,3072]{1,0:T(8,128)}, f32[96,3072]{1,0:T(8,128)}) custom-call(f32[8,128]{1,0:T(8,128)S(1)} %fold.3.refs_0_, f32[8,128]{1,0:T(8,128)S(1)} %collective-permute-done.20.refs_1_, f32[8,128]{1,0:T(8,128)S(1)} %collective-permute-done.21.refs_2_, f32[8,128]{1,0:T(8,128)S(1)} %collective-permute-done.22.refs_3_, ...), custom_call_target="tpu_custom_call" | custom-call | tf_op jit(solution)/shard_map/basis/pallas_call | solution.py:577
  (6 shorter events, 0.0 us)
Async XLA Ops:
  0.6 16.6 %copy-start = (f32[3,24576]{1,0:T(4,128)S(1)}, f32[3,24576]{1,0:T(4,128)}, u32[]{:S(2)}) copy-start(f32[3,24576]{1,0:T(4,128)} %refs_7_.1) | copy-start | bytes 884740
  8.2 5.9 %collective-permute-start = (f32[80,128]{1,0:T(8,128)S(1)}, f32[80,128]{1,0:T(8,128)S(1)}, u32[]{:S(2)}, u32[]{:S(2)}) collective-permute-start(f32[80,128]{1,0:T(8,128)S(1)} %get-tuple-element.41.refs_0_), channel_id=1, source_target_pairs={{0,24},{8,16},{16,8},{24,0},{1,25},{9,17},{17,9},{25,1},{2,26},{10... | collective-permute-start | bytes 122888 | tf_op jit(solution)/shard_map/ppermute | solution.py:509
  12.2 4.0 %collective-permute-start.1 = (f32[80,128]{1,0:T(8,128)S(1)}, f32[80,128]{1,0:T(8,128)S(1)}, u32[]{:S(2)}, u32[]{:S(2)}) collective-permute-start(f32[80,128]{1,0:T(8,128)S(1)} %get-tuple-element.41.refs_0_), channel_id=1, source_target_pairs={{0,16},{8,24},{16,0},{24,8},{1,17},{9,25},{17,1},{25,9},{2,18},{10... | collective-permute-start | bytes 122888 | tf_op jit(solution)/shard_map/ppermute | solution.py:509
  12.7 4.0 %collective-permute-start.2 = (f32[80,128]{1,0:T(8,128)S(1)}, f32[80,128]{1,0:T(8,128)S(1)}, u32[]{:S(2)}, u32[]{:S(2)}) collective-permute-start(f32[80,128]{1,0:T(8,128)S(1)} %get-tuple-element.41.refs_0_), channel_id=1, source_target_pairs={{0,8},{8,0},{16,24},{24,16},{1,9},{9,1},{17,25},{25,17},{2,10},{10... | collective-permute-start | bytes 122888 | tf_op jit(solution)/shard_map/ppermute | solution.py:509
  17.5 1.9 %collective-permute-start.4 = (bf16[72,3072]{1,0:T(8,128)(2,1)S(1)}, bf16[72,3072]{1,0:T(8,128)(2,1)S(1)}, u32[]{:S(2)}, u32[]{:S(2)}) collective-permute-start(bf16[72,3072]{1,0:T(8,128)(2,1)S(1)} %displace.4), channel_id=1, source_target_pairs={{0,1},{1,0},{2,3},{3,2},{4,5},{5,4},{6,7},{7,6},{8,9},{9,8},{10,11... | collective-permute-start | bytes 1327112 | tf_op jit(solution)/shard_map/ppermute | solution.py:684
  17.6 1.8 %collective-permute-start.3 = (f32[24,128]{1,0:T(8,128)S(1)}, f32[24,128]{1,0:T(8,128)S(1)}, u32[]{:S(2)}, u32[]{:S(2)}) collective-permute-start(f32[24,128]{1,0:T(8,128)S(1)} %get-tuple-element.42.own_ref), channel_id=1, source_target_pairs={{0,1},{1,0},{2,3},{3,2},{4,5},{5,4},{6,7},{7,6},{8,9},{9,8},{10,11... | collective-permute-start | bytes 36872 | tf_op jit(solution)/shard_map/ppermute | solution.py:676
  19.4 12.1 %collective-permute-start.5 = (bf16[72,9216]{1,0:T(8,128)(2,1)S(1)}, bf16[72,9216]{1,0:T(8,128)(2,1)S(1)}, u32[]{:S(2)}, u32[]{:S(2)}) collective-permute-start(bf16[72,9216]{1,0:T(8,128)(2,1)S(1)} %displace.7), channel_id=1, source_target_pairs={{0,1},{1,0},{2,3},{3,2},{4,5},{5,4},{6,7},{7,6},{8,9},{9,8},{10,11... | collective-permute-start | bytes 3981320 | tf_op jit(solution)/shard_map/ppermute | solution.py:687
  20.1 11.4 %collective-permute-start.6 = (bf16[96,1664]{1,0:T(8,128)(2,1)S(1)}, bf16[96,1664]{1,0:T(8,128)(2,1)S(1)}, u32[]{:S(2)}, u32[]{:S(2)}) collective-permute-start(bf16[96,1664]{1,0:T(8,128)(2,1)S(1)} %term.11), channel_id=1, source_target_pairs={{0,2},{1,3},{6,4},{7,5},{8,10},{9,11},{14,12},{15,13},{16,18},{17,... | collective-permute-start | bytes 958472 | tf_op jit(solution)/shard_map/ppermute | solution.py:615
  24.0 13.9 %collective-permute-start.11 = (bf16[96,1536]{1,0:T(8,128)(2,1)S(1)}, bf16[96,1536]{1,0:T(8,128)(2,1)S(1)}, u32[]{:S(2)}, u32[]{:S(2)}) collective-permute-start(bf16[96,1536]{1,0:T(8,128)(2,1)S(1)} %term.10), channel_id=1, source_target_pairs={{0,2},{1,3},{6,4},{7,5},{8,10},{9,11},{14,12},{15,13},{16,18},{17,... | collective-permute-start | bytes 884744 | tf_op jit(solution)/shard_map/ppermute | solution.py:615
  31.9 12.8 %collective-permute-start.7 = (bf16[96,1664]{1,0:T(8,128)(2,1)S(1)}, bf16[96,1664]{1,0:T(8,128)(2,1)S(1)}, u32[]{:S(2)}, u32[]{:S(2)}) collective-permute-start(bf16[96,1664]{1,0:T(8,128)(2,1)S(1)} %term.12), channel_id=1, source_target_pairs={{0,2},{1,3},{6,4},{7,5},{8,10},{9,11},{14,12},{15,13},{16,18},{17,... | collective-permute-start | bytes 958472 | tf_op jit(solution)/shard_map/ppermute | solution.py:619
  36.9 7.7 %collective-permute-start.8 = (bf16[96,1664]{1,0:T(8,128)(2,1)S(1)}, bf16[96,1664]{1,0:T(8,128)(2,1)S(1)}, u32[]{:S(2)}, u32[]{:S(2)}) collective-permute-start(bf16[96,1664]{1,0:T(8,128)(2,1)S(1)} %term.13), channel_id=1, source_target_pairs={{2,4},{3,5},{4,2},{5,3},{10,12},{11,13},{12,10},{13,11},{18,20},{1... | collective-permute-start | bytes 958472 | tf_op jit(solution)/shard_map/ppermute | solution.py:621
  38.1 12.9 %collective-permute-start.12 = (bf16[96,1536]{1,0:T(8,128)(2,1)S(1)}, bf16[96,1536]{1,0:T(8,128)(2,1)S(1)}, u32[]{:S(2)}, u32[]{:S(2)}) collective-permute-start(bf16[96,1536]{1,0:T(8,128)(2,1)S(1)} %term.16), channel_id=1, source_target_pairs={{0,2},{1,3},{6,4},{7,5},{8,10},{9,11},{14,12},{15,13},{16,18},{17,... | collective-permute-start | bytes 884744 | tf_op jit(solution)/shard_map/ppermute | solution.py:619
  43.0 8.0 %collective-permute-start.13 = (bf16[96,1536]{1,0:T(8,128)(2,1)S(1)}, bf16[96,1536]{1,0:T(8,128)(2,1)S(1)}, u32[]{:S(2)}, u32[]{:S(2)}) collective-permute-start(bf16[96,1536]{1,0:T(8,128)(2,1)S(1)} %term.17), channel_id=1, source_target_pairs={{2,4},{3,5},{4,2},{5,3},{10,12},{11,13},{12,10},{13,11},{18,20},{1... | collective-permute-start | bytes 884744 | tf_op jit(solution)/shard_map/ppermute | solution.py:621
  45.3 12.6 %collective-permute-start.9 = (bf16[96,1664]{1,0:T(8,128)(2,1)S(1)}, bf16[96,1664]{1,0:T(8,128)(2,1)S(1)}, u32[]{:S(2)}, u32[]{:S(2)}) collective-permute-start(bf16[96,1664]{1,0:T(8,128)(2,1)S(1)} %term.14), channel_id=1, source_target_pairs={{0,2},{1,3},{6,4},{7,5},{4,6},{5,7},{2,0},{3,1},{8,10},{9,11},{14,... | collective-permute-start | bytes 958472 | tf_op jit(solution)/shard_map/ppermute | solution.py:625
  48.6 9.2 %collective-permute-start.10 = (bf16[96,1664]{1,0:T(8,128)(2,1)S(1)}, bf16[96,1664]{1,0:T(8,128)(2,1)S(1)}, u32[]{:S(2)}, u32[]{:S(2)}) collective-permute-start(bf16[96,1664]{1,0:T(8,128)(2,1)S(1)} %term.15), channel_id=1, source_target_pairs={{2,4},{3,5},{4,2},{5,3},{10,12},{11,13},{12,10},{13,11},{18,20},{1... | collective-permute-start | bytes 958472 | tf_op jit(solution)/shard_map/ppermute | solution.py:627
  51.4 12.2 %collective-permute-start.14 = (bf16[96,1536]{1,0:T(8,128)(2,1)S(1)}, bf16[96,1536]{1,0:T(8,128)(2,1)S(1)}, u32[]{:S(2)}, u32[]{:S(2)}) collective-permute-start(bf16[96,1536]{1,0:T(8,128)(2,1)S(1)} %term.18), channel_id=1, source_target_pairs={{0,2},{1,3},{6,4},{7,5},{4,6},{5,7},{2,0},{3,1},{8,10},{9,11},{14,... | collective-permute-start | bytes 884744 | tf_op jit(solution)/shard_map/ppermute | solution.py:625
  54.9 8.7 %collective-permute-start.15 = (bf16[96,1536]{1,0:T(8,128)(2,1)S(1)}, bf16[96,1536]{1,0:T(8,128)(2,1)S(1)}, u32[]{:S(2)}, u32[]{:S(2)}) collective-permute-start(bf16[96,1536]{1,0:T(8,128)(2,1)S(1)} %term.19), channel_id=1, source_target_pairs={{2,4},{3,5},{4,2},{5,3},{10,12},{11,13},{12,10},{13,11},{18,20},{1... | collective-permute-start | bytes 884744 | tf_op jit(solution)/shard_map/ppermute | solution.py:627
  64.1 4.5 %collective-permute-start.16 = (f32[8,128]{1,0:T(8,128)S(1)}, f32[8,128]{1,0:T(8,128)S(1)}, u32[]{:S(2)}, u32[]{:S(2)}) collective-permute-start(f32[8,128]{1,0:T(8,128)S(1)} %get-tuple-element.73.refs_0_), channel_id=1, source_target_pairs={{0,24},{8,16},{16,8},{24,0},{1,25},{9,17},{17,9},{25,1},{2,26},{10... | collective-permute-start | bytes 12296 | tf_op jit(solution)/shard_map/ppermute | solution.py:509
  65.6 3.6 %collective-permute-start.17 = (f32[8,128]{1,0:T(8,128)S(1)}, f32[8,128]{1,0:T(8,128)S(1)}, u32[]{:S(2)}, u32[]{:S(2)}) collective-permute-start(f32[8,128]{1,0:T(8,128)S(1)} %get-tuple-element.73.refs_0_), channel_id=1, source_target_pairs={{0,16},{8,24},{16,0},{24,8},{1,17},{9,25},{17,1},{25,9},{2,18},{10... | collective-permute-start | bytes 12296 | tf_op jit(solution)/shard_map/ppermute | solution.py:509
  66.1 3.6 %collective-permute-start.18 = (f32[8,128]{1,0:T(8,128)S(1)}, f32[8,128]{1,0:T(8,128)S(1)}, u32[]{:S(2)}, u32[]{:S(2)}) collective-permute-start(f32[8,128]{1,0:T(8,128)S(1)} %get-tuple-element.73.refs_0_), channel_id=1, source_target_pairs={{0,8},{8,0},{16,24},{24,16},{1,9},{9,1},{17,25},{25,17},{2,10},{10... | collective-permute-start | bytes 12296 | tf_op jit(solution)/shard_map/ppermute | solution.py:509
  69.7 1.2 %collective-permute-start.19 = (f32[8,128]{1,0:T(8,128)S(1)}, f32[8,128]{1,0:T(8,128)S(1)}, u32[]{:S(2)}, u32[]{:S(2)}) collective-permute-start(f32[8,128]{1,0:T(8,128)S(1)} %fold.2.refs_0_), channel_id=1, source_target_pairs={{0,1},{1,0},{2,3},{3,2},{4,5},{5,4},{6,7},{7,6},{8,9},{9,8},{10,11... | collective-permute-start | bytes 12296 | tf_op jit(solution)/shard_map/ppermute | solution.py:509
  70.9 5.4 %collective-permute-start.20 = (f32[8,128]{1,0:T(8,128)S(1)}, f32[8,128]{1,0:T(8,128)S(1)}, u32[]{:S(2)}, u32[]{:S(2)}) collective-permute-start(f32[8,128]{1,0:T(8,128)S(1)} %fold.3.refs_0_), channel_id=1, source_target_pairs={{0,6},{1,7},{2,4},{3,5},{4,2},{5,3},{6,0},{7,1},{8,14},{9,15},{10,... | collective-permute-start | bytes 12296 | tf_op jit(solution)/shard_map/ppermute | solution.py:509
  73.3 4.5 %collective-permute-start.21 = (f32[8,128]{1,0:T(8,128)S(1)}, f32[8,128]{1,0:T(8,128)S(1)}, u32[]{:S(2)}, u32[]{:S(2)}) collective-permute-start(f32[8,128]{1,0:T(8,128)S(1)} %fold.3.refs_0_), channel_id=1, source_target_pairs={{0,4},{1,5},{2,6},{3,7},{4,0},{5,1},{6,2},{7,3},{8,12},{9,13},{10,... | collective-permute-start | bytes 12296 | tf_op jit(solution)/shard_map/ppermute | solution.py:509
  74.9 3.6 %collective-permute-start.22 = (f32[8,128]{1,0:T(8,128)S(1)}, f32[8,128]{1,0:T(8,128)S(1)}, u32[]{:S(2)}, u32[]{:S(2)}) collective-permute-start(f32[8,128]{1,0:T(8,128)S(1)} %fold.3.refs_0_), channel_id=1, source_target_pairs={{0,2},{1,3},{2,0},{3,1},{4,6},{5,7},{6,4},{7,5},{8,10},{9,11},{10,... | collective-permute-start | bytes 12296 | tf_op jit(solution)/shard_map/ppermute | solution.py:509

commit v4 on v3

--- a/solution.py
+++ b/solution.py
@@ -78,30 +78,26 @@
     row = lax.broadcasted_iota(jnp.int32, (8, TILE), 0)
     ones = jnp.where(row == 3, 1.0, 0.0)
     total = jnp.zeros(out_ref.shape, F32)
-
-    def product(t):
-        sums = dot_nt(lhs_ref[t % 2], rhs_ref[:, t * chunk : (t + 1) * chunk])
-        return sums[0:n] + sums[n : 2 * n]
-
     for t in range(chunks):
         for copy in copies[t + 1]:
             copy.wait()
+        slot, half = t // 2 % 2, t % 2 * chunk
         for start in range(0, chunk, TILE):
             lanes = slice(t * chunk + start, t * chunk + start + TILE)
-            here = slice(start, start + TILE)
+            here = slice(half + start, half + start + TILE)
             left = ones
             for i in range(3):
                 left = jnp.where(row == i, m_ref[i : i + 1, lanes], left)
             value = jnp.concatenate([x_ref[:, lanes], left], axis=0)
             high = value.astype(BF16)
-            lhs_ref[t % 2, 0:n, here] = high
-            lhs_ref[t % 2, n : 2 * n, here] = (value - high.astype(F32)).astype(BF16)
+            lhs_ref[slot, 0:n, here] = high
+            lhs_ref[slot, n : 2 * n, here] = (value - high.astype(F32)).astype(BF16)
             pieces = [v.astype(F32) for v in split3(left * w_ref[:, lanes])]
             aux = jnp.concatenate(pieces + [jnp.zeros(left.shape, F32)], axis=0)
             rhs_ref[vectors:, lanes] = aux.astype(BF16)
-        if t > 0:
-            total = total + product(t - 1)
-    total = total + product(chunks - 1)
+        if t % 2 == 1:
+            sums = dot_nt(lhs_ref[slot], rhs_ref[:, (t - 1) * chunk : (t + 1) * chunk])
+            total = total + (sums[0:n] + sums[n : 2 * n])
     out_ref[...] = total
 
 
@@ -119,7 +115,7 @@
         scratch_shapes=[
             pltpu.VMEM(mean.shape, F32),
             pltpu.VMEM(weight.shape, F32),
-            pltpu.VMEM((2, 2 * n, chunk), BF16),
+            pltpu.VMEM((2, 2 * n, 2 * chunk), BF16),
             pltpu.VMEM((LANES, atoms), BF16),
             pltpu.SemaphoreType.DMA((2, chunks + 1)),
         ],
@@ -543,7 +539,11 @@
         ]
         for q in range(PANEL):
             j = panel + q
-            factor = columns[q] * (1.0 / columns[q][j : j + 1, :])
+            pivot = columns[q][j : j + 1, :]
+            inverse = pl.reciprocal(pivot, approx=True)
+            for _ in range(2):
+                inverse = inverse * (2.0 - pivot * inverse)
+            factor = columns[q] * inverse
             factor = jnp.where(row > j, factor, 0.0)
             for r in range(q + 1, PANEL):
                 columns[r] = columns[r] - factor * columns[r][j : j + 1, :]

time: 81.4 us -> 81.1 us (level)
  no operation moved by 1% of the time
where the time goes in v4:
time: 81.1 us; the launch traced here: 80.8 us
  starting transfers between devices  35.2 us (43%)
  waiting for transfers between devices  25.4 us (31%)
  Pallas kernels  19.2 us (24%)
  between operations  1 us (1%)
    ppermute x10, starting transfers between devices, exchanged(): lax.ppermute(value, axis, [(i, i ^ mask) for i in range(size)])  12.5 us
    ppermute x10, waiting for transfers between devices, exchanged(): lax.ppermute(value, axis, [(i, i ^ mask) for i in range(size)])  10.3 us
    ppermute x2, starting transfers between devices, along_four(): ends.append(lax.ppermute(out, 'frames', inward))  8.8 us
    pallas_call x1, Pallas kernels, moments(): pl.pallas_call(moments_kernel, in_specs=[pl.BlockSpec(memory_space=pltpu....  6.94 us
    ppermute x2, waiting for transfers between devices, along_four(): end = lax.ppermute(out, 'frames', inward + outward)  6.76 us
    ppermute x2, starting transfers between devices, along_four(): end = lax.ppermute(out, 'frames', inward + outward)  5.69 us
    ppermute x2, waiting for transfers between devices, along_four(): first = [lax.ppermute(make_first(p), 'frames', inward) for p in each]  5.47 us
    ppermute x2, starting transfers between devices, along_four(): first = [lax.ppermute(make_first(p), 'frames', inward) for p in each]  4.82 us
  transfers between devices with their start and end apart: 23, of which 17 were waited for; matrix products, arithmetic and copies ran while one was open for 0% of the time, Pallas kernels for 10%

profile of v4, /device:TPU:0, one launch (start us, length us, event | category | flops | bytes accessed | tf_op | source)
XLA Modules:
  0.0 80.8 jit_solution(1711677511222594846)
XLA Ops:
  0.6 6.9 %moments.1 = (f32[80,128]{1,0:T(8,128)S(1)}, f32[72,24576]{1,0:T(8,128)S(1)}) custom-call(s32[1]{0:T(128)} %bitcast._.idx, f32[72,24576]{1,0:T(8,128)} %bitcast.14, f32[3,24576]{1,0:T(4,128)} %refs_7_.1, f32[1,24576]{1,0:T(1,128)} %bitcast.16, bf16[96,24576]{1,0:T(8,128)(2,1)} %bitcast.15), custom_call_target="tpu_custom_call" | custom-call | tf_op jit(solution)/shard_map/moments/pallas_call | solution.py:110
  7.6 4.0 %collective-permute-start = (f32[80,128]{1,0:T(8,128)S(1)}, f32[80,128]{1,0:T(8,128)S(1)}, u32[]{:S(2)}, u32[]{:S(2)}) collective-permute-start(f32[80,128]{1,0:T(8,128)S(1)} %get-tuple-element.41.refs_0_), channel_id=1, source_target_pairs={{0,24},{8,16},{16,8},{24,0},{1,25},{9,17},{17,9},{25,1},{2,26},{10... | collective-permute-start | bytes 122888 | tf_op jit(solution)/shard_map/ppermute | solution.py:505
  11.6 0.5 collective-permute-start.1
  12.1 0.1 collective-permute-start.2
  12.2 1.3 %collective-permute-done.refs_1_ = f32[80,128]{1,0:T(8,128)S(1)} collective-permute-done((f32[80,128]{1,0:T(8,128)S(1)}, f32[80,128]{1,0:T(8,128)S(1)}, u32[]{:S(2)}, u32[]{:S(2)}) %collective-permute-start) | collective-permute-done | bytes 40992 | tf_op jit(solution)/shard_map/ppermute | solution.py:505
  13.5 2.0 %collective-permute-done.1.refs_2_ = f32[80,128]{1,0:T(8,128)S(1)} collective-permute-done((f32[80,128]{1,0:T(8,128)S(1)}, f32[80,128]{1,0:T(8,128)S(1)}, u32[]{:S(2)}, u32[]{:S(2)}) %collective-permute-start.1) | collective-permute-done | bytes 40992 | tf_op jit(solution)/shard_map/ppermute | solution.py:505
  15.6 0.5 collective-permute-done.2.refs_3_
  16.1 0.6 rotate.1
  16.7 0.3 displace.4
  16.9 0.1 collective-permute-start.4
  17.0 0.5 collective-permute-start.3
  17.5 0.3 displace.5.refs_3_
  17.8 0.9 %displace.7 = bf16[72,9216]{1,0:T(8,128)(2,1)S(1)} custom-call(s32[1]{0:T(128)} %bitcast._.idx, f32[72,24576]{1,0:T(8,128)S(1)} %get-tuple-element.46.x_ref, f32[3,24576]{1,0:T(4,128)S(1)} %copy-done, f32[288,128]{1,0:T(8,128)S(1)} %get-tuple-element.50.coef_ref), custom_call_target="tpu_custom_call" | custom-call | tf_op jit(solution)/shard_map/displace/pallas_call | solution.py:235
  18.7 0.1 collective-permute-done.3.other_ref
  18.8 0.0 collective-permute-done.4.refs_4_
  18.8 0.1 collective-permute-start.5
  18.9 0.2 weights.1
  19.1 0.4 term.11
  19.5 3.5 %collective-permute-start.6 = (bf16[96,1664]{1,0:T(8,128)(2,1)S(1)}, bf16[96,1664]{1,0:T(8,128)(2,1)S(1)}, u32[]{:S(2)}, u32[]{:S(2)}) collective-permute-start(bf16[96,1664]{1,0:T(8,128)(2,1)S(1)} %term.11), channel_id=1, source_target_pairs={{0,2},{1,3},{6,4},{7,5},{8,10},{9,11},{14,12},{15,13},{16,18},{17,... | collective-permute-start | bytes 958472 | tf_op jit(solution)/shard_map/ppermute | solution.py:615
  23.1 0.3 term.10
  23.4 1.3 %collective-permute-start.11 = (bf16[96,1536]{1,0:T(8,128)(2,1)S(1)}, bf16[96,1536]{1,0:T(8,128)(2,1)S(1)}, u32[]{:S(2)}, u32[]{:S(2)}) collective-permute-start(bf16[96,1536]{1,0:T(8,128)(2,1)S(1)} %term.10), channel_id=1, source_target_pairs={{0,2},{1,3},{6,4},{7,5},{8,10},{9,11},{14,12},{15,13},{16,18},{17,... | collective-permute-start | bytes 884744 | tf_op jit(solution)/shard_map/ppermute | solution.py:615
  24.7 0.9 %displace.6.refs_3_.refs_5_ = bf16[72,9216]{1,0:T(8,128)(2,1)S(1)} custom-call(s32[1]{0:T(128)} %bitcast._.idx, f32[72,24576]{1,0:T(8,128)S(1)} %get-tuple-element.46.x_ref, f32[3,24576]{1,0:T(4,128)S(1)} %copy-done, f32[288,128]{1,0:T(8,128)S(1)} %get-tuple-element.50.coef_ref), custom_call_target="tpu_custom_call" | custom-call | tf_op jit(solution)/shard_map/displace/pallas_call | solution.py:235
  25.6 5.3 %collective-permute-done.6.refs_5_ = bf16[96,1664]{1,0:T(8,128)(2,1)S(1)} collective-permute-done((bf16[96,1664]{1,0:T(8,128)(2,1)S(1)}, bf16[96,1664]{1,0:T(8,128)(2,1)S(1)}, u32[]{:S(2)}, u32[]{:S(2)}) %collective-permute-start.6) | collective-permute-done | bytes 319520 | tf_op jit(solution)/shard_map/ppermute | solution.py:615
  30.9 0.0 collective-permute-done.5.refs_4_.refs_6_
  30.9 0.4 term.12
  31.3 4.4 %collective-permute-start.7 = (bf16[96,1664]{1,0:T(8,128)(2,1)S(1)}, bf16[96,1664]{1,0:T(8,128)(2,1)S(1)}, u32[]{:S(2)}, u32[]{:S(2)}) collective-permute-start(bf16[96,1664]{1,0:T(8,128)(2,1)S(1)} %term.12), channel_id=1, source_target_pairs={{0,2},{1,3},{6,4},{7,5},{8,10},{9,11},{14,12},{15,13},{16,18},{17,... | collective-permute-start | bytes 958472 | tf_op jit(solution)/shard_map/ppermute | solution.py:619
  35.7 0.6 term.13
  36.3 0.7 collective-permute-start.8
  37.0 0.2 collective-permute-done.11.refs_6_
  37.2 0.3 term.16
  37.5 4.4 %collective-permute-start.12 = (bf16[96,1536]{1,0:T(8,128)(2,1)S(1)}, bf16[96,1536]{1,0:T(8,128)(2,1)S(1)}, u32[]{:S(2)}, u32[]{:S(2)}) collective-permute-start(bf16[96,1536]{1,0:T(8,128)(2,1)S(1)} %term.16), channel_id=1, source_target_pairs={{0,2},{1,3},{6,4},{7,5},{8,10},{9,11},{14,12},{15,13},{16,18},{17,... | collective-permute-start | bytes 884744 | tf_op jit(solution)/shard_map/ppermute | solution.py:619
  41.9 0.5 term.17
  42.4 0.7 collective-permute-start.13
  43.1 1.0 %collective-permute-done.7.refs_5_ = bf16[96,1664]{1,0:T(8,128)(2,1)S(1)} collective-permute-done((bf16[96,1664]{1,0:T(8,128)(2,1)S(1)}, bf16[96,1664]{1,0:T(8,128)(2,1)S(1)}, u32[]{:S(2)}, u32[]{:S(2)}) %collective-permute-start.7) | collective-permute-done | bytes 319520 | tf_op jit(solution)/shard_map/ppermute | solution.py:619
  44.1 0.0 collective-permute-done.8.refs_5_
  44.1 0.6 term.14
  44.7 2.7 %collective-permute-start.9 = (bf16[96,1664]{1,0:T(8,128)(2,1)S(1)}, bf16[96,1664]{1,0:T(8,128)(2,1)S(1)}, u32[]{:S(2)}, u32[]{:S(2)}) collective-permute-start(bf16[96,1664]{1,0:T(8,128)(2,1)S(1)} %term.14), channel_id=1, source_target_pairs={{0,2},{1,3},{6,4},{7,5},{4,6},{5,7},{2,0},{3,1},{8,10},{9,11},{14,... | collective-permute-start | bytes 958472 | tf_op jit(solution)/shard_map/ppermute | solution.py:625
  47.4 0.6 term.15
  48.0 0.7 collective-permute-start.10
  48.7 1.7 %collective-permute-done.12.refs_6_ = bf16[96,1536]{1,0:T(8,128)(2,1)S(1)} collective-permute-done((bf16[96,1536]{1,0:T(8,128)(2,1)S(1)}, bf16[96,1536]{1,0:T(8,128)(2,1)S(1)}, u32[]{:S(2)}, u32[]{:S(2)}) %collective-permute-start.12) | collective-permute-done | bytes 294944 | tf_op jit(solution)/shard_map/ppermute | solution.py:619
  50.4 0.0 collective-permute-done.13.refs_6_
  50.4 0.4 term.18
  50.8 3.0 %collective-permute-start.14 = (bf16[96,1536]{1,0:T(8,128)(2,1)S(1)}, bf16[96,1536]{1,0:T(8,128)(2,1)S(1)}, u32[]{:S(2)}, u32[]{:S(2)}) collective-permute-start(bf16[96,1536]{1,0:T(8,128)(2,1)S(1)} %term.18), channel_id=1, source_target_pairs={{0,2},{1,3},{6,4},{7,5},{4,6},{5,7},{2,0},{3,1},{8,10},{9,11},{14,... | collective-permute-start | bytes 884744 | tf_op jit(solution)/shard_map/ppermute | solution.py:625
  53.8 0.4 term.19
  54.2 0.7 collective-permute-start.15
  54.9 2.3 %collective-permute-done.9.refs_8_ = bf16[96,1664]{1,0:T(8,128)(2,1)S(1)} collective-permute-done((bf16[96,1664]{1,0:T(8,128)(2,1)S(1)}, bf16[96,1664]{1,0:T(8,128)(2,1)S(1)}, u32[]{:S(2)}, u32[]{:S(2)}) %collective-permute-start.9) | collective-permute-done | bytes 319520 | tf_op jit(solution)/shard_map/ppermute | solution.py:625
  57.2 0.0 collective-permute-done.10.refs_9_
  57.2 1.3 %first_piece.1 = (f32[96,1536]{1,0:T(8,128)S(1)}, f32[8,128]{1,0:T(8,128)S(1)}, f32[3,3072]{1,0:T(4,128)}, f32[96,1536]{1,0:T(8,128)S(1)}) custom-call(s32[1]{0:T(128)} %bitcast._.idx, bf16[96,72]{1,0:T(8,128)(2,1)S(1)} %get-tuple-element.70.refs_0_, bf16[96,72]{1,0:T(8,128)(2,1)S(1)} %get-tuple-element.71.refs_1_, f32[8,128]{1,0:T(8,128)S(1)} %get-tuple-element.72.refs_2_, ...), custom_call_target="tpu_custom_call" | custom-call | flops 2000000000 | bytes 1 | tf_op jit(solution)/shard_map/first_piece/pallas_call | solution.py:445
  58.5 4.4 %collective-permute-done.14.refs_0_ = bf16[96,1536]{1,0:T(8,128)(2,1)S(1)} collective-permute-done((bf16[96,1536]{1,0:T(8,128)(2,1)S(1)}, bf16[96,1536]{1,0:T(8,128)(2,1)S(1)}, u32[]{:S(2)}, u32[]{:S(2)}) %collective-permute-start.14) | collective-permute-done | bytes 294944 | tf_op jit(solution)/shard_map/ppermute | solution.py:625
  63.0 0.4 second_piece.1
  63.4 1.5 %collective-permute-start.16 = (f32[8,128]{1,0:T(8,128)S(1)}, f32[8,128]{1,0:T(8,128)S(1)}, u32[]{:S(2)}, u32[]{:S(2)}) collective-permute-start(f32[8,128]{1,0:T(8,128)S(1)} %get-tuple-element.73.refs_0_), channel_id=1, source_target_pairs={{0,24},{8,16},{16,8},{24,0},{1,25},{9,17},{17,9},{25,1},{2,26},{10... | collective-permute-start | bytes 12296 | tf_op jit(solution)/shard_map/ppermute | solution.py:505
  65.0 0.5 collective-permute-start.17
  65.5 1.5 %collective-permute-start.18 = (f32[8,128]{1,0:T(8,128)S(1)}, f32[8,128]{1,0:T(8,128)S(1)}, u32[]{:S(2)}, u32[]{:S(2)}) collective-permute-start(f32[8,128]{1,0:T(8,128)S(1)} %get-tuple-element.73.refs_0_), channel_id=1, source_target_pairs={{0,8},{8,0},{16,24},{24,16},{1,9},{9,1},{17,25},{25,17},{2,10},{10... | collective-permute-start | bytes 12296 | tf_op jit(solution)/shard_map/ppermute | solution.py:505
  66.9 1.0 %collective-permute-done.16.refs_1_ = f32[8,128]{1,0:T(8,128)S(1)} collective-permute-done((f32[8,128]{1,0:T(8,128)S(1)}, f32[8,128]{1,0:T(8,128)S(1)}, u32[]{:S(2)}, u32[]{:S(2)}) %collective-permute-start.16) | collective-permute-done | bytes 4128 | tf_op jit(solution)/shard_map/ppermute | solution.py:505
  68.0 0.6 collective-permute-done.17.refs_2_
  68.6 0.5 collective-permute-done.18.refs_3_
  69.1 1.2 %collective-permute-done.19.refs_1_ = f32[8,128]{1,0:T(8,128)S(1)} collective-permute-done((f32[8,128]{1,0:T(8,128)S(1)}, f32[8,128]{1,0:T(8,128)S(1)}, u32[]{:S(2)}, u32[]{:S(2)}) %collective-permute-start.19) | collective-permute-done | bytes 4128 | tf_op jit(solution)/shard_map/ppermute | solution.py:505
  70.2 2.5 %collective-permute-start.20 = (f32[8,128]{1,0:T(8,128)S(1)}, f32[8,128]{1,0:T(8,128)S(1)}, u32[]{:S(2)}, u32[]{:S(2)}) collective-permute-start(f32[8,128]{1,0:T(8,128)S(1)} %fold.3.refs_0_), channel_id=1, source_target_pairs={{0,6},{1,7},{2,4},{3,5},{4,2},{5,3},{6,0},{7,1},{8,14},{9,15},{10,... | collective-permute-start | bytes 12296 | tf_op jit(solution)/shard_map/ppermute | solution.py:505
  72.7 1.5 %collective-permute-start.21 = (f32[8,128]{1,0:T(8,128)S(1)}, f32[8,128]{1,0:T(8,128)S(1)}, u32[]{:S(2)}, u32[]{:S(2)}) collective-permute-start(f32[8,128]{1,0:T(8,128)S(1)} %fold.3.refs_0_), channel_id=1, source_target_pairs={{0,4},{1,5},{2,6},{3,7},{4,0},{5,1},{6,2},{7,3},{8,12},{9,13},{10,... | collective-permute-start | bytes 12296 | tf_op jit(solution)/shard_map/ppermute | solution.py:505
  74.2 0.4 collective-permute-start.22
  74.6 1.0 %collective-permute-done.20.refs_1_ = f32[8,128]{1,0:T(8,128)S(1)} collective-permute-done((f32[8,128]{1,0:T(8,128)S(1)}, f32[8,128]{1,0:T(8,128)S(1)}, u32[]{:S(2)}, u32[]{:S(2)}) %collective-permute-start.20) | collective-permute-done | bytes 4128 | tf_op jit(solution)/shard_map/ppermute | solution.py:505
  75.6 1.6 %collective-permute-done.21.refs_2_ = f32[8,128]{1,0:T(8,128)S(1)} collective-permute-done((f32[8,128]{1,0:T(8,128)S(1)}, f32[8,128]{1,0:T(8,128)S(1)}, u32[]{:S(2)}, u32[]{:S(2)}) %collective-permute-start.21) | collective-permute-done | bytes 4128 | tf_op jit(solution)/shard_map/ppermute | solution.py:505
  77.2 0.6 collective-permute-done.22.refs_3_
  77.8 2.8 %basis.1 = (f32[96,3072]{1,0:T(8,128)}, f32[96,3072]{1,0:T(8,128)}) custom-call(f32[8,128]{1,0:T(8,128)S(1)} %fold.3.refs_0_, f32[8,128]{1,0:T(8,128)S(1)} %collective-permute-done.20.refs_1_, f32[8,128]{1,0:T(8,128)S(1)} %collective-permute-done.21.refs_2_, f32[8,128]{1,0:T(8,128)S(1)} %collective-permute-done.22.refs_3_, ...), custom_call_target="tpu_custom_call" | custom-call | tf_op jit(solution)/shard_map/basis/pallas_call | solution.py:577
  (6 shorter events, 0.0 us)
Async XLA Ops:
  0.6 16.0 %copy-start = (f32[3,24576]{1,0:T(4,128)S(1)}, f32[3,24576]{1,0:T(4,128)}, u32[]{:S(2)}) copy-start(f32[3,24576]{1,0:T(4,128)} %refs_7_.1) | copy-start | bytes 884740
  7.6 5.9 %collective-permute-start = (f32[80,128]{1,0:T(8,128)S(1)}, f32[80,128]{1,0:T(8,128)S(1)}, u32[]{:S(2)}, u32[]{:S(2)}) collective-permute-start(f32[80,128]{1,0:T(8,128)S(1)} %get-tuple-element.41.refs_0_), channel_id=1, source_target_pairs={{0,24},{8,16},{16,8},{24,0},{1,25},{9,17},{17,9},{25,1},{2,26},{10... | collective-permute-start | bytes 122888 | tf_op jit(solution)/shard_map/ppermute | solution.py:505
  11.6 4.0 %collective-permute-start.1 = (f32[80,128]{1,0:T(8,128)S(1)}, f32[80,128]{1,0:T(8,128)S(1)}, u32[]{:S(2)}, u32[]{:S(2)}) collective-permute-start(f32[80,128]{1,0:T(8,128)S(1)} %get-tuple-element.41.refs_0_), channel_id=1, source_target_pairs={{0,16},{8,24},{16,0},{24,8},{1,17},{9,25},{17,1},{25,9},{2,18},{10... | collective-permute-start | bytes 122888 | tf_op jit(solution)/shard_map/ppermute | solution.py:505
  12.1 4.0 %collective-permute-start.2 = (f32[80,128]{1,0:T(8,128)S(1)}, f32[80,128]{1,0:T(8,128)S(1)}, u32[]{:S(2)}, u32[]{:S(2)}) collective-permute-start(f32[80,128]{1,0:T(8,128)S(1)} %get-tuple-element.41.refs_0_), channel_id=1, source_target_pairs={{0,8},{8,0},{16,24},{24,16},{1,9},{9,1},{17,25},{25,17},{2,10},{10... | collective-permute-start | bytes 122888 | tf_op jit(solution)/shard_map/ppermute | solution.py:505
  16.9 1.9 %collective-permute-start.4 = (bf16[72,3072]{1,0:T(8,128)(2,1)S(1)}, bf16[72,3072]{1,0:T(8,128)(2,1)S(1)}, u32[]{:S(2)}, u32[]{:S(2)}) collective-permute-start(bf16[72,3072]{1,0:T(8,128)(2,1)S(1)} %displace.4), channel_id=1, source_target_pairs={{0,1},{1,0},{2,3},{3,2},{4,5},{5,4},{6,7},{7,6},{8,9},{9,8},{10,11... | collective-permute-start | bytes 1327112 | tf_op jit(solution)/shard_map/ppermute | solution.py:684
  17.0 1.8 %collective-permute-start.3 = (f32[24,128]{1,0:T(8,128)S(1)}, f32[24,128]{1,0:T(8,128)S(1)}, u32[]{:S(2)}, u32[]{:S(2)}) collective-permute-start(f32[24,128]{1,0:T(8,128)S(1)} %get-tuple-element.42.own_ref), channel_id=1, source_target_pairs={{0,1},{1,0},{2,3},{3,2},{4,5},{5,4},{6,7},{7,6},{8,9},{9,8},{10,11... | collective-permute-start | bytes 36872 | tf_op jit(solution)/shard_map/ppermute | solution.py:676
  18.8 12.1 %collective-permute-start.5 = (bf16[72,9216]{1,0:T(8,128)(2,1)S(1)}, bf16[72,9216]{1,0:T(8,128)(2,1)S(1)}, u32[]{:S(2)}, u32[]{:S(2)}) collective-permute-start(bf16[72,9216]{1,0:T(8,128)(2,1)S(1)} %displace.7), channel_id=1, source_target_pairs={{0,1},{1,0},{2,3},{3,2},{4,5},{5,4},{6,7},{7,6},{8,9},{9,8},{10,11... | collective-permute-start | bytes 3981320 | tf_op jit(solution)/shard_map/ppermute | solution.py:687
  19.5 11.4 %collective-permute-start.6 = (bf16[96,1664]{1,0:T(8,128)(2,1)S(1)}, bf16[96,1664]{1,0:T(8,128)(2,1)S(1)}, u32[]{:S(2)}, u32[]{:S(2)}) collective-permute-start(bf16[96,1664]{1,0:T(8,128)(2,1)S(1)} %term.11), channel_id=1, source_target_pairs={{0,2},{1,3},{6,4},{7,5},{8,10},{9,11},{14,12},{15,13},{16,18},{17,... | collective-permute-start | bytes 958472 | tf_op jit(solution)/shard_map/ppermute | solution.py:615
  23.4 13.9 %collective-permute-start.11 = (bf16[96,1536]{1,0:T(8,128)(2,1)S(1)}, bf16[96,1536]{1,0:T(8,128)(2,1)S(1)}, u32[]{:S(2)}, u32[]{:S(2)}) collective-permute-start(bf16[96,1536]{1,0:T(8,128)(2,1)S(1)} %term.10), channel_id=1, source_target_pairs={{0,2},{1,3},{6,4},{7,5},{8,10},{9,11},{14,12},{15,13},{16,18},{17,... | collective-permute-start | bytes 884744 | tf_op jit(solution)/shard_map/ppermute | solution.py:615
  31.3 12.7 %collective-permute-start.7 = (bf16[96,1664]{1,0:T(8,128)(2,1)S(1)}, bf16[96,1664]{1,0:T(8,128)(2,1)S(1)}, u32[]{:S(2)}, u32[]{:S(2)}) collective-permute-start(bf16[96,1664]{1,0:T(8,128)(2,1)S(1)} %term.12), channel_id=1, source_target_pairs={{0,2},{1,3},{6,4},{7,5},{8,10},{9,11},{14,12},{15,13},{16,18},{17,... | collective-permute-start | bytes 958472 | tf_op jit(solution)/shard_map/ppermute | solution.py:619
  36.3 7.7 %collective-permute-start.8 = (bf16[96,1664]{1,0:T(8,128)(2,1)S(1)}, bf16[96,1664]{1,0:T(8,128)(2,1)S(1)}, u32[]{:S(2)}, u32[]{:S(2)}) collective-permute-start(bf16[96,1664]{1,0:T(8,128)(2,1)S(1)} %term.13), channel_id=1, source_target_pairs={{2,4},{3,5},{4,2},{5,3},{10,12},{11,13},{12,10},{13,11},{18,20},{1... | collective-permute-start | bytes 958472 | tf_op jit(solution)/shard_map/ppermute | solution.py:621
  37.5 12.9 %collective-permute-start.12 = (bf16[96,1536]{1,0:T(8,128)(2,1)S(1)}, bf16[96,1536]{1,0:T(8,128)(2,1)S(1)}, u32[]{:S(2)}, u32[]{:S(2)}) collective-permute-start(bf16[96,1536]{1,0:T(8,128)(2,1)S(1)} %term.16), channel_id=1, source_target_pairs={{0,2},{1,3},{6,4},{7,5},{8,10},{9,11},{14,12},{15,13},{16,18},{17,... | collective-permute-start | bytes 884744 | tf_op jit(solution)/shard_map/ppermute | solution.py:619
  42.4 8.0 %collective-permute-start.13 = (bf16[96,1536]{1,0:T(8,128)(2,1)S(1)}, bf16[96,1536]{1,0:T(8,128)(2,1)S(1)}, u32[]{:S(2)}, u32[]{:S(2)}) collective-permute-start(bf16[96,1536]{1,0:T(8,128)(2,1)S(1)} %term.17), channel_id=1, source_target_pairs={{2,4},{3,5},{4,2},{5,3},{10,12},{11,13},{12,10},{13,11},{18,20},{1... | collective-permute-start | bytes 884744 | tf_op jit(solution)/shard_map/ppermute | solution.py:621
  44.7 12.6 %collective-permute-start.9 = (bf16[96,1664]{1,0:T(8,128)(2,1)S(1)}, bf16[96,1664]{1,0:T(8,128)(2,1)S(1)}, u32[]{:S(2)}, u32[]{:S(2)}) collective-permute-start(bf16[96,1664]{1,0:T(8,128)(2,1)S(1)} %term.14), channel_id=1, source_target_pairs={{0,2},{1,3},{6,4},{7,5},{4,6},{5,7},{2,0},{3,1},{8,10},{9,11},{14,... | collective-permute-start | bytes 958472 | tf_op jit(solution)/shard_map/ppermute | solution.py:625
  48.0 9.2 %collective-permute-start.10 = (bf16[96,1664]{1,0:T(8,128)(2,1)S(1)}, bf16[96,1664]{1,0:T(8,128)(2,1)S(1)}, u32[]{:S(2)}, u32[]{:S(2)}) collective-permute-start(bf16[96,1664]{1,0:T(8,128)(2,1)S(1)} %term.15), channel_id=1, source_target_pairs={{2,4},{3,5},{4,2},{5,3},{10,12},{11,13},{12,10},{13,11},{18,20},{1... | collective-permute-start | bytes 958472 | tf_op jit(solution)/shard_map/ppermute | solution.py:627
  50.8 12.2 %collective-permute-start.14 = (bf16[96,1536]{1,0:T(8,128)(2,1)S(1)}, bf16[96,1536]{1,0:T(8,128)(2,1)S(1)}, u32[]{:S(2)}, u32[]{:S(2)}) collective-permute-start(bf16[96,1536]{1,0:T(8,128)(2,1)S(1)} %term.18), channel_id=1, source_target_pairs={{0,2},{1,3},{6,4},{7,5},{4,6},{5,7},{2,0},{3,1},{8,10},{9,11},{14,... | collective-permute-start | bytes 884744 | tf_op jit(solution)/shard_map/ppermute | solution.py:625
  54.2 8.8 %collective-permute-start.15 = (bf16[96,1536]{1,0:T(8,128)(2,1)S(1)}, bf16[96,1536]{1,0:T(8,128)(2,1)S(1)}, u32[]{:S(2)}, u32[]{:S(2)}) collective-permute-start(bf16[96,1536]{1,0:T(8,128)(2,1)S(1)} %term.19), channel_id=1, source_target_pairs={{2,4},{3,5},{4,2},{5,3},{10,12},{11,13},{12,10},{13,11},{18,20},{1... | collective-permute-start | bytes 884744 | tf_op jit(solution)/shard_map/ppermute | solution.py:627
  63.4 4.5 %collective-permute-start.16 = (f32[8,128]{1,0:T(8,128)S(1)}, f32[8,128]{1,0:T(8,128)S(1)}, u32[]{:S(2)}, u32[]{:S(2)}) collective-permute-start(f32[8,128]{1,0:T(8,128)S(1)} %get-tuple-element.73.refs_0_), channel_id=1, source_target_pairs={{0,24},{8,16},{16,8},{24,0},{1,25},{9,17},{17,9},{25,1},{2,26},{10... | collective-permute-start | bytes 12296 | tf_op jit(solution)/shard_map/ppermute | solution.py:505
  65.0 3.6 %collective-permute-start.17 = (f32[8,128]{1,0:T(8,128)S(1)}, f32[8,128]{1,0:T(8,128)S(1)}, u32[]{:S(2)}, u32[]{:S(2)}) collective-permute-start(f32[8,128]{1,0:T(8,128)S(1)} %get-tuple-element.73.refs_0_), channel_id=1, source_target_pairs={{0,16},{8,24},{16,0},{24,8},{1,17},{9,25},{17,1},{25,9},{2,18},{10... | collective-permute-start | bytes 12296 | tf_op jit(solution)/shard_map/ppermute | solution.py:505
  65.5 3.6 %collective-permute-start.18 = (f32[8,128]{1,0:T(8,128)S(1)}, f32[8,128]{1,0:T(8,128)S(1)}, u32[]{:S(2)}, u32[]{:S(2)}) collective-permute-start(f32[8,128]{1,0:T(8,128)S(1)} %get-tuple-element.73.refs_0_), channel_id=1, source_target_pairs={{0,8},{8,0},{16,24},{24,16},{1,9},{9,1},{17,25},{25,17},{2,10},{10... | collective-permute-start | bytes 12296 | tf_op jit(solution)/shard_map/ppermute | solution.py:505
  69.1 1.2 %collective-permute-start.19 = (f32[8,128]{1,0:T(8,128)S(1)}, f32[8,128]{1,0:T(8,128)S(1)}, u32[]{:S(2)}, u32[]{:S(2)}) collective-permute-start(f32[8,128]{1,0:T(8,128)S(1)} %fold.2.refs_0_), channel_id=1, source_target_pairs={{0,1},{1,0},{2,3},{3,2},{4,5},{5,4},{6,7},{7,6},{8,9},{9,8},{10,11... | collective-permute-start | bytes 12296 | tf_op jit(solution)/shard_map/ppermute | solution.py:505
  70.2 5.4 %collective-permute-start.20 = (f32[8,128]{1,0:T(8,128)S(1)}, f32[8,128]{1,0:T(8,128)S(1)}, u32[]{:S(2)}, u32[]{:S(2)}) collective-permute-start(f32[8,128]{1,0:T(8,128)S(1)} %fold.3.refs_0_), channel_id=1, source_target_pairs={{0,6},{1,7},{2,4},{3,5},{4,2},{5,3},{6,0},{7,1},{8,14},{9,15},{10,... | collective-permute-start | bytes 12296 | tf_op jit(solution)/shard_map/ppermute | solution.py:505
  72.7 4.5 %collective-permute-start.21 = (f32[8,128]{1,0:T(8,128)S(1)}, f32[8,128]{1,0:T(8,128)S(1)}, u32[]{:S(2)}, u32[]{:S(2)}) collective-permute-start(f32[8,128]{1,0:T(8,128)S(1)} %fold.3.refs_0_), channel_id=1, source_target_pairs={{0,4},{1,5},{2,6},{3,7},{4,0},{5,1},{6,2},{7,3},{8,12},{9,13},{10,... | collective-permute-start | bytes 12296 | tf_op jit(solution)/shard_map/ppermute | solution.py:505
  74.2 3.6 %collective-permute-start.22 = (f32[8,128]{1,0:T(8,128)S(1)}, f32[8,128]{1,0:T(8,128)S(1)}, u32[]{:S(2)}, u32[]{:S(2)}) collective-permute-start(f32[8,128]{1,0:T(8,128)S(1)} %fold.3.refs_0_), channel_id=1, source_target_pairs={{0,2},{1,3},{2,0},{3,1},{4,6},{5,7},{6,4},{7,5},{8,10},{9,11},{10,... | collective-permute-start | bytes 12296 | tf_op jit(solution)/shard_map/ppermute | solution.py:505

commit v5 on v4

--- a/solution.py
+++ b/solution.py
@@ -12,6 +12,7 @@
 F32 = jnp.float32
 BF16 = jnp.bfloat16
 TILE = 256
+CHUNKS = 16
 PANEL = 4
 VMEM_LIMIT = 24 * 1024 * 1024
 
@@ -47,27 +48,23 @@
 
 
 def moments_kernel(
-    _, x_hbm, m_hbm, w_hbm, s_hbm, out_ref, x_ref, m_ref, w_ref, lhs_ref, rhs_ref, sems
+    _, x_hbm, m_hbm, w_hbm, s_hbm, out_ref, x_ref, m_ref, w_ref, s_ref, sems
 ):
     rows, atoms = x_ref.shape
-    vectors = s_hbm.shape[0]
-    chunks = sems.shape[1] - 1
-    chunk = atoms // chunks
     n = rows + 8
+    spans = [(t * atoms // CHUNKS, (t + 1) * atoms // CHUNKS) for t in range(CHUNKS)]
     copies = [
         [
-            pltpu.make_async_copy(m_hbm, m_ref, sems.at[0, chunks]),
-            pltpu.make_async_copy(w_hbm, w_ref, sems.at[1, chunks]),
+            pltpu.make_async_copy(m_hbm, m_ref, sems.at[0, CHUNKS]),
+            pltpu.make_async_copy(w_hbm, w_ref, sems.at[1, CHUNKS]),
         ]
     ]
-    for t in range(chunks):
-        lanes = pl.ds(t * chunk, chunk)
+    for t, (begin, end) in enumerate(spans):
+        lanes = pl.ds(begin, end - begin)
         copies.append(
             [
                 pltpu.make_async_copy(x_hbm.at[:, lanes], x_ref.at[:, lanes], sems.at[0, t]),
-                pltpu.make_async_copy(
-                    s_hbm.at[:, lanes], rhs_ref.at[0:vectors, lanes], sems.at[1, t]
-                ),
+                pltpu.make_async_copy(s_hbm.at[:, lanes], s_ref.at[:, lanes], sems.at[1, t]),
             ]
         )
     for group in copies:
@@ -78,35 +75,29 @@
     row = lax.broadcasted_iota(jnp.int32, (8, TILE), 0)
     ones = jnp.where(row == 3, 1.0, 0.0)
     total = jnp.zeros(out_ref.shape, F32)
-    for t in range(chunks):
+    for t, (begin, end) in enumerate(spans):
         for copy in copies[t + 1]:
             copy.wait()
-        slot, half = t // 2 % 2, t % 2 * chunk
-        for start in range(0, chunk, TILE):
-            lanes = slice(t * chunk + start, t * chunk + start + TILE)
-            here = slice(half + start, half + start + TILE)
+        for start in range(begin, end, TILE):
+            lanes = slice(start, start + TILE)
             left = ones
             for i in range(3):
                 left = jnp.where(row == i, m_ref[i : i + 1, lanes], left)
             value = jnp.concatenate([x_ref[:, lanes], left], axis=0)
             high = value.astype(BF16)
-            lhs_ref[slot, 0:n, here] = high
-            lhs_ref[slot, n : 2 * n, here] = (value - high.astype(F32)).astype(BF16)
+            low = (value - high.astype(F32)).astype(BF16)
             pieces = [v.astype(F32) for v in split3(left * w_ref[:, lanes])]
             aux = jnp.concatenate(pieces + [jnp.zeros(left.shape, F32)], axis=0)
-            rhs_ref[vectors:, lanes] = aux.astype(BF16)
-        if t % 2 == 1:
-            sums = dot_nt(lhs_ref[slot], rhs_ref[:, (t - 1) * chunk : (t + 1) * chunk])
+            rhs = jnp.concatenate([s_ref[:, lanes], aux.astype(BF16)], axis=0)
+            sums = dot_nt(jnp.concatenate([high, low], axis=0), rhs)
             total = total + (sums[0:n] + sums[n : 2 * n])
     out_ref[...] = total
 
 
 def moments(where_, x, mean, weight, sub):
     rows, atoms = x.shape
-    vectors = sub.shape[0]
-    chunks = 16
-    chunk = atoms // chunks
     n = rows + 8
+    assert atoms % (CHUNKS * TILE) == 0
     return pl.pallas_call(
         moments_kernel,
         in_specs=[pl.BlockSpec(memory_space=pltpu.SMEM)] + [pl.BlockSpec(memory_space=pl.ANY)] * 4,
@@ -115,9 +106,8 @@
         scratch_shapes=[
             pltpu.VMEM(mean.shape, F32),
             pltpu.VMEM(weight.shape, F32),
-            pltpu.VMEM((2, 2 * n, 2 * chunk), BF16),
-            pltpu.VMEM((LANES, atoms), BF16),
-            pltpu.SemaphoreType.DMA((2, chunks + 1)),
+            pltpu.VMEM(sub.shape, BF16),
+            pltpu.SemaphoreType.DMA((2, CHUNKS + 1)),
         ],
         compiler_params=params(),
         name="moments",
@@ -540,10 +530,7 @@
         for q in range(PANEL):
             j = panel + q
             pivot = columns[q][j : j + 1, :]
-            inverse = pl.reciprocal(pivot, approx=True)
-            for _ in range(2):
-                inverse = inverse * (2.0 - pivot * inverse)
-            factor = columns[q] * inverse
+            factor = columns[q] * (1.0 / pivot)
             factor = jnp.where(row > j, factor, 0.0)
             for r in range(q + 1, PANEL):
                 columns[r] = columns[r] - factor * columns[r][j : j + 1, :]

time: 81.1 us -> 80.4 us (level)
  no operation moved by 1% of the time
where the time goes in v5:
time: 80.4 us; the launch traced here: 80.2 us
  starting transfers between devices  35.4 us (44%)
  waiting for transfers between devices  25.5 us (32%)
  Pallas kernels  18.5 us (23%)
  between operations  0.84 us (1%)
    ppermute x10, starting transfers between devices, exchanged(): lax.ppermute(value, axis, [(i, i ^ mask) for i in range(size)])  12.5 us
    ppermute x10, waiting for transfers between devices, exchanged(): lax.ppermute(value, axis, [(i, i ^ mask) for i in range(size)])  10.3 us
    ppermute x2, starting transfers between devices, along_four(): ends.append(lax.ppermute(out, 'frames', inward))  8.83 us
    ppermute x2, waiting for transfers between devices, along_four(): end = lax.ppermute(out, 'frames', inward + outward)  6.88 us
    pallas_call x1, Pallas kernels, moments(): pl.pallas_call(moments_kernel, in_specs=[pl.BlockSpec(memory_space=pltpu....  6.58 us
    ppermute x2, starting transfers between devices, along_four(): end = lax.ppermute(out, 'frames', inward + outward)  5.77 us
    ppermute x2, waiting for transfers between devices, along_four(): first = [lax.ppermute(make_first(p), 'frames', inward) for p in each]  5.47 us
    ppermute x2, starting transfers between devices, along_four(): first = [lax.ppermute(make_first(p), 'frames', inward) for p in each]  4.83 us
  transfers between devices with their start and end apart: 23, of which 17 were waited for; matrix products, arithmetic and copies ran while one was open for 0% of the time, Pallas kernels for 10%

profile of v5, /device:TPU:0, one launch (start us, length us, event | category | flops | bytes accessed | tf_op | source)
XLA Modules:
  0.0 80.2 jit_solution(3953002672619330611)
XLA Ops:
  0.6 6.6 %moments.1 = (f32[80,128]{1,0:T(8,128)S(1)}, f32[72,24576]{1,0:T(8,128)S(1)}) custom-call(s32[1]{0:T(128)} %bitcast._.idx, f32[72,24576]{1,0:T(8,128)} %bitcast.14, f32[3,24576]{1,0:T(4,128)} %refs_7_.1, f32[1,24576]{1,0:T(1,128)} %bitcast.16, bf16[96,24576]{1,0:T(8,128)(2,1)} %bitcast.15), custom_call_target="tpu_custom_call" | custom-call | tf_op jit(solution)/shard_map/moments/pallas_call | solution.py:101
  7.2 4.0 %collective-permute-start = (f32[80,128]{1,0:T(8,128)S(1)}, f32[80,128]{1,0:T(8,128)S(1)}, u32[]{:S(2)}, u32[]{:S(2)}) collective-permute-start(f32[80,128]{1,0:T(8,128)S(1)} %get-tuple-element.41.refs_0_), channel_id=1, source_target_pairs={{0,24},{8,16},{16,8},{24,0},{1,25},{9,17},{17,9},{25,1},{2,26},{10... | collective-permute-start | bytes 122888 | tf_op jit(solution)/shard_map/ppermute | solution.py:495
  11.2 0.5 collective-permute-start.1
  11.7 0.1 collective-permute-start.2
  11.8 1.3 %collective-permute-done.refs_1_ = f32[80,128]{1,0:T(8,128)S(1)} collective-permute-done((f32[80,128]{1,0:T(8,128)S(1)}, f32[80,128]{1,0:T(8,128)S(1)}, u32[]{:S(2)}, u32[]{:S(2)}) %collective-permute-start) | collective-permute-done | bytes 40992 | tf_op jit(solution)/shard_map/ppermute | solution.py:495
  13.2 2.0 %collective-permute-done.1.refs_2_ = f32[80,128]{1,0:T(8,128)S(1)} collective-permute-done((f32[80,128]{1,0:T(8,128)S(1)}, f32[80,128]{1,0:T(8,128)S(1)}, u32[]{:S(2)}, u32[]{:S(2)}) %collective-permute-start.1) | collective-permute-done | bytes 40992 | tf_op jit(solution)/shard_map/ppermute | solution.py:495
  15.2 0.5 collective-permute-done.2.refs_3_
  15.7 0.6 rotate.1
  16.3 0.3 displace.4
  16.6 0.1 collective-permute-start.4
  16.6 0.5 collective-permute-start.3
  17.1 0.3 displace.5.refs_3_
  17.4 0.9 %displace.7 = bf16[72,9216]{1,0:T(8,128)(2,1)S(1)} custom-call(s32[1]{0:T(128)} %bitcast._.idx, f32[72,24576]{1,0:T(8,128)S(1)} %get-tuple-element.46.x_ref, f32[3,24576]{1,0:T(4,128)S(1)} %copy-done, f32[288,128]{1,0:T(8,128)S(1)} %get-tuple-element.50.coef_ref), custom_call_target="tpu_custom_call" | custom-call | tf_op jit(solution)/shard_map/displace/pallas_call | solution.py:225
  18.3 0.1 collective-permute-done.3.other_ref
  18.4 0.0 collective-permute-done.4.refs_4_
  18.4 0.1 collective-permute-start.5
  18.6 0.2 weights.1
  18.7 0.4 term.11
  19.2 3.5 %collective-permute-start.6 = (bf16[96,1664]{1,0:T(8,128)(2,1)S(1)}, bf16[96,1664]{1,0:T(8,128)(2,1)S(1)}, u32[]{:S(2)}, u32[]{:S(2)}) collective-permute-start(bf16[96,1664]{1,0:T(8,128)(2,1)S(1)} %term.11), channel_id=1, source_target_pairs={{0,2},{1,3},{6,4},{7,5},{8,10},{9,11},{14,12},{15,13},{16,18},{17,... | collective-permute-start | bytes 958472 | tf_op jit(solution)/shard_map/ppermute | solution.py:602
  22.7 0.3 term.10
  23.0 1.3 %collective-permute-start.11 = (bf16[96,1536]{1,0:T(8,128)(2,1)S(1)}, bf16[96,1536]{1,0:T(8,128)(2,1)S(1)}, u32[]{:S(2)}, u32[]{:S(2)}) collective-permute-start(bf16[96,1536]{1,0:T(8,128)(2,1)S(1)} %term.10), channel_id=1, source_target_pairs={{0,2},{1,3},{6,4},{7,5},{8,10},{9,11},{14,12},{15,13},{16,18},{17,... | collective-permute-start | bytes 884744 | tf_op jit(solution)/shard_map/ppermute | solution.py:602
  24.3 0.9 %displace.6.refs_3_.refs_5_ = bf16[72,9216]{1,0:T(8,128)(2,1)S(1)} custom-call(s32[1]{0:T(128)} %bitcast._.idx, f32[72,24576]{1,0:T(8,128)S(1)} %get-tuple-element.46.x_ref, f32[3,24576]{1,0:T(4,128)S(1)} %copy-done, f32[288,128]{1,0:T(8,128)S(1)} %get-tuple-element.50.coef_ref), custom_call_target="tpu_custom_call" | custom-call | tf_op jit(solution)/shard_map/displace/pallas_call | solution.py:225
  25.2 5.3 %collective-permute-done.6.refs_5_ = bf16[96,1664]{1,0:T(8,128)(2,1)S(1)} collective-permute-done((bf16[96,1664]{1,0:T(8,128)(2,1)S(1)}, bf16[96,1664]{1,0:T(8,128)(2,1)S(1)}, u32[]{:S(2)}, u32[]{:S(2)}) %collective-permute-start.6) | collective-permute-done | bytes 319520 | tf_op jit(solution)/shard_map/ppermute | solution.py:602
  30.5 0.0 collective-permute-done.5.refs_4_.refs_6_
  30.5 0.4 term.12
  30.9 4.4 %collective-permute-start.7 = (bf16[96,1664]{1,0:T(8,128)(2,1)S(1)}, bf16[96,1664]{1,0:T(8,128)(2,1)S(1)}, u32[]{:S(2)}, u32[]{:S(2)}) collective-permute-start(bf16[96,1664]{1,0:T(8,128)(2,1)S(1)} %term.12), channel_id=1, source_target_pairs={{0,2},{1,3},{6,4},{7,5},{8,10},{9,11},{14,12},{15,13},{16,18},{17,... | collective-permute-start | bytes 958472 | tf_op jit(solution)/shard_map/ppermute | solution.py:606
  35.4 0.6 term.13
  36.0 0.7 collective-permute-start.8
  36.7 0.2 collective-permute-done.11.refs_6_
  36.8 0.3 term.16
  37.1 4.4 %collective-permute-start.12 = (bf16[96,1536]{1,0:T(8,128)(2,1)S(1)}, bf16[96,1536]{1,0:T(8,128)(2,1)S(1)}, u32[]{:S(2)}, u32[]{:S(2)}) collective-permute-start(bf16[96,1536]{1,0:T(8,128)(2,1)S(1)} %term.16), channel_id=1, source_target_pairs={{0,2},{1,3},{6,4},{7,5},{8,10},{9,11},{14,12},{15,13},{16,18},{17,... | collective-permute-start | bytes 884744 | tf_op jit(solution)/shard_map/ppermute | solution.py:606
  41.5 0.4 term.17
  42.0 0.7 collective-permute-start.13
  42.7 1.0 %collective-permute-done.7.refs_5_ = bf16[96,1664]{1,0:T(8,128)(2,1)S(1)} collective-permute-done((bf16[96,1664]{1,0:T(8,128)(2,1)S(1)}, bf16[96,1664]{1,0:T(8,128)(2,1)S(1)}, u32[]{:S(2)}, u32[]{:S(2)}) %collective-permute-start.7) | collective-permute-done | bytes 319520 | tf_op jit(solution)/shard_map/ppermute | solution.py:606
  43.7 0.0 collective-permute-done.8.refs_5_
  43.7 0.6 term.14
  44.3 2.8 %collective-permute-start.9 = (bf16[96,1664]{1,0:T(8,128)(2,1)S(1)}, bf16[96,1664]{1,0:T(8,128)(2,1)S(1)}, u32[]{:S(2)}, u32[]{:S(2)}) collective-permute-start(bf16[96,1664]{1,0:T(8,128)(2,1)S(1)} %term.14), channel_id=1, source_target_pairs={{0,2},{1,3},{6,4},{7,5},{4,6},{5,7},{2,0},{3,1},{8,10},{9,11},{14,... | collective-permute-start | bytes 958472 | tf_op jit(solution)/shard_map/ppermute | solution.py:612
  47.0 0.6 term.15
  47.6 0.7 collective-permute-start.10
  48.3 1.7 %collective-permute-done.12.refs_6_ = bf16[96,1536]{1,0:T(8,128)(2,1)S(1)} collective-permute-done((bf16[96,1536]{1,0:T(8,128)(2,1)S(1)}, bf16[96,1536]{1,0:T(8,128)(2,1)S(1)}, u32[]{:S(2)}, u32[]{:S(2)}) %collective-permute-start.12) | collective-permute-done | bytes 294944 | tf_op jit(solution)/shard_map/ppermute | solution.py:606
  50.0 0.0 collective-permute-done.13.refs_6_
  50.0 0.4 term.18
  50.5 3.0 %collective-permute-start.14 = (bf16[96,1536]{1,0:T(8,128)(2,1)S(1)}, bf16[96,1536]{1,0:T(8,128)(2,1)S(1)}, u32[]{:S(2)}, u32[]{:S(2)}) collective-permute-start(bf16[96,1536]{1,0:T(8,128)(2,1)S(1)} %term.18), channel_id=1, source_target_pairs={{0,2},{1,3},{6,4},{7,5},{4,6},{5,7},{2,0},{3,1},{8,10},{9,11},{14,... | collective-permute-start | bytes 884744 | tf_op jit(solution)/shard_map/ppermute | solution.py:612
  53.5 0.4 term.19
  53.9 0.7 collective-permute-start.15
  54.6 2.2 %collective-permute-done.9.refs_8_ = bf16[96,1664]{1,0:T(8,128)(2,1)S(1)} collective-permute-done((bf16[96,1664]{1,0:T(8,128)(2,1)S(1)}, bf16[96,1664]{1,0:T(8,128)(2,1)S(1)}, u32[]{:S(2)}, u32[]{:S(2)}) %collective-permute-start.9) | collective-permute-done | bytes 319520 | tf_op jit(solution)/shard_map/ppermute | solution.py:612
  56.9 1.1 %first_piece.1 = (f32[96,1536]{1,0:T(8,128)S(1)}, f32[8,128]{1,0:T(8,128)S(1)}, f32[3,3072]{1,0:T(4,128)}, f32[96,1536]{1,0:T(8,128)S(1)}) custom-call(s32[1]{0:T(128)} %bitcast._.idx, bf16[96,72]{1,0:T(8,128)(2,1)S(1)} %get-tuple-element.70.refs_0_, bf16[96,72]{1,0:T(8,128)(2,1)S(1)} %get-tuple-element.71.refs_1_, f32[8,128]{1,0:T(8,128)S(1)} %get-tuple-element.72.refs_2_, ...), custom_call_target="tpu_custom_call" | custom-call | flops 2000000000 | bytes 1 | tf_op jit(solution)/shard_map/first_piece/pallas_call | solution.py:435
  58.0 4.6 %collective-permute-done.14.refs_0_ = bf16[96,1536]{1,0:T(8,128)(2,1)S(1)} collective-permute-done((bf16[96,1536]{1,0:T(8,128)(2,1)S(1)}, bf16[96,1536]{1,0:T(8,128)(2,1)S(1)}, u32[]{:S(2)}, u32[]{:S(2)}) %collective-permute-start.14) | collective-permute-done | bytes 294944 | tf_op jit(solution)/shard_map/ppermute | solution.py:612
  62.6 0.0 collective-permute-done.15.refs_1_
  62.6 0.4 second_piece.1
  63.1 1.5 %collective-permute-start.16 = (f32[8,128]{1,0:T(8,128)S(1)}, f32[8,128]{1,0:T(8,128)S(1)}, u32[]{:S(2)}, u32[]{:S(2)}) collective-permute-start(f32[8,128]{1,0:T(8,128)S(1)} %get-tuple-element.73.refs_0_), channel_id=1, source_target_pairs={{0,24},{8,16},{16,8},{24,0},{1,25},{9,17},{17,9},{25,1},{2,26},{10... | collective-permute-start | bytes 12296 | tf_op jit(solution)/shard_map/ppermute | solution.py:495
  64.6 0.5 collective-permute-start.17
  65.1 1.5 %collective-permute-start.18 = (f32[8,128]{1,0:T(8,128)S(1)}, f32[8,128]{1,0:T(8,128)S(1)}, u32[]{:S(2)}, u32[]{:S(2)}) collective-permute-start(f32[8,128]{1,0:T(8,128)S(1)} %get-tuple-element.73.refs_0_), channel_id=1, source_target_pairs={{0,8},{8,0},{16,24},{24,16},{1,9},{9,1},{17,25},{25,17},{2,10},{10... | collective-permute-start | bytes 12296 | tf_op jit(solution)/shard_map/ppermute | solution.py:495
  66.6 1.0 %collective-permute-done.16.refs_1_ = f32[8,128]{1,0:T(8,128)S(1)} collective-permute-done((f32[8,128]{1,0:T(8,128)S(1)}, f32[8,128]{1,0:T(8,128)S(1)}, u32[]{:S(2)}, u32[]{:S(2)}) %collective-permute-start.16) | collective-permute-done | bytes 4128 | tf_op jit(solution)/shard_map/ppermute | solution.py:495
  67.6 0.6 collective-permute-done.17.refs_2_
  68.2 0.5 collective-permute-done.18.refs_3_
  68.7 1.2 %collective-permute-done.19.refs_1_ = f32[8,128]{1,0:T(8,128)S(1)} collective-permute-done((f32[8,128]{1,0:T(8,128)S(1)}, f32[8,128]{1,0:T(8,128)S(1)}, u32[]{:S(2)}, u32[]{:S(2)}) %collective-permute-start.19) | collective-permute-done | bytes 4128 | tf_op jit(solution)/shard_map/ppermute | solution.py:495
  69.9 2.5 %collective-permute-start.20 = (f32[8,128]{1,0:T(8,128)S(1)}, f32[8,128]{1,0:T(8,128)S(1)}, u32[]{:S(2)}, u32[]{:S(2)}) collective-permute-start(f32[8,128]{1,0:T(8,128)S(1)} %fold.3.refs_0_), channel_id=1, source_target_pairs={{0,6},{1,7},{2,4},{3,5},{4,2},{5,3},{6,0},{7,1},{8,14},{9,15},{10,... | collective-permute-start | bytes 12296 | tf_op jit(solution)/shard_map/ppermute | solution.py:495
  72.4 1.5 %collective-permute-start.21 = (f32[8,128]{1,0:T(8,128)S(1)}, f32[8,128]{1,0:T(8,128)S(1)}, u32[]{:S(2)}, u32[]{:S(2)}) collective-permute-start(f32[8,128]{1,0:T(8,128)S(1)} %fold.3.refs_0_), channel_id=1, source_target_pairs={{0,4},{1,5},{2,6},{3,7},{4,0},{5,1},{6,2},{7,3},{8,12},{9,13},{10,... | collective-permute-start | bytes 12296 | tf_op jit(solution)/shard_map/ppermute | solution.py:495
  73.9 0.4 collective-permute-start.22
  74.3 1.0 %collective-permute-done.20.refs_1_ = f32[8,128]{1,0:T(8,128)S(1)} collective-permute-done((f32[8,128]{1,0:T(8,128)S(1)}, f32[8,128]{1,0:T(8,128)S(1)}, u32[]{:S(2)}, u32[]{:S(2)}) %collective-permute-start.20) | collective-permute-done | bytes 4128 | tf_op jit(solution)/shard_map/ppermute | solution.py:495
  75.3 1.6 %collective-permute-done.21.refs_2_ = f32[8,128]{1,0:T(8,128)S(1)} collective-permute-done((f32[8,128]{1,0:T(8,128)S(1)}, f32[8,128]{1,0:T(8,128)S(1)}, u32[]{:S(2)}, u32[]{:S(2)}) %collective-permute-start.21) | collective-permute-done | bytes 4128 | tf_op jit(solution)/shard_map/ppermute | solution.py:495
  76.9 0.6 collective-permute-done.22.refs_3_
  77.5 2.7 %basis.1 = (f32[96,3072]{1,0:T(8,128)}, f32[96,3072]{1,0:T(8,128)}) custom-call(f32[8,128]{1,0:T(8,128)S(1)} %fold.3.refs_0_, f32[8,128]{1,0:T(8,128)S(1)} %collective-permute-done.20.refs_1_, f32[8,128]{1,0:T(8,128)S(1)} %collective-permute-done.21.refs_2_, f32[8,128]{1,0:T(8,128)S(1)} %collective-permute-done.22.refs_3_, ...), custom_call_target="tpu_custom_call" | custom-call | tf_op jit(solution)/shard_map/basis/pallas_call | solution.py:564
  (6 shorter events, 0.0 us)
Async XLA Ops:
  0.6 15.7 %copy-start = (f32[3,24576]{1,0:T(4,128)S(1)}, f32[3,24576]{1,0:T(4,128)}, u32[]{:S(2)}) copy-start(f32[3,24576]{1,0:T(4,128)} %refs_7_.1) | copy-start | bytes 884740
  7.2 5.9 %collective-permute-start = (f32[80,128]{1,0:T(8,128)S(1)}, f32[80,128]{1,0:T(8,128)S(1)}, u32[]{:S(2)}, u32[]{:S(2)}) collective-permute-start(f32[80,128]{1,0:T(8,128)S(1)} %get-tuple-element.41.refs_0_), channel_id=1, source_target_pairs={{0,24},{8,16},{16,8},{24,0},{1,25},{9,17},{17,9},{25,1},{2,26},{10... | collective-permute-start | bytes 122888 | tf_op jit(solution)/shard_map/ppermute | solution.py:495
  11.2 4.0 %collective-permute-start.1 = (f32[80,128]{1,0:T(8,128)S(1)}, f32[80,128]{1,0:T(8,128)S(1)}, u32[]{:S(2)}, u32[]{:S(2)}) collective-permute-start(f32[80,128]{1,0:T(8,128)S(1)} %get-tuple-element.41.refs_0_), channel_id=1, source_target_pairs={{0,16},{8,24},{16,0},{24,8},{1,17},{9,25},{17,1},{25,9},{2,18},{10... | collective-permute-start | bytes 122888 | tf_op jit(solution)/shard_map/ppermute | solution.py:495
  11.7 4.0 %collective-permute-start.2 = (f32[80,128]{1,0:T(8,128)S(1)}, f32[80,128]{1,0:T(8,128)S(1)}, u32[]{:S(2)}, u32[]{:S(2)}) collective-permute-start(f32[80,128]{1,0:T(8,128)S(1)} %get-tuple-element.41.refs_0_), channel_id=1, source_target_pairs={{0,8},{8,0},{16,24},{24,16},{1,9},{9,1},{17,25},{25,17},{2,10},{10... | collective-permute-start | bytes 122888 | tf_op jit(solution)/shard_map/ppermute | solution.py:495
  16.6 1.9 %collective-permute-start.4 = (bf16[72,3072]{1,0:T(8,128)(2,1)S(1)}, bf16[72,3072]{1,0:T(8,128)(2,1)S(1)}, u32[]{:S(2)}, u32[]{:S(2)}) collective-permute-start(bf16[72,3072]{1,0:T(8,128)(2,1)S(1)} %displace.4), channel_id=1, source_target_pairs={{0,1},{1,0},{2,3},{3,2},{4,5},{5,4},{6,7},{7,6},{8,9},{9,8},{10,11... | collective-permute-start | bytes 1327112 | tf_op jit(solution)/shard_map/ppermute | solution.py:671
  16.6 1.8 %collective-permute-start.3 = (f32[24,128]{1,0:T(8,128)S(1)}, f32[24,128]{1,0:T(8,128)S(1)}, u32[]{:S(2)}, u32[]{:S(2)}) collective-permute-start(f32[24,128]{1,0:T(8,128)S(1)} %get-tuple-element.42.own_ref), channel_id=1, source_target_pairs={{0,1},{1,0},{2,3},{3,2},{4,5},{5,4},{6,7},{7,6},{8,9},{9,8},{10,11... | collective-permute-start | bytes 36872 | tf_op jit(solution)/shard_map/ppermute | solution.py:663
  18.4 12.1 %collective-permute-start.5 = (bf16[72,9216]{1,0:T(8,128)(2,1)S(1)}, bf16[72,9216]{1,0:T(8,128)(2,1)S(1)}, u32[]{:S(2)}, u32[]{:S(2)}) collective-permute-start(bf16[72,9216]{1,0:T(8,128)(2,1)S(1)} %displace.7), channel_id=1, source_target_pairs={{0,1},{1,0},{2,3},{3,2},{4,5},{5,4},{6,7},{7,6},{8,9},{9,8},{10,11... | collective-permute-start | bytes 3981320 | tf_op jit(solution)/shard_map/ppermute | solution.py:674
  19.2 11.4 %collective-permute-start.6 = (bf16[96,1664]{1,0:T(8,128)(2,1)S(1)}, bf16[96,1664]{1,0:T(8,128)(2,1)S(1)}, u32[]{:S(2)}, u32[]{:S(2)}) collective-permute-start(bf16[96,1664]{1,0:T(8,128)(2,1)S(1)} %term.11), channel_id=1, source_target_pairs={{0,2},{1,3},{6,4},{7,5},{8,10},{9,11},{14,12},{15,13},{16,18},{17,... | collective-permute-start | bytes 958472 | tf_op jit(solution)/shard_map/ppermute | solution.py:602
  23.0 13.9 %collective-permute-start.11 = (bf16[96,1536]{1,0:T(8,128)(2,1)S(1)}, bf16[96,1536]{1,0:T(8,128)(2,1)S(1)}, u32[]{:S(2)}, u32[]{:S(2)}) collective-permute-start(bf16[96,1536]{1,0:T(8,128)(2,1)S(1)} %term.10), channel_id=1, source_target_pairs={{0,2},{1,3},{6,4},{7,5},{8,10},{9,11},{14,12},{15,13},{16,18},{17,... | collective-permute-start | bytes 884744 | tf_op jit(solution)/shard_map/ppermute | solution.py:602
  30.9 12.8 %collective-permute-start.7 = (bf16[96,1664]{1,0:T(8,128)(2,1)S(1)}, bf16[96,1664]{1,0:T(8,128)(2,1)S(1)}, u32[]{:S(2)}, u32[]{:S(2)}) collective-permute-start(bf16[96,1664]{1,0:T(8,128)(2,1)S(1)} %term.12), channel_id=1, source_target_pairs={{0,2},{1,3},{6,4},{7,5},{8,10},{9,11},{14,12},{15,13},{16,18},{17,... | collective-permute-start | bytes 958472 | tf_op jit(solution)/shard_map/ppermute | solution.py:606
  36.0 7.7 %collective-permute-start.8 = (bf16[96,1664]{1,0:T(8,128)(2,1)S(1)}, bf16[96,1664]{1,0:T(8,128)(2,1)S(1)}, u32[]{:S(2)}, u32[]{:S(2)}) collective-permute-start(bf16[96,1664]{1,0:T(8,128)(2,1)S(1)} %term.13), channel_id=1, source_target_pairs={{2,4},{3,5},{4,2},{5,3},{10,12},{11,13},{12,10},{13,11},{18,20},{1... | collective-permute-start | bytes 958472 | tf_op jit(solution)/shard_map/ppermute | solution.py:608
  37.1 12.9 %collective-permute-start.12 = (bf16[96,1536]{1,0:T(8,128)(2,1)S(1)}, bf16[96,1536]{1,0:T(8,128)(2,1)S(1)}, u32[]{:S(2)}, u32[]{:S(2)}) collective-permute-start(bf16[96,1536]{1,0:T(8,128)(2,1)S(1)} %term.16), channel_id=1, source_target_pairs={{0,2},{1,3},{6,4},{7,5},{8,10},{9,11},{14,12},{15,13},{16,18},{17,... | collective-permute-start | bytes 884744 | tf_op jit(solution)/shard_map/ppermute | solution.py:606
  42.0 8.0 %collective-permute-start.13 = (bf16[96,1536]{1,0:T(8,128)(2,1)S(1)}, bf16[96,1536]{1,0:T(8,128)(2,1)S(1)}, u32[]{:S(2)}, u32[]{:S(2)}) collective-permute-start(bf16[96,1536]{1,0:T(8,128)(2,1)S(1)} %term.17), channel_id=1, source_target_pairs={{2,4},{3,5},{4,2},{5,3},{10,12},{11,13},{12,10},{13,11},{18,20},{1... | collective-permute-start | bytes 884744 | tf_op jit(solution)/shard_map/ppermute | solution.py:608
  44.3 12.6 %collective-permute-start.9 = (bf16[96,1664]{1,0:T(8,128)(2,1)S(1)}, bf16[96,1664]{1,0:T(8,128)(2,1)S(1)}, u32[]{:S(2)}, u32[]{:S(2)}) collective-permute-start(bf16[96,1664]{1,0:T(8,128)(2,1)S(1)} %term.14), channel_id=1, source_target_pairs={{0,2},{1,3},{6,4},{7,5},{4,6},{5,7},{2,0},{3,1},{8,10},{9,11},{14,... | collective-permute-start | bytes 958472 | tf_op jit(solution)/shard_map/ppermute | solution.py:612
  47.6 9.2 %collective-permute-start.10 = (bf16[96,1664]{1,0:T(8,128)(2,1)S(1)}, bf16[96,1664]{1,0:T(8,128)(2,1)S(1)}, u32[]{:S(2)}, u32[]{:S(2)}) collective-permute-start(bf16[96,1664]{1,0:T(8,128)(2,1)S(1)} %term.15), channel_id=1, source_target_pairs={{2,4},{3,5},{4,2},{5,3},{10,12},{11,13},{12,10},{13,11},{18,20},{1... | collective-permute-start | bytes 958472 | tf_op jit(solution)/shard_map/ppermute | solution.py:614
  50.5 12.2 %collective-permute-start.14 = (bf16[96,1536]{1,0:T(8,128)(2,1)S(1)}, bf16[96,1536]{1,0:T(8,128)(2,1)S(1)}, u32[]{:S(2)}, u32[]{:S(2)}) collective-permute-start(bf16[96,1536]{1,0:T(8,128)(2,1)S(1)} %term.18), channel_id=1, source_target_pairs={{0,2},{1,3},{6,4},{7,5},{4,6},{5,7},{2,0},{3,1},{8,10},{9,11},{14,... | collective-permute-start | bytes 884744 | tf_op jit(solution)/shard_map/ppermute | solution.py:612
  53.9 8.7 %collective-permute-start.15 = (bf16[96,1536]{1,0:T(8,128)(2,1)S(1)}, bf16[96,1536]{1,0:T(8,128)(2,1)S(1)}, u32[]{:S(2)}, u32[]{:S(2)}) collective-permute-start(bf16[96,1536]{1,0:T(8,128)(2,1)S(1)} %term.19), channel_id=1, source_target_pairs={{2,4},{3,5},{4,2},{5,3},{10,12},{11,13},{12,10},{13,11},{18,20},{1... | collective-permute-start | bytes 884744 | tf_op jit(solution)/shard_map/ppermute | solution.py:614
  63.1 4.5 %collective-permute-start.16 = (f32[8,128]{1,0:T(8,128)S(1)}, f32[8,128]{1,0:T(8,128)S(1)}, u32[]{:S(2)}, u32[]{:S(2)}) collective-permute-start(f32[8,128]{1,0:T(8,128)S(1)} %get-tuple-element.73.refs_0_), channel_id=1, source_target_pairs={{0,24},{8,16},{16,8},{24,0},{1,25},{9,17},{17,9},{25,1},{2,26},{10... | collective-permute-start | bytes 12296 | tf_op jit(solution)/shard_map/ppermute | solution.py:495
  64.6 3.6 %collective-permute-start.17 = (f32[8,128]{1,0:T(8,128)S(1)}, f32[8,128]{1,0:T(8,128)S(1)}, u32[]{:S(2)}, u32[]{:S(2)}) collective-permute-start(f32[8,128]{1,0:T(8,128)S(1)} %get-tuple-element.73.refs_0_), channel_id=1, source_target_pairs={{0,16},{8,24},{16,0},{24,8},{1,17},{9,25},{17,1},{25,9},{2,18},{10... | collective-permute-start | bytes 12296 | tf_op jit(solution)/shard_map/ppermute | solution.py:495
  65.1 3.6 %collective-permute-start.18 = (f32[8,128]{1,0:T(8,128)S(1)}, f32[8,128]{1,0:T(8,128)S(1)}, u32[]{:S(2)}, u32[]{:S(2)}) collective-permute-start(f32[8,128]{1,0:T(8,128)S(1)} %get-tuple-element.73.refs_0_), channel_id=1, source_target_pairs={{0,8},{8,0},{16,24},{24,16},{1,9},{9,1},{17,25},{25,17},{2,10},{10... | collective-permute-start | bytes 12296 | tf_op jit(solution)/shard_map/ppermute | solution.py:495
  68.7 1.2 %collective-permute-start.19 = (f32[8,128]{1,0:T(8,128)S(1)}, f32[8,128]{1,0:T(8,128)S(1)}, u32[]{:S(2)}, u32[]{:S(2)}) collective-permute-start(f32[8,128]{1,0:T(8,128)S(1)} %fold.2.refs_0_), channel_id=1, source_target_pairs={{0,1},{1,0},{2,3},{3,2},{4,5},{5,4},{6,7},{7,6},{8,9},{9,8},{10,11... | collective-permute-start | bytes 12296 | tf_op jit(solution)/shard_map/ppermute | solution.py:495
  69.9 5.4 %collective-permute-start.20 = (f32[8,128]{1,0:T(8,128)S(1)}, f32[8,128]{1,0:T(8,128)S(1)}, u32[]{:S(2)}, u32[]{:S(2)}) collective-permute-start(f32[8,128]{1,0:T(8,128)S(1)} %fold.3.refs_0_), channel_id=1, source_target_pairs={{0,6},{1,7},{2,4},{3,5},{4,2},{5,3},{6,0},{7,1},{8,14},{9,15},{10,... | collective-permute-start | bytes 12296 | tf_op jit(solution)/shard_map/ppermute | solution.py:495
  72.4 4.5 %collective-permute-start.21 = (f32[8,128]{1,0:T(8,128)S(1)}, f32[8,128]{1,0:T(8,128)S(1)}, u32[]{:S(2)}, u32[]{:S(2)}) collective-permute-start(f32[8,128]{1,0:T(8,128)S(1)} %fold.3.refs_0_), channel_id=1, source_target_pairs={{0,4},{1,5},{2,6},{3,7},{4,0},{5,1},{6,2},{7,3},{8,12},{9,13},{10,... | collective-permute-start | bytes 12296 | tf_op jit(solution)/shard_map/ppermute | solution.py:495
  73.9 3.6 %collective-permute-start.22 = (f32[8,128]{1,0:T(8,128)S(1)}, f32[8,128]{1,0:T(8,128)S(1)}, u32[]{:S(2)}, u32[]{:S(2)}) collective-permute-start(f32[8,128]{1,0:T(8,128)S(1)} %fold.3.refs_0_), channel_id=1, source_target_pairs={{0,2},{1,3},{2,0},{3,1},{4,6},{5,7},{6,4},{7,5},{8,10},{9,11},{10,... | collective-permute-start | bytes 12296 | tf_op jit(solution)/shard_map/ppermute | solution.py:495

commit v6 on v5

--- a/solution.py
+++ b/solution.py
@@ -12,7 +12,7 @@
 F32 = jnp.float32
 BF16 = jnp.bfloat16
 TILE = 256
-CHUNKS = 16
+CHUNKS = 12
 PANEL = 4
 VMEM_LIMIT = 24 * 1024 * 1024
 

time: 80.4 us -> 80.3 us (level)
  no operation moved by 1% of the time
where the time goes in v6:
time: 80.3 us; the launch traced here: 80 us
  starting transfers between devices  35.3 us (44%)
  waiting for transfers between devices  25.5 us (32%)
  Pallas kernels  18.4 us (23%)
  between operations  0.84 us (1%)
    ppermute x10, starting transfers between devices, exchanged(): lax.ppermute(value, axis, [(i, i ^ mask) for i in range(size)])  12.5 us
    ppermute x10, waiting for transfers between devices, exchanged(): lax.ppermute(value, axis, [(i, i ^ mask) for i in range(size)])  10.4 us
    ppermute x2, starting transfers between devices, along_four(): ends.append(lax.ppermute(out, 'frames', inward))  8.8 us
    ppermute x2, waiting for transfers between devices, along_four(): end = lax.ppermute(out, 'frames', inward + outward)  6.9 us
    pallas_call x1, Pallas kernels, moments(): pl.pallas_call(moments_kernel, in_specs=[pl.BlockSpec(memory_space=pltpu....  6.42 us
    ppermute x2, starting transfers between devices, along_four(): end = lax.ppermute(out, 'frames', inward + outward)  5.75 us
    ppermute x2, waiting for transfers between devices, along_four(): first = [lax.ppermute(make_first(p), 'frames', inward) for p in each]  5.47 us
    ppermute x2, starting transfers between devices, along_four(): first = [lax.ppermute(make_first(p), 'frames', inward) for p in each]  4.83 us
  transfers between devices with their start and end apart: 23, of which 17 were waited for; matrix products, arithmetic and copies ran while one was open for 0% of the time, Pallas kernels for 10%

profile of v6, /device:TPU:0, one launch (start us, length us, event | category | flops | bytes accessed | tf_op | source)
XLA Modules:
  0.0 80.0 jit_solution(18124590103094925169)
XLA Ops:
  0.6 6.4 %moments.1 = (f32[80,128]{1,0:T(8,128)S(1)}, f32[72,24576]{1,0:T(8,128)S(1)}) custom-call(s32[1]{0:T(128)} %bitcast._.idx, f32[72,24576]{1,0:T(8,128)} %bitcast.14, f32[3,24576]{1,0:T(4,128)} %refs_7_.1, f32[1,24576]{1,0:T(1,128)} %bitcast.16, bf16[96,24576]{1,0:T(8,128)(2,1)} %bitcast.15), custom_call_target="tpu_custom_call" | custom-call | tf_op jit(solution)/shard_map/moments/pallas_call | solution.py:101
  7.1 4.0 %collective-permute-start = (f32[80,128]{1,0:T(8,128)S(1)}, f32[80,128]{1,0:T(8,128)S(1)}, u32[]{:S(2)}, u32[]{:S(2)}) collective-permute-start(f32[80,128]{1,0:T(8,128)S(1)} %get-tuple-element.41.refs_0_), channel_id=1, source_target_pairs={{0,24},{8,16},{16,8},{24,0},{1,25},{9,17},{17,9},{25,1},{2,26},{10... | collective-permute-start | bytes 122888 | tf_op jit(solution)/shard_map/ppermute | solution.py:495
  11.0 0.5 collective-permute-start.1
  11.5 0.1 collective-permute-start.2
  11.7 1.3 %collective-permute-done.refs_1_ = f32[80,128]{1,0:T(8,128)S(1)} collective-permute-done((f32[80,128]{1,0:T(8,128)S(1)}, f32[80,128]{1,0:T(8,128)S(1)}, u32[]{:S(2)}, u32[]{:S(2)}) %collective-permute-start) | collective-permute-done | bytes 40992 | tf_op jit(solution)/shard_map/ppermute | solution.py:495
  13.0 2.0 %collective-permute-done.1.refs_2_ = f32[80,128]{1,0:T(8,128)S(1)} collective-permute-done((f32[80,128]{1,0:T(8,128)S(1)}, f32[80,128]{1,0:T(8,128)S(1)}, u32[]{:S(2)}, u32[]{:S(2)}) %collective-permute-start.1) | collective-permute-done | bytes 40992 | tf_op jit(solution)/shard_map/ppermute | solution.py:495
  15.0 0.5 collective-permute-done.2.refs_3_
  15.5 0.6 rotate.1
  16.1 0.3 displace.4
  16.4 0.1 collective-permute-start.4
  16.5 0.5 collective-permute-start.3
  17.0 0.3 displace.5.refs_3_
  17.2 0.9 %displace.7 = bf16[72,9216]{1,0:T(8,128)(2,1)S(1)} custom-call(s32[1]{0:T(128)} %bitcast._.idx, f32[72,24576]{1,0:T(8,128)S(1)} %get-tuple-element.46.x_ref, f32[3,24576]{1,0:T(4,128)S(1)} %copy-done, f32[288,128]{1,0:T(8,128)S(1)} %get-tuple-element.50.coef_ref), custom_call_target="tpu_custom_call" | custom-call | tf_op jit(solution)/shard_map/displace/pallas_call | solution.py:225
  18.2 0.1 collective-permute-done.3.other_ref
  18.3 0.0 collective-permute-done.4.refs_4_
  18.3 0.1 collective-permute-start.5
  18.4 0.2 weights.1
  18.6 0.4 term.11
  19.0 3.5 %collective-permute-start.6 = (bf16[96,1664]{1,0:T(8,128)(2,1)S(1)}, bf16[96,1664]{1,0:T(8,128)(2,1)S(1)}, u32[]{:S(2)}, u32[]{:S(2)}) collective-permute-start(bf16[96,1664]{1,0:T(8,128)(2,1)S(1)} %term.11), channel_id=1, source_target_pairs={{0,2},{1,3},{6,4},{7,5},{8,10},{9,11},{14,12},{15,13},{16,18},{17,... | collective-permute-start | bytes 958472 | tf_op jit(solution)/shard_map/ppermute | solution.py:602
  22.5 0.3 term.10
  22.8 1.3 %collective-permute-start.11 = (bf16[96,1536]{1,0:T(8,128)(2,1)S(1)}, bf16[96,1536]{1,0:T(8,128)(2,1)S(1)}, u32[]{:S(2)}, u32[]{:S(2)}) collective-permute-start(bf16[96,1536]{1,0:T(8,128)(2,1)S(1)} %term.10), channel_id=1, source_target_pairs={{0,2},{1,3},{6,4},{7,5},{8,10},{9,11},{14,12},{15,13},{16,18},{17,... | collective-permute-start | bytes 884744 | tf_op jit(solution)/shard_map/ppermute | solution.py:602
  24.1 0.9 %displace.6.refs_3_.refs_5_ = bf16[72,9216]{1,0:T(8,128)(2,1)S(1)} custom-call(s32[1]{0:T(128)} %bitcast._.idx, f32[72,24576]{1,0:T(8,128)S(1)} %get-tuple-element.46.x_ref, f32[3,24576]{1,0:T(4,128)S(1)} %copy-done, f32[288,128]{1,0:T(8,128)S(1)} %get-tuple-element.50.coef_ref), custom_call_target="tpu_custom_call" | custom-call | tf_op jit(solution)/shard_map/displace/pallas_call | solution.py:225
  25.1 5.3 %collective-permute-done.6.refs_5_ = bf16[96,1664]{1,0:T(8,128)(2,1)S(1)} collective-permute-done((bf16[96,1664]{1,0:T(8,128)(2,1)S(1)}, bf16[96,1664]{1,0:T(8,128)(2,1)S(1)}, u32[]{:S(2)}, u32[]{:S(2)}) %collective-permute-start.6) | collective-permute-done | bytes 319520 | tf_op jit(solution)/shard_map/ppermute | solution.py:602
  30.4 0.4 term.12
  30.8 4.4 %collective-permute-start.7 = (bf16[96,1664]{1,0:T(8,128)(2,1)S(1)}, bf16[96,1664]{1,0:T(8,128)(2,1)S(1)}, u32[]{:S(2)}, u32[]{:S(2)}) collective-permute-start(bf16[96,1664]{1,0:T(8,128)(2,1)S(1)} %term.12), channel_id=1, source_target_pairs={{0,2},{1,3},{6,4},{7,5},{8,10},{9,11},{14,12},{15,13},{16,18},{17,... | collective-permute-start | bytes 958472 | tf_op jit(solution)/shard_map/ppermute | solution.py:606
  35.2 0.6 term.13
  35.8 0.7 collective-permute-start.8
  36.5 0.2 collective-permute-done.11.refs_6_
  36.7 0.3 term.16
  37.0 4.4 %collective-permute-start.12 = (bf16[96,1536]{1,0:T(8,128)(2,1)S(1)}, bf16[96,1536]{1,0:T(8,128)(2,1)S(1)}, u32[]{:S(2)}, u32[]{:S(2)}) collective-permute-start(bf16[96,1536]{1,0:T(8,128)(2,1)S(1)} %term.16), channel_id=1, source_target_pairs={{0,2},{1,3},{6,4},{7,5},{8,10},{9,11},{14,12},{15,13},{16,18},{17,... | collective-permute-start | bytes 884744 | tf_op jit(solution)/shard_map/ppermute | solution.py:606
  41.4 0.5 term.17
  41.9 0.7 collective-permute-start.13
  42.5 1.0 %collective-permute-done.7.refs_5_ = bf16[96,1664]{1,0:T(8,128)(2,1)S(1)} collective-permute-done((bf16[96,1664]{1,0:T(8,128)(2,1)S(1)}, bf16[96,1664]{1,0:T(8,128)(2,1)S(1)}, u32[]{:S(2)}, u32[]{:S(2)}) %collective-permute-start.7) | collective-permute-done | bytes 319520 | tf_op jit(solution)/shard_map/ppermute | solution.py:606
  43.5 0.0 collective-permute-done.8.refs_5_
  43.5 0.6 term.14
  44.1 2.8 %collective-permute-start.9 = (bf16[96,1664]{1,0:T(8,128)(2,1)S(1)}, bf16[96,1664]{1,0:T(8,128)(2,1)S(1)}, u32[]{:S(2)}, u32[]{:S(2)}) collective-permute-start(bf16[96,1664]{1,0:T(8,128)(2,1)S(1)} %term.14), channel_id=1, source_target_pairs={{0,2},{1,3},{6,4},{7,5},{4,6},{5,7},{2,0},{3,1},{8,10},{9,11},{14,... | collective-permute-start | bytes 958472 | tf_op jit(solution)/shard_map/ppermute | solution.py:612
  46.9 0.6 term.15
  47.5 0.7 collective-permute-start.10
  48.2 1.7 %collective-permute-done.12.refs_6_ = bf16[96,1536]{1,0:T(8,128)(2,1)S(1)} collective-permute-done((bf16[96,1536]{1,0:T(8,128)(2,1)S(1)}, bf16[96,1536]{1,0:T(8,128)(2,1)S(1)}, u32[]{:S(2)}, u32[]{:S(2)}) %collective-permute-start.12) | collective-permute-done | bytes 294944 | tf_op jit(solution)/shard_map/ppermute | solution.py:606
  49.8 0.0 collective-permute-done.13.refs_6_
  49.9 0.4 term.18
  50.3 3.0 %collective-permute-start.14 = (bf16[96,1536]{1,0:T(8,128)(2,1)S(1)}, bf16[96,1536]{1,0:T(8,128)(2,1)S(1)}, u32[]{:S(2)}, u32[]{:S(2)}) collective-permute-start(bf16[96,1536]{1,0:T(8,128)(2,1)S(1)} %term.18), channel_id=1, source_target_pairs={{0,2},{1,3},{6,4},{7,5},{4,6},{5,7},{2,0},{3,1},{8,10},{9,11},{14,... | collective-permute-start | bytes 884744 | tf_op jit(solution)/shard_map/ppermute | solution.py:612
  53.3 0.4 term.19
  53.7 0.7 collective-permute-start.15
  54.4 2.3 %collective-permute-done.9.refs_8_ = bf16[96,1664]{1,0:T(8,128)(2,1)S(1)} collective-permute-done((bf16[96,1664]{1,0:T(8,128)(2,1)S(1)}, bf16[96,1664]{1,0:T(8,128)(2,1)S(1)}, u32[]{:S(2)}, u32[]{:S(2)}) %collective-permute-start.9) | collective-permute-done | bytes 319520 | tf_op jit(solution)/shard_map/ppermute | solution.py:612
  56.7 0.0 collective-permute-done.10.refs_9_
  56.7 1.1 %first_piece.1 = (f32[96,1536]{1,0:T(8,128)S(1)}, f32[8,128]{1,0:T(8,128)S(1)}, f32[3,3072]{1,0:T(4,128)}, f32[96,1536]{1,0:T(8,128)S(1)}) custom-call(s32[1]{0:T(128)} %bitcast._.idx, bf16[96,72]{1,0:T(8,128)(2,1)S(1)} %get-tuple-element.70.refs_0_, bf16[96,72]{1,0:T(8,128)(2,1)S(1)} %get-tuple-element.71.refs_1_, f32[8,128]{1,0:T(8,128)S(1)} %get-tuple-element.72.refs_2_, ...), custom_call_target="tpu_custom_call" | custom-call | flops 2000000000 | bytes 1 | tf_op jit(solution)/shard_map/first_piece/pallas_call | solution.py:435
  57.8 4.6 %collective-permute-done.14.refs_0_ = bf16[96,1536]{1,0:T(8,128)(2,1)S(1)} collective-permute-done((bf16[96,1536]{1,0:T(8,128)(2,1)S(1)}, bf16[96,1536]{1,0:T(8,128)(2,1)S(1)}, u32[]{:S(2)}, u32[]{:S(2)}) %collective-permute-start.14) | collective-permute-done | bytes 294944 | tf_op jit(solution)/shard_map/ppermute | solution.py:612
  62.5 0.4 second_piece.1
  62.9 1.5 %collective-permute-start.16 = (f32[8,128]{1,0:T(8,128)S(1)}, f32[8,128]{1,0:T(8,128)S(1)}, u32[]{:S(2)}, u32[]{:S(2)}) collective-permute-start(f32[8,128]{1,0:T(8,128)S(1)} %get-tuple-element.73.refs_0_), channel_id=1, source_target_pairs={{0,24},{8,16},{16,8},{24,0},{1,25},{9,17},{17,9},{25,1},{2,26},{10... | collective-permute-start | bytes 12296 | tf_op jit(solution)/shard_map/ppermute | solution.py:495
  64.4 0.5 collective-permute-start.17
  64.9 1.5 %collective-permute-start.18 = (f32[8,128]{1,0:T(8,128)S(1)}, f32[8,128]{1,0:T(8,128)S(1)}, u32[]{:S(2)}, u32[]{:S(2)}) collective-permute-start(f32[8,128]{1,0:T(8,128)S(1)} %get-tuple-element.73.refs_0_), channel_id=1, source_target_pairs={{0,8},{8,0},{16,24},{24,16},{1,9},{9,1},{17,25},{25,17},{2,10},{10... | collective-permute-start | bytes 12296 | tf_op jit(solution)/shard_map/ppermute | solution.py:495
  66.4 1.0 %collective-permute-done.16.refs_1_ = f32[8,128]{1,0:T(8,128)S(1)} collective-permute-done((f32[8,128]{1,0:T(8,128)S(1)}, f32[8,128]{1,0:T(8,128)S(1)}, u32[]{:S(2)}, u32[]{:S(2)}) %collective-permute-start.16) | collective-permute-done | bytes 4128 | tf_op jit(solution)/shard_map/ppermute | solution.py:495
  67.4 0.6 collective-permute-done.17.refs_2_
  68.0 0.5 collective-permute-done.18.refs_3_
  68.5 0.0 collective-permute-start.19
  68.6 1.2 %collective-permute-done.19.refs_1_ = f32[8,128]{1,0:T(8,128)S(1)} collective-permute-done((f32[8,128]{1,0:T(8,128)S(1)}, f32[8,128]{1,0:T(8,128)S(1)}, u32[]{:S(2)}, u32[]{:S(2)}) %collective-permute-start.19) | collective-permute-done | bytes 4128 | tf_op jit(solution)/shard_map/ppermute | solution.py:495
  69.7 2.5 %collective-permute-start.20 = (f32[8,128]{1,0:T(8,128)S(1)}, f32[8,128]{1,0:T(8,128)S(1)}, u32[]{:S(2)}, u32[]{:S(2)}) collective-permute-start(f32[8,128]{1,0:T(8,128)S(1)} %fold.3.refs_0_), channel_id=1, source_target_pairs={{0,6},{1,7},{2,4},{3,5},{4,2},{5,3},{6,0},{7,1},{8,14},{9,15},{10,... | collective-permute-start | bytes 12296 | tf_op jit(solution)/shard_map/ppermute | solution.py:495
  72.2 1.5 %collective-permute-start.21 = (f32[8,128]{1,0:T(8,128)S(1)}, f32[8,128]{1,0:T(8,128)S(1)}, u32[]{:S(2)}, u32[]{:S(2)}) collective-permute-start(f32[8,128]{1,0:T(8,128)S(1)} %fold.3.refs_0_), channel_id=1, source_target_pairs={{0,4},{1,5},{2,6},{3,7},{4,0},{5,1},{6,2},{7,3},{8,12},{9,13},{10,... | collective-permute-start | bytes 12296 | tf_op jit(solution)/shard_map/ppermute | solution.py:495
  73.7 0.4 collective-permute-start.22
  74.1 1.0 %collective-permute-done.20.refs_1_ = f32[8,128]{1,0:T(8,128)S(1)} collective-permute-done((f32[8,128]{1,0:T(8,128)S(1)}, f32[8,128]{1,0:T(8,128)S(1)}, u32[]{:S(2)}, u32[]{:S(2)}) %collective-permute-start.20) | collective-permute-done | bytes 4128 | tf_op jit(solution)/shard_map/ppermute | solution.py:495
  75.1 1.6 %collective-permute-done.21.refs_2_ = f32[8,128]{1,0:T(8,128)S(1)} collective-permute-done((f32[8,128]{1,0:T(8,128)S(1)}, f32[8,128]{1,0:T(8,128)S(1)}, u32[]{:S(2)}, u32[]{:S(2)}) %collective-permute-start.21) | collective-permute-done | bytes 4128 | tf_op jit(solution)/shard_map/ppermute | solution.py:495
  76.7 0.6 collective-permute-done.22.refs_3_
  77.3 2.7 %basis.1 = (f32[96,3072]{1,0:T(8,128)}, f32[96,3072]{1,0:T(8,128)}) custom-call(f32[8,128]{1,0:T(8,128)S(1)} %fold.3.refs_0_, f32[8,128]{1,0:T(8,128)S(1)} %collective-permute-done.20.refs_1_, f32[8,128]{1,0:T(8,128)S(1)} %collective-permute-done.21.refs_2_, f32[8,128]{1,0:T(8,128)S(1)} %collective-permute-done.22.refs_3_, ...), custom_call_target="tpu_custom_call" | custom-call | tf_op jit(solution)/shard_map/basis/pallas_call | solution.py:564
  (6 shorter events, 0.0 us)
Async XLA Ops:
  0.6 15.5 %copy-start = (f32[3,24576]{1,0:T(4,128)S(1)}, f32[3,24576]{1,0:T(4,128)}, u32[]{:S(2)}) copy-start(f32[3,24576]{1,0:T(4,128)} %refs_7_.1) | copy-start | bytes 884740
  7.1 5.9 %collective-permute-start = (f32[80,128]{1,0:T(8,128)S(1)}, f32[80,128]{1,0:T(8,128)S(1)}, u32[]{:S(2)}, u32[]{:S(2)}) collective-permute-start(f32[80,128]{1,0:T(8,128)S(1)} %get-tuple-element.41.refs_0_), channel_id=1, source_target_pairs={{0,24},{8,16},{16,8},{24,0},{1,25},{9,17},{17,9},{25,1},{2,26},{10... | collective-permute-start | bytes 122888 | tf_op jit(solution)/shard_map/ppermute | solution.py:495
  11.0 4.0 %collective-permute-start.1 = (f32[80,128]{1,0:T(8,128)S(1)}, f32[80,128]{1,0:T(8,128)S(1)}, u32[]{:S(2)}, u32[]{:S(2)}) collective-permute-start(f32[80,128]{1,0:T(8,128)S(1)} %get-tuple-element.41.refs_0_), channel_id=1, source_target_pairs={{0,16},{8,24},{16,0},{24,8},{1,17},{9,25},{17,1},{25,9},{2,18},{10... | collective-permute-start | bytes 122888 | tf_op jit(solution)/shard_map/ppermute | solution.py:495
  11.5 4.0 %collective-permute-start.2 = (f32[80,128]{1,0:T(8,128)S(1)}, f32[80,128]{1,0:T(8,128)S(1)}, u32[]{:S(2)}, u32[]{:S(2)}) collective-permute-start(f32[80,128]{1,0:T(8,128)S(1)} %get-tuple-element.41.refs_0_), channel_id=1, source_target_pairs={{0,8},{8,0},{16,24},{24,16},{1,9},{9,1},{17,25},{25,17},{2,10},{10... | collective-permute-start | bytes 122888 | tf_op jit(solution)/shard_map/ppermute | solution.py:495
  16.4 1.9 %collective-permute-start.4 = (bf16[72,3072]{1,0:T(8,128)(2,1)S(1)}, bf16[72,3072]{1,0:T(8,128)(2,1)S(1)}, u32[]{:S(2)}, u32[]{:S(2)}) collective-permute-start(bf16[72,3072]{1,0:T(8,128)(2,1)S(1)} %displace.4), channel_id=1, source_target_pairs={{0,1},{1,0},{2,3},{3,2},{4,5},{5,4},{6,7},{7,6},{8,9},{9,8},{10,11... | collective-permute-start | bytes 1327112 | tf_op jit(solution)/shard_map/ppermute | solution.py:671
  16.5 1.8 %collective-permute-start.3 = (f32[24,128]{1,0:T(8,128)S(1)}, f32[24,128]{1,0:T(8,128)S(1)}, u32[]{:S(2)}, u32[]{:S(2)}) collective-permute-start(f32[24,128]{1,0:T(8,128)S(1)} %get-tuple-element.42.own_ref), channel_id=1, source_target_pairs={{0,1},{1,0},{2,3},{3,2},{4,5},{5,4},{6,7},{7,6},{8,9},{9,8},{10,11... | collective-permute-start | bytes 36872 | tf_op jit(solution)/shard_map/ppermute | solution.py:663
  18.3 12.1 %collective-permute-start.5 = (bf16[72,9216]{1,0:T(8,128)(2,1)S(1)}, bf16[72,9216]{1,0:T(8,128)(2,1)S(1)}, u32[]{:S(2)}, u32[]{:S(2)}) collective-permute-start(bf16[72,9216]{1,0:T(8,128)(2,1)S(1)} %displace.7), channel_id=1, source_target_pairs={{0,1},{1,0},{2,3},{3,2},{4,5},{5,4},{6,7},{7,6},{8,9},{9,8},{10,11... | collective-permute-start | bytes 3981320 | tf_op jit(solution)/shard_map/ppermute | solution.py:674
  19.0 11.4 %collective-permute-start.6 = (bf16[96,1664]{1,0:T(8,128)(2,1)S(1)}, bf16[96,1664]{1,0:T(8,128)(2,1)S(1)}, u32[]{:S(2)}, u32[]{:S(2)}) collective-permute-start(bf16[96,1664]{1,0:T(8,128)(2,1)S(1)} %term.11), channel_id=1, source_target_pairs={{0,2},{1,3},{6,4},{7,5},{8,10},{9,11},{14,12},{15,13},{16,18},{17,... | collective-permute-start | bytes 958472 | tf_op jit(solution)/shard_map/ppermute | solution.py:602
  22.8 13.9 %collective-permute-start.11 = (bf16[96,1536]{1,0:T(8,128)(2,1)S(1)}, bf16[96,1536]{1,0:T(8,128)(2,1)S(1)}, u32[]{:S(2)}, u32[]{:S(2)}) collective-permute-start(bf16[96,1536]{1,0:T(8,128)(2,1)S(1)} %term.10), channel_id=1, source_target_pairs={{0,2},{1,3},{6,4},{7,5},{8,10},{9,11},{14,12},{15,13},{16,18},{17,... | collective-permute-start | bytes 884744 | tf_op jit(solution)/shard_map/ppermute | solution.py:602
  30.8 12.7 %collective-permute-start.7 = (bf16[96,1664]{1,0:T(8,128)(2,1)S(1)}, bf16[96,1664]{1,0:T(8,128)(2,1)S(1)}, u32[]{:S(2)}, u32[]{:S(2)}) collective-permute-start(bf16[96,1664]{1,0:T(8,128)(2,1)S(1)} %term.12), channel_id=1, source_target_pairs={{0,2},{1,3},{6,4},{7,5},{8,10},{9,11},{14,12},{15,13},{16,18},{17,... | collective-permute-start | bytes 958472 | tf_op jit(solution)/shard_map/ppermute | solution.py:606
  35.8 7.7 %collective-permute-start.8 = (bf16[96,1664]{1,0:T(8,128)(2,1)S(1)}, bf16[96,1664]{1,0:T(8,128)(2,1)S(1)}, u32[]{:S(2)}, u32[]{:S(2)}) collective-permute-start(bf16[96,1664]{1,0:T(8,128)(2,1)S(1)} %term.13), channel_id=1, source_target_pairs={{2,4},{3,5},{4,2},{5,3},{10,12},{11,13},{12,10},{13,11},{18,20},{1... | collective-permute-start | bytes 958472 | tf_op jit(solution)/shard_map/ppermute | solution.py:608
  37.0 12.9 %collective-permute-start.12 = (bf16[96,1536]{1,0:T(8,128)(2,1)S(1)}, bf16[96,1536]{1,0:T(8,128)(2,1)S(1)}, u32[]{:S(2)}, u32[]{:S(2)}) collective-permute-start(bf16[96,1536]{1,0:T(8,128)(2,1)S(1)} %term.16), channel_id=1, source_target_pairs={{0,2},{1,3},{6,4},{7,5},{8,10},{9,11},{14,12},{15,13},{16,18},{17,... | collective-permute-start | bytes 884744 | tf_op jit(solution)/shard_map/ppermute | solution.py:606
  41.9 8.0 %collective-permute-start.13 = (bf16[96,1536]{1,0:T(8,128)(2,1)S(1)}, bf16[96,1536]{1,0:T(8,128)(2,1)S(1)}, u32[]{:S(2)}, u32[]{:S(2)}) collective-permute-start(bf16[96,1536]{1,0:T(8,128)(2,1)S(1)} %term.17), channel_id=1, source_target_pairs={{2,4},{3,5},{4,2},{5,3},{10,12},{11,13},{12,10},{13,11},{18,20},{1... | collective-permute-start | bytes 884744 | tf_op jit(solution)/shard_map/ppermute | solution.py:608
  44.1 12.6 %collective-permute-start.9 = (bf16[96,1664]{1,0:T(8,128)(2,1)S(1)}, bf16[96,1664]{1,0:T(8,128)(2,1)S(1)}, u32[]{:S(2)}, u32[]{:S(2)}) collective-permute-start(bf16[96,1664]{1,0:T(8,128)(2,1)S(1)} %term.14), channel_id=1, source_target_pairs={{0,2},{1,3},{6,4},{7,5},{4,6},{5,7},{2,0},{3,1},{8,10},{9,11},{14,... | collective-permute-start | bytes 958472 | tf_op jit(solution)/shard_map/ppermute | solution.py:612
  47.5 9.2 %collective-permute-start.10 = (bf16[96,1664]{1,0:T(8,128)(2,1)S(1)}, bf16[96,1664]{1,0:T(8,128)(2,1)S(1)}, u32[]{:S(2)}, u32[]{:S(2)}) collective-permute-start(bf16[96,1664]{1,0:T(8,128)(2,1)S(1)} %term.15), channel_id=1, source_target_pairs={{2,4},{3,5},{4,2},{5,3},{10,12},{11,13},{12,10},{13,11},{18,20},{1... | collective-permute-start | bytes 958472 | tf_op jit(solution)/shard_map/ppermute | solution.py:614
  50.3 12.2 %collective-permute-start.14 = (bf16[96,1536]{1,0:T(8,128)(2,1)S(1)}, bf16[96,1536]{1,0:T(8,128)(2,1)S(1)}, u32[]{:S(2)}, u32[]{:S(2)}) collective-permute-start(bf16[96,1536]{1,0:T(8,128)(2,1)S(1)} %term.18), channel_id=1, source_target_pairs={{0,2},{1,3},{6,4},{7,5},{4,6},{5,7},{2,0},{3,1},{8,10},{9,11},{14,... | collective-permute-start | bytes 884744 | tf_op jit(solution)/shard_map/ppermute | solution.py:612
  53.7 8.7 %collective-permute-start.15 = (bf16[96,1536]{1,0:T(8,128)(2,1)S(1)}, bf16[96,1536]{1,0:T(8,128)(2,1)S(1)}, u32[]{:S(2)}, u32[]{:S(2)}) collective-permute-start(bf16[96,1536]{1,0:T(8,128)(2,1)S(1)} %term.19), channel_id=1, source_target_pairs={{2,4},{3,5},{4,2},{5,3},{10,12},{11,13},{12,10},{13,11},{18,20},{1... | collective-permute-start | bytes 884744 | tf_op jit(solution)/shard_map/ppermute | solution.py:614
  62.9 4.5 %collective-permute-start.16 = (f32[8,128]{1,0:T(8,128)S(1)}, f32[8,128]{1,0:T(8,128)S(1)}, u32[]{:S(2)}, u32[]{:S(2)}) collective-permute-start(f32[8,128]{1,0:T(8,128)S(1)} %get-tuple-element.73.refs_0_), channel_id=1, source_target_pairs={{0,24},{8,16},{16,8},{24,0},{1,25},{9,17},{17,9},{25,1},{2,26},{10... | collective-permute-start | bytes 12296 | tf_op jit(solution)/shard_map/ppermute | solution.py:495
  64.4 3.6 %collective-permute-start.17 = (f32[8,128]{1,0:T(8,128)S(1)}, f32[8,128]{1,0:T(8,128)S(1)}, u32[]{:S(2)}, u32[]{:S(2)}) collective-permute-start(f32[8,128]{1,0:T(8,128)S(1)} %get-tuple-element.73.refs_0_), channel_id=1, source_target_pairs={{0,16},{8,24},{16,0},{24,8},{1,17},{9,25},{17,1},{25,9},{2,18},{10... | collective-permute-start | bytes 12296 | tf_op jit(solution)/shard_map/ppermute | solution.py:495
  64.9 3.6 %collective-permute-start.18 = (f32[8,128]{1,0:T(8,128)S(1)}, f32[8,128]{1,0:T(8,128)S(1)}, u32[]{:S(2)}, u32[]{:S(2)}) collective-permute-start(f32[8,128]{1,0:T(8,128)S(1)} %get-tuple-element.73.refs_0_), channel_id=1, source_target_pairs={{0,8},{8,0},{16,24},{24,16},{1,9},{9,1},{17,25},{25,17},{2,10},{10... | collective-permute-start | bytes 12296 | tf_op jit(solution)/shard_map/ppermute | solution.py:495
  68.5 1.2 %collective-permute-start.19 = (f32[8,128]{1,0:T(8,128)S(1)}, f32[8,128]{1,0:T(8,128)S(1)}, u32[]{:S(2)}, u32[]{:S(2)}) collective-permute-start(f32[8,128]{1,0:T(8,128)S(1)} %fold.2.refs_0_), channel_id=1, source_target_pairs={{0,1},{1,0},{2,3},{3,2},{4,5},{5,4},{6,7},{7,6},{8,9},{9,8},{10,11... | collective-permute-start | bytes 12296 | tf_op jit(solution)/shard_map/ppermute | solution.py:495
  69.7 5.4 %collective-permute-start.20 = (f32[8,128]{1,0:T(8,128)S(1)}, f32[8,128]{1,0:T(8,128)S(1)}, u32[]{:S(2)}, u32[]{:S(2)}) collective-permute-start(f32[8,128]{1,0:T(8,128)S(1)} %fold.3.refs_0_), channel_id=1, source_target_pairs={{0,6},{1,7},{2,4},{3,5},{4,2},{5,3},{6,0},{7,1},{8,14},{9,15},{10,... | collective-permute-start | bytes 12296 | tf_op jit(solution)/shard_map/ppermute | solution.py:495
  72.2 4.5 %collective-permute-start.21 = (f32[8,128]{1,0:T(8,128)S(1)}, f32[8,128]{1,0:T(8,128)S(1)}, u32[]{:S(2)}, u32[]{:S(2)}) collective-permute-start(f32[8,128]{1,0:T(8,128)S(1)} %fold.3.refs_0_), channel_id=1, source_target_pairs={{0,4},{1,5},{2,6},{3,7},{4,0},{5,1},{6,2},{7,3},{8,12},{9,13},{10,... | collective-permute-start | bytes 12296 | tf_op jit(solution)/shard_map/ppermute | solution.py:495
  73.7 3.6 %collective-permute-start.22 = (f32[8,128]{1,0:T(8,128)S(1)}, f32[8,128]{1,0:T(8,128)S(1)}, u32[]{:S(2)}, u32[]{:S(2)}) collective-permute-start(f32[8,128]{1,0:T(8,128)S(1)} %fold.3.refs_0_), channel_id=1, source_target_pairs={{0,2},{1,3},{2,0},{3,1},{4,6},{5,7},{6,4},{7,5},{8,10},{9,11},{10,... | collective-permute-start | bytes 12296 | tf_op jit(solution)/shard_map/ppermute | solution.py:495
